TPU v7x, 256 devices: a whole 4x4x8 slice. The times are simulated.
256 devices in a mesh: dp: 2 (over core), ctx: 4 (over x), head: 32 (over z, y).
Axes of the slice: x: 4, y: 4, z: 8, core: 2. Of those that a mesh axis runs over, the one named last changes fastest.
Arguments:
- query: bfloat16 [2, 2048, 24576], P('dp', 'ctx', 'head'), may hold values from -240 to 240
- kv_latent: bfloat16 [2, 2048, 576], P('dp', ('ctx', 'head')), may hold values from -4 to 4
- kv_weight: bfloat16 [512, 32768], P(None, 'head'), may hold values from -0.25 to 0.25
- grad_out: bfloat16 [2, 2048, 16384], P('dp', 'ctx', 'head'), may hold values from -6 to 6
- doc_lengths: int32 [2, 16], P('dp'), may hold values from 1 to 512, 2048 in all within a row
Outputs:
- d_query: bfloat16 [2, 2048, 24576], P('dp', 'ctx', 'head')
- d_latent: bfloat16 [2, 2048, 576], P('dp', ('ctx', 'head'))
- d_kv_weight: float32 [512, 32768], P(None, 'head')
Inputs may be any that keep to these rules, and one draw needn't show every extreme that they name: `doc_lengths`: each row sums to 2048 and holds one length of exactly 512.
All inputs are finite; a program needn't handle non-finite values.
Results may differ from a plain program's by a relative error of at most 0.014.
Values may be sent and summed in bfloat16 or wider, within the bound.
No kernel may reach another device: no remote copies, remote signals or barrier semaphores. Data moves between devices by JAX's collectives and lax.ppermute only.
A program may use at most 128 MiB of HBM per device.

v0:
```python
import jax
import jax.numpy as jnp
from jax import lax
from jax.sharding import PartitionSpec as P

LATENT = 512
ROPE = 64
NOPE = 128
VDIM = 128
HEADS_DEV = 4
TOK_CTX = 512
DOC_MAX = 512
BLOCK = 512
TILE = 128


def passed_along(array, axis, by):
    length = lax.axis_size(axis)
    pairs = [(i, i + by) for i in range(length) if 0 <= i + by < length]
    return lax.ppermute(array, axis, pairs)


def attend(
    query_block,
    grad_block,
    key_nope,
    key_rope,
    value_rows,
    query_doc,
    key_doc,
    query_pos,
    key_pos,
    factor,
):
    query_nope = query_block[..., :NOPE]
    query_rope = query_block[..., NOPE:]
    scores = (
        jnp.einsum("qhd,khd->hqk", query_nope, key_nope, preferred_element_type=jnp.float32)
        + jnp.einsum("qhd,kd->hqk", query_rope, key_rope, preferred_element_type=jnp.float32)
    ) * factor
    allowed = (query_doc[:, None] == key_doc[None, :]) & (key_pos[None, :] <= query_pos[:, None])
    scores = jnp.where(allowed[None], scores, -1e30)
    top_score = jnp.max(scores, axis=-1, keepdims=True)
    weights = jnp.where(allowed[None], jnp.exp(scores - top_score), 0.0)
    prob = weights / jnp.sum(weights, axis=-1, keepdims=True)
    prob_low = prob.astype(jnp.bfloat16)
    output = jnp.einsum("hqk,khd->qhd", prob_low, value_rows, preferred_element_type=jnp.float32)
    delta = jnp.sum(grad_block.astype(jnp.float32) * output, axis=-1)
    dots = jnp.einsum("qhd,khd->hqk", grad_block, value_rows, preferred_element_type=jnp.float32)
    slope = (prob * (dots - delta.T[:, :, None])).astype(jnp.bfloat16)
    grad_nope = (
        jnp.einsum("hqk,khd->qhd", slope, key_nope, preferred_element_type=jnp.float32) * factor
    )
    grad_rot = (
        jnp.einsum("hqk,kd->qhd", slope, key_rope, preferred_element_type=jnp.float32) * factor
    )
    grad_query = jnp.concatenate([grad_nope, grad_rot], axis=-1).astype(jnp.bfloat16)
    grad_key = (
        jnp.einsum("hqk,qhd->khd", slope, query_nope, preferred_element_type=jnp.float32) * factor
    )
    grad_value = jnp.einsum(
        "hqk,qhd->khd", prob_low, grad_block, preferred_element_type=jnp.float32
    )
    grad_rope = (
        jnp.einsum("hqk,qhd->kd", slope, query_rope, preferred_element_type=jnp.float32) * factor
    )
    return (grad_query, jnp.concatenate([grad_key, grad_value], axis=-1), grad_rope)


def on_device(query, kv_latent, kv_weight, grad_out, doc_lengths):
    factor = (NOPE + ROPE) ** (-0.5)
    kv_width = NOPE + VDIM
    window_rows = TOK_CTX + DOC_MAX
    back_tiles = DOC_MAX // TILE
    prev_shard = passed_along(kv_latent, "ctx", 1)
    prev_all, own_all = (
        lax.all_gather(prev_shard, "head", axis=1, tiled=True),
        lax.all_gather(kv_latent, "head", axis=1, tiled=True),
    )
    prev_tail = prev_all[0, TOK_CTX - DOC_MAX :]
    window = jnp.concatenate([prev_tail, own_all[0]], axis=0)
    kv_rows = jnp.dot(window[:, :LATENT], kv_weight, preferred_element_type=jnp.float32).astype(
        jnp.bfloat16
    )
    kv_rows = kv_rows.reshape(window_rows, HEADS_DEV, kv_width)
    key_nope = kv_rows[..., :NOPE]
    value_rows = kv_rows[..., NOPE:]
    key_rope = window[:, LATENT:]
    ctx_pos = lax.axis_index("ctx")
    lengths = doc_lengths[0]
    starts = jnp.cumsum(lengths) - lengths
    positions = ctx_pos * TOK_CTX - DOC_MAX + jnp.arange(window_rows, dtype=jnp.int32)
    doc_ids = jnp.sum((positions[:, None] >= starts[None, :]).astype(jnp.int32), axis=1) - 1
    offsets = jnp.arange(window_rows, dtype=jnp.int32)
    queries = query[0].reshape(TOK_CTX, HEADS_DEV, NOPE + ROPE)
    upstream = grad_out[0].reshape(TOK_CTX, HEADS_DEV, VDIM)
    accum_kv = jnp.zeros((window_rows, HEADS_DEV, kv_width), jnp.float32)
    accum_rope = jnp.zeros((window_rows, ROPE), jnp.float32)
    key_lower = DOC_MAX - back_tiles * TILE
    key_upper = DOC_MAX + BLOCK
    grad_query, grad_kv, grad_rope = attend(
        queries,
        upstream,
        key_nope,
        key_rope,
        value_rows,
        doc_ids[DOC_MAX:key_upper],
        doc_ids,
        offsets[DOC_MAX:key_upper],
        offsets,
        factor,
    )
    accum_kv, accum_rope, grad_query = (
        accum_kv.at[key_lower:key_upper].add(grad_kv),
        accum_rope.at[key_lower:key_upper].add(grad_rope),
        grad_query,
    )
    d_query = grad_query.reshape(1, TOK_CTX, HEADS_DEV * (NOPE + ROPE))
    key_grads = accum_kv.astype(jnp.bfloat16).reshape(window_rows, HEADS_DEV * kv_width)
    weight_part = jnp.dot(window[:, :LATENT].T, key_grads, preferred_element_type=jnp.float32)
    d_kv_weight = lax.psum(weight_part, ("dp", "ctx"))
    latent_term = jnp.concatenate(
        [jnp.dot(key_grads, kv_weight.T, preferred_element_type=jnp.float32), accum_rope], axis=1
    )
    incoming = passed_along(latent_term[:DOC_MAX].astype(jnp.bfloat16), "ctx", -1).astype(
        jnp.float32
    )
    own_term = latent_term[DOC_MAX:].at[TOK_CTX - DOC_MAX :].add(incoming)
    summed = lax.psum_scatter(own_term, "head", scatter_dimension=0, tiled=True)
    d_latent = summed.astype(jnp.bfloat16)[None]
    return (d_query, d_latent, d_kv_weight)


def solution(mesh):
    return jax.shard_map(
        on_device,
        mesh=mesh,
        in_specs=(
            P("dp", "ctx", "head"),
            P("dp", ("ctx", "head"), None),
            P(None, "head"),
            P("dp", "ctx", "head"),
            P("dp", None),
        ),
        out_specs=(P("dp", "ctx", "head"), P("dp", ("ctx", "head"), None), P(None, "head")),
        check_vma=False,
    )
```

profile of v0, /device:TPU:1, one launch (start us, length us, event | category | flops | bytes accessed | tf_op | source)
XLA Modules:
  0.0 386.4 jit_solution(9034208312707482677)
XLA Ops:
  8.1 4.7 %collective-permute-start = (bf16[1,16,576]{2,1,0:T(8,128)(2,1)}, bf16[1,16,576]{2,1,0:T(8,128)(2,1)}, u32[]{:S(2)}, u32[]{:S(2)}) collective-permute-start(bf16[1,16,576]{2,1,0:T(8,128)(2,1)} %param.18), channel_id=1, source_target_pairs={{0,32},{32,64},{64,96},{1,33},{33,65},{65,97},{2,34},{34,66},{66,9... | collective-permute-start | bytes 55304 | tf_op jit(solution)/shard_map/ppermute | solution.py:20
  14.4 1.3 fusion.5
  15.6 41.1 %all_gather.7 = bf16[1,512,576]{2,1,0:T(8,128)(2,1)S(1)} all-gather(bf16[1,16,576]{2,1,0:T(8,128)(2,1)} %param.18), channel_id=1, replica_groups=mesh['dp'=2,'ctx'=4,'head'=32] {'head'}, dimensions={1}, use_global_device_ids=true | all-gather | bytes 608256 | tf_op jit(solution)/shard_map/all_gather | solution.py:78
  57.0 1.2 copy.68
  58.1 1.3 copy.71
  59.4 36.7 %all_gather.6 = bf16[1,512,576]{2,1,0:T(8,128)(2,1)S(1)} all-gather(bf16[1,16,576]{2,1,0:T(8,128)(2,1)} %collective-permute-done), channel_id=1, replica_groups=mesh['dp'=2,'ctx'=4,'head'=32] {'head'}, dimensions={1}, use_global_device_ids=true | all-gather | bytes 608256 | tf_op jit(solution)/shard_map/all_gather | solution.py:77
  96.4 2.6 convolution_convert_fusion
  99.1 4.5 %fusion.26 = f32[1024,512,4]{1,0,2:T(8,128)} fusion(bf16[1024,64,1]{0,1,2:T(8,128)(2,1)S(1)} %fusion.28, bf16[512,4,192]{0,2,1:T(8,128)(2,1)S(1)} %bitcast.73), kind=kOutput, calls=%fused_computation.45 | convolution fusion | flops 268435456 | bytes 8781824 | tf_op jit(solution)/shard_map/qhd,kd->hqk/dot_general | solution.py:39
  103.6 11.3 %fusion.32 = (f32[4,512]{1,0:T(4,128)S(1)}, f32[4,512,1024]{1,2,0:T(8,128)}) fusion(pred[512,1024]{0,1:T(8,128)(4,1)} %fusion.5, f32[1024,512,4]{1,0,2:T(8,128)} %fusion.26, bf16[1024,4,256]{0,2,1:T(8,128)(2,1)} %bitcast.82, bf16[512,4,192]{0,2,1:T(8,128)(2,1)S(1)} %bitcast.74), kind=kOutput, calls=%fused_computation.55 | convolution fusion | flops 549454848 | bytes 19406848 | tf_op jit(solution)/shard_map/sub | solution.py:44
  114.8 4.8 %fusion.4 = bf16[4,512,1024]{1,2,0:T(8,128)(2,1)S(1)} fusion(f32[4,512,1024]{1,2,0:T(8,128)} %get-tuple-element.76, f32[4,512]{1,0:T(4,128)S(1)} %get-tuple-element.75), kind=kLoop, calls=%fused_computation.8 | loop fusion | flops 4194304 | bytes 12591104 | tf_op jit(solution)/shard_map/convert_element_type | solution.py:46
  120.4 1.5 fusion.6
  121.9 1.8 fusion.1
  123.7 1.5 fusion.7
  125.6 1.4 fusion.17
  127.2 1.3 fusion.37
  128.7 1.3 collective-permute-start.1
  130.0 9.3 %collective-permute-done.1 = bf16[512,576]{0,1:T(8,128)(2,1)S(1)} collective-permute-done((bf16[512,576]{0,1:T(8,128)(2,1)S(1)}, bf16[512,576]{0,1:T(8,128)(2,1)S(1)}, u32[]{:S(2)}, u32[]{:S(2)}) %collective-permute-start.1) | collective-permute-done | bytes 589856 | tf_op jit(solution)/shard_map/ppermute | solution.py:20
  139.5 1.5 copy.94
  141.1 4.2 %fusion.29 = f32[512,1024]{1,0:T(8,128)} fusion(bf16[1024,1024]{0,1:T(8,128)(2,1)} %bitcast.78, bf16[512,576]{0,1:T(8,128)(2,1)S(1)} %bitcast.72, bf16[512,576]{0,1:T(8,128)(2,1)S(1)} %bitcast.69), kind=kOutput, calls=%fused_computation.54 | convolution fusion | flops 1075838976 | bytes 5373952 | tf_op jit(solution)/shard_map/dot_general | solution.py:120
  146.2 3.2 fusion.16
  150.6 1.2 copy.82
  151.7 222.4 %reduce-scatter.4.cloned.1.call-done = f32[16,576]{1,0:T(8,128)} async-done(((f32[512,576]{1,0:T(8,128)}), f32[16,576]{1,0:T(8,128)}) %reduce-scatter.4.cloned.1.call-update) | async-done | bytes 36880
  374.2 0.9 copy.95
  375.8 3.2 copy.100
  (49 shorter events, 6.8 us)
Async XLA Ops:
  8.0 88.4 %copy-start = (bf16[512,1024]{1,0:T(8,128)(2,1)S(1)}, bf16[512,1024]{1,0:T(8,128)(2,1)}, u32[]{:S(2)}) copy-start(bf16[512,1024]{1,0:T(8,128)(2,1)} %param.19) | copy-start | bytes 3145732
  8.0 49.0 %copy-start.9 = (bf16[1,512,768]{2,1,0:T(8,128)(2,1)S(1)}, bf16[1,512,768]{2,1,0:T(8,128)(2,1)}, u32[]{:S(2)}) copy-start(bf16[1,512,768]{2,1,0:T(8,128)(2,1)} %param.17) | copy-start | bytes 2359300
  8.0 366.2 %reduce-scatter.4.cloned.1.call-start = ((), (), s32[]{:S(2)}) async-start(), calls=%async_computation.2 | async-start | bytes 1351680
  8.1 51.3 %collective-permute-start = (bf16[1,16,576]{2,1,0:T(8,128)(2,1)}, bf16[1,16,576]{2,1,0:T(8,128)(2,1)}, u32[]{:S(2)}, u32[]{:S(2)}) collective-permute-start(bf16[1,16,576]{2,1,0:T(8,128)(2,1)} %param.18), channel_id=1, source_target_pairs={{0,32},{32,64},{64,96},{1,33},{33,65},{65,97},{2,34},{34,66},{66,9... | collective-permute-start | bytes 55304 | tf_op jit(solution)/shard_map/ppermute | solution.py:20
  96.4 2.6 copy-start.5
  96.4 2.6 copy-start.3
  114.8 4.8 %copy-start.7 = (bf16[1024,1024]{0,1:T(8,128)(2,1)S(1)}, bf16[1024,1024]{0,1:T(8,128)(2,1)}, u32[]{:S(2)}) copy-start(bf16[1024,1024]{0,1:T(8,128)(2,1)} %convolution_convert_fusion) | copy-start | bytes 6291460
  114.8 7.1 %slice-start = ((s8[8388608]{0:T(1024)(128)(4,1)}), s8[4194304]{0:T(1024)(128)(4,1)S(1)}, s32[]{:S(2)}) async-start(s8[8388608]{0:T(1024)(128)(4,1)} %bitcast.64), calls=%async_computation.3 | async-start | bytes 8388608
  119.6 2.3 slice-start.1
  123.7 1.9 copy-start.1
  127.2 1.3 copy-start.4
  128.7 10.6 %collective-permute-start.1 = (bf16[512,576]{0,1:T(8,128)(2,1)S(1)}, bf16[512,576]{0,1:T(8,128)(2,1)S(1)}, u32[]{:S(2)}, u32[]{:S(2)}) collective-permute-start(bf16[512,576]{0,1:T(8,128)(2,1)S(1)} %fusion.15), channel_id=1, source_target_pairs={{32,0},{64,32},{96,64},{33,1},{65,33},{97,65},{34,2},{66,34},{98,6... | collective-permute-start | bytes 1769480 | tf_op jit(solution)/shard_map/ppermute | solution.py:20
  141.0 234.8 %all-reduce.2.cloned.1.call-start = ((), (), s32[]{:S(2)}) async-start(), calls=%async_computation.1 | async-start | bytes 4194304 | tf_op jit(solution)/shard_map/psum | solution.py:121
  145.3 0.9 copy-start.6
  145.3 4.1 %copy-start.8 = (bf16[1024,1024]{0,1:T(8,128)(2,1)S(1)}, bf16[1024,1024]{0,1:T(8,128)(2,1)}, u32[]{:S(2)}) copy-start(bf16[1024,1024]{0,1:T(8,128)(2,1)} %convolution_convert_fusion) | copy-start | bytes 6291460
  146.2 3.6 copy-start.2
Sparse Core Ops, SparseCore 0:
  141.2 232.9 reduce-scatter.3
Sparse Core Ops, SparseCore 1:
  145.4 91.4 all-reduce.1
where the time goes:
time: 391 us; the launch traced here: 386 us
  waiting for transfers between devices  232 us (59%)
  blocking collectives  77.8 us (20%)
  matrix products  34.6 us (9%)
  between operations  15.7 us (4%)
  local copies, waits for them, and re-layouts  12.2 us (3%)
  other arithmetic  8.13 us (2%)
  starting transfers between devices  6.06 us (2%)
    unnamed x3, waiting for transfers between devices  222 us
    all_gather x1, blocking collectives, on_device(): lax.all_gather(kv_latent, 'head', axis=1, tiled=True)  41.1 us
    all_gather x1, blocking collectives, on_device(): lax.all_gather(prev_shard, 'head', axis=1, tiled=True)  36.7 us
    unnamed x31, local copies, waits for them, and re-layouts  11.7 us
    sub x1, matrix products, attend(): weights = jnp.where(allowed[None], jnp.exp(scores - top_score), 0.0)  11.3 us
    ppermute x2, waiting for transfers between devices, passed_along(): return lax.ppermute(array, axis, pairs)  9.33 us
  transfers between devices with their start and end apart: 4, of which 2 were waited for; matrix products, arithmetic and copies ran while one was open for 4% of the time, Pallas kernels for 0%

commit v1 on v0

--- a/solution.py
+++ b/solution.py
@@ -12,12 +12,45 @@
 DOC_MAX = 512
 BLOCK = 512
 TILE = 128
+N_CTX = 4
+HEAD_DEVS = 32
 
 
 def passed_along(array, axis, by):
     length = lax.axis_size(axis)
     pairs = [(i, i + by) for i in range(length) if 0 <= i + by < length]
     return lax.ppermute(array, axis, pairs)
+
+
+def shift_pairs(by):
+    return [(i, (i + by) % N_CTX) for i in range(N_CTX)]
+
+
+def gathered_rows(rows):
+    copies = jnp.broadcast_to(rows[None], (HEAD_DEVS, *rows.shape))
+    return lax.all_to_all(copies, "head", 0, 0).reshape(-1, rows.shape[-1])
+
+
+def summed_weight(part):
+    core = lax.axis_index("dp")
+    place = lax.axis_index("ctx")
+    half, quarter = LATENT // 2, LATENT // 8
+    swap = [(0, 1), (1, 0)]
+    low = part.astype(jnp.bfloat16)
+    other = lax.ppermute(lax.dynamic_slice_in_dim(low, (1 - core) * half, half), "dp", swap)
+    mine = lax.dynamic_slice_in_dim(part, core * half, half) + other.astype(jnp.float32)
+    low = mine.astype(jnp.bfloat16)
+    total = lax.dynamic_slice_in_dim(mine, place * quarter, quarter)
+    for by in range(1, N_CTX):
+        chunk = lax.dynamic_slice_in_dim(low, (place + by) % N_CTX * quarter, quarter)
+        total = total + lax.ppermute(chunk, "ctx", shift_pairs(by)).astype(jnp.float32)
+    low = total.astype(jnp.bfloat16)
+    pieces = [low] + [lax.ppermute(low, "ctx", shift_pairs(by)) for by in range(1, N_CTX)]
+    line = jnp.concatenate(pieces[::-1] + pieces[:0:-1], axis=0)
+    mine = lax.dynamic_slice_in_dim(line, (N_CTX - 1 - place) * quarter, half)
+    other = lax.ppermute(mine, "dp", swap)
+    line = jnp.concatenate([mine, other, mine], axis=0)
+    return lax.dynamic_slice_in_dim(line, core * half, LATENT).astype(jnp.float32)
 
 
 def attend(
@@ -72,13 +105,9 @@
     kv_width = NOPE + VDIM
     window_rows = TOK_CTX + DOC_MAX
     back_tiles = DOC_MAX // TILE
-    prev_shard = passed_along(kv_latent, "ctx", 1)
-    prev_all, own_all = (
-        lax.all_gather(prev_shard, "head", axis=1, tiled=True),
-        lax.all_gather(kv_latent, "head", axis=1, tiled=True),
-    )
-    prev_tail = prev_all[0, TOK_CTX - DOC_MAX :]
-    window = jnp.concatenate([prev_tail, own_all[0]], axis=0)
+    own_all = gathered_rows(kv_latent[0])
+    prev_all = passed_along(own_all, "ctx", 1)
+    window = jnp.concatenate([prev_all, own_all], axis=0)
     kv_rows = jnp.dot(window[:, :LATENT], kv_weight, preferred_element_type=jnp.float32).astype(
         jnp.bfloat16
     )
@@ -118,7 +147,7 @@
     d_query = grad_query.reshape(1, TOK_CTX, HEADS_DEV * (NOPE + ROPE))
     key_grads = accum_kv.astype(jnp.bfloat16).reshape(window_rows, HEADS_DEV * kv_width)
     weight_part = jnp.dot(window[:, :LATENT].T, key_grads, preferred_element_type=jnp.float32)
-    d_kv_weight = lax.psum(weight_part, ("dp", "ctx"))
+    d_kv_weight = summed_weight(weight_part)
     latent_term = jnp.concatenate(
         [jnp.dot(key_grads, kv_weight.T, preferred_element_type=jnp.float32), accum_rope], axis=1
     )
@@ -126,7 +155,10 @@
         jnp.float32
     )
     own_term = latent_term[DOC_MAX:].at[TOK_CTX - DOC_MAX :].add(incoming)
-    summed = lax.psum_scatter(own_term, "head", scatter_dimension=0, tiled=True)
+    terms = lax.all_to_all(
+        own_term.astype(jnp.bfloat16).reshape(HEAD_DEVS, -1, LATENT + ROPE), "head", 0, 0
+    )
+    summed = jnp.sum(terms.astype(jnp.float32), axis=0)
     d_latent = summed.astype(jnp.bfloat16)[None]
     return (d_query, d_latent, d_kv_weight)
 

time: 391 us -> 146 us (0.37); the launches traced: 386 us -> 146 us
  waiting for transfers between devices: 232 us -> 38.4 us
  blocking collectives: 77.8 us -> 0 us
  starting transfers between devices: 6.06 us -> 39.9 us
  between operations: 15.7 us -> 1.03 us
  other arithmetic: 8.13 us -> 18.9 us
    unnamed x3 -> x0, waiting for transfers between devices: 222 us -> none
    all_gather x2 -> x0, blocking collectives: 77.8 us -> none  [the longest x1 41.1 us: on_device(): lax.all_gather(kv_latent, 'head', axis=1, tiled=True)]
    all_to_all x0 -> x2, starting transfers between devices: none -> 17.5 us  [the longest x1 12 us: gathered_rows(): return lax.all_to_all(copies, 'head', 0, 0).reshape(-1, rows.shape[-1])]
    all_to_all x0 -> x2, waiting for transfers between devices: none -> 17.2 us  [the longest x1 17.2 us: gathered_rows(): return lax.all_to_all(copies, 'head', 0, 0).reshape(-1, rows.shape[-1])]
    ppermute x0 -> x8, starting transfers between devices: none -> 17.1 us  [the longest x3 6.79 us: summed_weight(): lax.ppermute(chunk, 'ctx', shift_pairs(by)).astype(jnp.float32)]
    ppermute x0 -> x8, waiting for transfers between devices: none -> 16.5 us  [the longest x3 13.8 us: summed_weight(): lax.ppermute(chunk, 'ctx', shift_pairs(by)).astype(jnp.float32)]
    convert_element_type x0 -> x4, other arithmetic: none -> 8.63 us  [the longest x1 3.54 us: summed_weight(): lax.dynamic_slice_in_dim(line, core * half, LATENT).astype(jnp.float32)]
    ppermute x2, waiting for transfers between devices: 9.33 us -> 4.72 us  [passed_along(): return lax.ppermute(array, axis, pairs)]
  transfers between devices with their start and end apart: 4 -> 12, of which waited for: 2 -> 6; matrix products, arithmetic and copies ran while one was open for 4% -> 21% of each run, Pallas kernels for 0% -> 0%
where the time goes in v1:
time: 146 us
  starting transfers between devices  39.9 us (27%)
  waiting for transfers between devices  38.4 us (26%)
  matrix products  32.3 us (22%)
  other arithmetic  18.9 us (13%)
  local copies, waits for them, and re-layouts  15.1 us (10%)
    all_to_all x1, waiting for transfers between devices, gathered_rows(): return lax.all_to_all(copies, 'head', 0, 0).reshape(-1, rows.shape[-1])  17.2 us
    ppermute x3, waiting for transfers between devices, summed_weight(): lax.ppermute(chunk, 'ctx', shift_pairs(by)).astype(jnp.float32)  13.8 us
    all_to_all x1, starting transfers between devices, gathered_rows(): return lax.all_to_all(copies, 'head', 0, 0).reshape(-1, rows.shape[-1])  12 us
    sub x1, matrix products, attend(): weights = jnp.where(allowed[None], jnp.exp(scores - top_score), 0.0)  10.9 us
    unnamed x37, local copies, waits for them, and re-layouts  10 us
    ppermute x3, starting transfers between devices, summed_weight(): lax.ppermute(chunk, 'ctx', shift_pairs(by)).astype(jnp.float32)  6.79 us
    all_to_all x1, starting transfers between devices, on_device(): lax.all_to_all(own_term.astype(jnp.bfloat16).reshape(HEAD_DEVS, -1, LATEN...  5.51 us
    ppermute x2, starting transfers between devices, passed_along(): return lax.ppermute(array, axis, pairs)  5.21 us
  transfers between devices with their start and end apart: 12, of which 6 were waited for; matrix products, arithmetic and copies ran while one was open for 21% of the time, Pallas kernels for 0%

profile of v1, /device:TPU:1, one launch (start us, length us, event | category | flops | bytes accessed | tf_op | source)
XLA Modules:
  0.0 145.6 jit_solution(9933219861615712781)
XLA Ops:
  2.4 12.0 %all-to-all-start = ((bf16[32,16,576]{2,1,0:T(8,128)(2,1)}), bf16[32,16,576]{2,1,0:T(8,128)(2,1)S(1)}, u32[]{:S(2)}, u32[]{:S(2)}) async-start(bf16[32,16,576]{2,1,0:T(8,128)(2,1)} %broadcast_in_dim.42), calls=%async_computation | async-start | bytes 1310720 | tf_op jit(solution)/shard_map/all_to_all | solution.py:31
  15.9 17.2 %all-to-all-done = bf16[32,16,576]{2,1,0:T(8,128)(2,1)S(1)} async-done(((bf16[32,16,576]{2,1,0:T(8,128)(2,1)}), bf16[32,16,576]{2,1,0:T(8,128)(2,1)S(1)}, u32[]{:S(2)}, u32[]{:S(2)}) %all-to-all-start) | async-done | bytes 589856 | tf_op jit(solution)/shard_map/all_to_all | solution.py:31
  33.4 3.9 %collective-permute-start = (bf16[512,576]{0,1:T(8,128)(2,1)S(1)}, bf16[512,576]{0,1:T(8,128)(2,1)}, u32[]{:S(2)}, u32[]{:S(2)}) collective-permute-start(bf16[512,576]{0,1:T(8,128)(2,1)S(1)} %copy.44), channel_id=1, source_target_pairs={{0,32},{32,64},{64,96},{1,33},{33,65},{65,97},{2,34},{34,66},{66,9... | collective-permute-start | bytes 1769480 | tf_op jit(solution)/shard_map/ppermute | solution.py:22
  38.6 2.1 %copy.50 = bf16[1,512,512]{1,2,0:T(8,128)(2,1)} copy(bf16[1,512,512]{2,1,0:T(8,128)(2,1)} %param.20) | data formatting | bytes 1048576 | tf_op args[3]
  41.9 4.7 %collective-permute-done = bf16[512,576]{0,1:T(8,128)(2,1)} collective-permute-done((bf16[512,576]{0,1:T(8,128)(2,1)S(1)}, bf16[512,576]{0,1:T(8,128)(2,1)}, u32[]{:S(2)}, u32[]{:S(2)}) %collective-permute-start) | collective-permute-done | bytes 589856 | tf_op jit(solution)/shard_map/ppermute | solution.py:22
  46.7 2.5 %convolution_convert_fusion = bf16[1024,1024]{0,1:T(8,128)(2,1)S(1)} fusion(bf16[512,1024]{1,0:T(8,128)(2,1)S(1)} %copy-done, bf16[512,576]{0,1:T(8,128)(2,1)} %collective-permute-done, bf16[512,576]{0,1:T(8,128)(2,1)} %copy-done.7), kind=kOutput, calls=%fused_computation.15 | convolution fusion | flops 1076887552 | bytes 4325376 | tf_op jit(solution)/shard_map/dot_general | solution.py:111
  49.2 4.5 %fusion.25 = f32[4,1024,512]{2,1,0:T(8,128)} fusion(bf16[1024,4,256]{0,2,1:T(8,128)(2,1)S(1)} %bitcast.64, bf16[512,4,192]{0,2,1:T(8,128)(2,1)S(1)} %bitcast.69), kind=kOutput, calls=%fused_computation.48 | convolution fusion | flops 536870912 | bytes 9961472 | tf_op jit(solution)/shard_map/qhd,khd->hqk/dot_general | solution.py:71
  54.6 10.9 %fusion.37 = (f32[4,512]{1,0:T(4,128)S(1)}, f32[4,512,1024]{1,2,0:T(8,128)}) fusion(pred[512,1024]{0,1:T(8,128)(4,1)} %fusion.5, f32[4,1024,512]{2,1,0:T(8,128)} %fusion.25, bf16[1024,64,1]{0,1,2:T(8,128)(2,1)S(1)} %fusion.32, bf16[512,4,192]{0,2,1:T(8,128)(2,1)} %bitcast.68), kind=kOutput, calls=%fused_computation.76 | convolution fusion | flops 281019392 | bytes 18227200 | tf_op jit(solution)/shard_map/sub | solution.py:77
  65.5 4.8 %fusion.4 = bf16[4,512,1024]{1,2,0:T(8,128)(2,1)S(1)} fusion(f32[4,512,1024]{1,2,0:T(8,128)} %get-tuple-element.78, f32[4,512]{1,0:T(4,128)S(1)} %get-tuple-element.77), kind=kLoop, calls=%fused_computation.8 | loop fusion | flops 4194304 | bytes 12591104 | tf_op jit(solution)/shard_map/convert_element_type | solution.py:79
  77.0 2.3 %fusion.33 = f32[512,1024]{1,0:T(8,128)S(1)} fusion(bf16[1024,1024]{0,1:T(8,128)(2,1)S(1)} %bitcast.74, bf16[512,576]{0,1:T(8,128)(2,1)} %collective-permute-done, bf16[512,576]{0,1:T(8,128)(2,1)S(1)} %copy-done.9), kind=kOutput, calls=%fused_computation.74 | convolution fusion | flops 1075838976 | bytes 5373952 | tf_op jit(solution)/shard_map/dot_general | solution.py:149
  79.5 3.5 %collective-permute-start.2 = (bf16[256,1024]{1,0:T(8,128)(2,1)S(1)}, bf16[256,1024]{1,0:T(8,128)(2,1)S(1)}, u32[]{:S(2)}, u32[]{:S(2)}) collective-permute-start(bf16[256,1024]{1,0:T(8,128)(2,1)S(1)} %dynamic-slice_convert_fusion), channel_id=1, source_target_pairs={{0,128},{128,0},{1,129},{129,1},{2,130},{130,2},{3,131},{131,3},{4... | collective-permute-start | bytes 1572872 | tf_op jit(solution)/shard_map/ppermute | solution.py:40
  89.7 2.9 %collective-permute-start.3 = (bf16[64,1024]{1,0:T(8,128)(2,1)}, bf16[64,1024]{1,0:T(8,128)(2,1)}, u32[]{:S(2)}, u32[]{:S(2)}) collective-permute-start(bf16[64,1024]{1,0:T(8,128)(2,1)} %get-tuple-element.74), channel_id=1, source_target_pairs={{0,32},{32,64},{64,96},{96,0},{1,33},{33,65},{65,97},{97,1},{2,34}... | collective-permute-start | bytes 393224 | tf_op jit(solution)/shard_map/ppermute | solution.py:46
  92.7 3.8 %collective-permute-start.4 = (bf16[64,1024]{1,0:T(8,128)(2,1)}, bf16[64,1024]{1,0:T(8,128)(2,1)}, u32[]{:S(2)}, u32[]{:S(2)}) collective-permute-start(bf16[64,1024]{1,0:T(8,128)(2,1)} %get-tuple-element.76), channel_id=1, source_target_pairs={{0,64},{32,96},{64,0},{96,32},{1,65},{33,97},{65,1},{97,33},{2,66}... | collective-permute-start | bytes 393224 | tf_op jit(solution)/shard_map/ppermute | solution.py:46
  96.5 2.8 %collective-permute-done.3 = bf16[64,1024]{1,0:T(8,128)(2,1)} collective-permute-done((bf16[64,1024]{1,0:T(8,128)(2,1)}, bf16[64,1024]{1,0:T(8,128)(2,1)}, u32[]{:S(2)}, u32[]{:S(2)}) %collective-permute-start.3) | collective-permute-done | bytes 131104 | tf_op jit(solution)/shard_map/ppermute | solution.py:46
  99.3 3.7 %collective-permute-done.4 = bf16[64,1024]{1,0:T(8,128)(2,1)} collective-permute-done((bf16[64,1024]{1,0:T(8,128)(2,1)}, bf16[64,1024]{1,0:T(8,128)(2,1)}, u32[]{:S(2)}, u32[]{:S(2)}) %collective-permute-start.4) | collective-permute-done | bytes 131104 | tf_op jit(solution)/shard_map/ppermute | solution.py:46
  102.9 7.4 %collective-permute-done.5 = bf16[64,1024]{1,0:T(8,128)(2,1)} collective-permute-done((bf16[64,1024]{1,0:T(8,128)(2,1)}, bf16[64,1024]{1,0:T(8,128)(2,1)}, u32[]{:S(2)}, u32[]{:S(2)}) %collective-permute-start.5) | collective-permute-done | bytes 131104 | tf_op jit(solution)/shard_map/ppermute | solution.py:46
  113.1 2.1 %collective-permute-start.7 = (bf16[64,1024]{1,0:T(8,128)(2,1)}, bf16[64,1024]{1,0:T(8,128)(2,1)}, u32[]{:S(2)}, u32[]{:S(2)}) collective-permute-start(bf16[64,1024]{1,0:T(8,128)(2,1)} %add_convert_fusion), channel_id=1, source_target_pairs={{0,64},{32,96},{64,0},{96,32},{1,65},{33,97},{65,1},{97,33},{2,66}... | collective-permute-start | bytes 393224 | tf_op jit(solution)/shard_map/ppermute | solution.py:48
  115.2 2.1 %fusion.15 = bf16[512,576]{0,1:T(8,128)(2,1)} fusion(f32[1024,512]{0,1:T(8,128)S(1)} %fusion.40, f32[1024,64]{0,1:T(8,128)S(1)} %fusion.18, bf16[512,576]{0,1:T(8,128)(2,1)} %collective-permute-done.1), kind=kLoop, calls=%fused_computation.32 | loop fusion | flops 1179648 | bytes 3538944 | tf_op jit(solution)/shard_map/convert_element_type | solution.py:159
  117.3 2.2 %copy.61 = bf16[512,576]{1,0:T(8,128)(2,1)} copy(bf16[512,576]{0,1:T(8,128)(2,1)} %fusion.15) | data formatting | bytes 1179648 | tf_op jit(solution)/shard_map/convert_element_type | solution.py:159
  119.4 5.5 %all-to-all-start.1 = ((bf16[32,16,576]{2,1,0:T(8,128)(2,1)}), bf16[32,16,576]{2,1,0:T(8,128)(2,1)S(1)}, u32[]{:S(2)}, u32[]{:S(2)}) async-start(bf16[32,16,576]{2,1,0:T(8,128)(2,1)} %bitcast.19), calls=%async_computation.1 | async-start | bytes 1310720 | tf_op jit(solution)/shard_map/all_to_all | solution.py:158
  127.5 2.7 %collective-permute-done.8 = bf16[64,1024]{1,0:T(8,128)(2,1)S(1)} collective-permute-done((bf16[64,1024]{1,0:T(8,128)(2,1)}, bf16[64,1024]{1,0:T(8,128)(2,1)S(1)}, u32[]{:S(2)}, u32[]{:S(2)}) %collective-permute-start.8) | collective-permute-done | bytes 131104 | tf_op jit(solution)/shard_map/ppermute | solution.py:48
  133.3 3.1 %collective-permute-start.9 = (bf16[256,1024]{1,0:T(8,128)(2,1)S(1)}, bf16[256,1024]{1,0:T(8,128)(2,1)}, u32[]{:S(2)}, u32[]{:S(2)}) collective-permute-start(bf16[256,1024]{1,0:T(8,128)(2,1)S(1)} %constant_dynamic-slice_fusion), channel_id=1, source_target_pairs={{0,128},{128,0},{1,129},{129,1},{2,130},{130,2},{3,131},{131,3},{4... | collective-permute-start | bytes 1572872 | tf_op jit(solution)/shard_map/ppermute | solution.py:51
  136.4 3.0 %fusion.17 = bf16[512,4,64]{0,2,1:T(8,128)(2,1)S(1)} fusion(bf16[1024,64,1]{0,1,2:T(8,128)(2,1)S(1)} %fusion.32, bf16[4,512,1024]{1,2,0:T(8,128)(2,1)} %copy-done.1), kind=kOutput, calls=%fused_computation.37 | convolution fusion | flops 268697600 | bytes 4587520 | tf_op jit(solution)/shard_map/hqk,kd->qhd/dot_general | solution.py:88
  141.4 3.5 %fusion.22 = f32[512,1024]{1,0:T(8,128)} fusion(s32[]{:T(128)S(6)} %select_n.58, bf16[256,1024]{1,0:T(8,128)(2,1)S(1)} %constant_dynamic-slice_fusion, bf16[256,1024]{1,0:T(8,128)(2,1)} %collective-permute-done.9), kind=kLoop, calls=%fused_computation.43 | loop fusion | flops 3145728 | bytes 3145732 | tf_op jit(solution)/shard_map/convert_element_type | solution.py:53
  (76 shorter events, 31.4 us)
Async XLA Ops:
  0.6 46.0 %copy-start = (bf16[512,1024]{1,0:T(8,128)(2,1)S(1)}, bf16[512,1024]{1,0:T(8,128)(2,1)}, u32[]{:S(2)}) copy-start(bf16[512,1024]{1,0:T(8,128)(2,1)} %param.19) | copy-start | bytes 3145732
  0.6 36.7 %copy-start.11 = (bf16[1,512,768]{2,1,0:T(8,128)(2,1)S(1)}, bf16[1,512,768]{2,1,0:T(8,128)(2,1)}, u32[]{:S(2)}) copy-start(bf16[1,512,768]{2,1,0:T(8,128)(2,1)} %param.17) | copy-start | bytes 2359300
  2.4 30.7 %all-to-all-start = ((bf16[32,16,576]{2,1,0:T(8,128)(2,1)}), bf16[32,16,576]{2,1,0:T(8,128)(2,1)S(1)}, u32[]{:S(2)}, u32[]{:S(2)}) async-start(bf16[32,16,576]{2,1,0:T(8,128)(2,1)} %broadcast_in_dim.42), calls=%async_computation | async-start | bytes 1310720 | tf_op jit(solution)/shard_map/all_to_all | solution.py:31
  33.4 8.6 %copy-start.7 = (bf16[512,576]{0,1:T(8,128)(2,1)}, bf16[512,576]{0,1:T(8,128)(2,1)S(1)}, u32[]{:S(2)}) copy-start(bf16[512,576]{0,1:T(8,128)(2,1)S(1)} %copy.44) | copy-start | bytes 1769476
  33.4 13.3 %collective-permute-start = (bf16[512,576]{0,1:T(8,128)(2,1)S(1)}, bf16[512,576]{0,1:T(8,128)(2,1)}, u32[]{:S(2)}, u32[]{:S(2)}) collective-permute-start(bf16[512,576]{0,1:T(8,128)(2,1)S(1)} %copy.44), channel_id=1, source_target_pairs={{0,32},{32,64},{64,96},{1,33},{33,65},{65,97},{2,34},{34,66},{66,9... | collective-permute-start | bytes 1769480 | tf_op jit(solution)/shard_map/ppermute | solution.py:22
  41.9 7.2 %copy-start.5 = (bf16[1,512,768]{1,2,0:T(8,128)(2,1)S(1)}, bf16[1,512,768]{1,2,0:T(8,128)(2,1)}, u32[]{:S(2)}) copy-start(bf16[1,512,768]{1,2,0:T(8,128)(2,1)} %copy.47) | copy-start | bytes 2359300
  49.2 23.4 %copy-start.3 = (bf16[1024,1024]{0,1:T(8,128)(2,1)}, bf16[1024,1024]{0,1:T(8,128)(2,1)S(1)}, u32[]{:S(2)}) copy-start(bf16[1024,1024]{0,1:T(8,128)(2,1)S(1)} %convolution_convert_fusion) | copy-start | bytes 6291460
  49.2 4.6 %copy-start.8 = (bf16[512,576]{0,1:T(8,128)(2,1)S(1)}, bf16[512,576]{0,1:T(8,128)(2,1)}, u32[]{:S(2)}) copy-start(bf16[512,576]{0,1:T(8,128)(2,1)} %copy-done.7) | copy-start | bytes 1769476
  65.5 4.8 %copy-start.10 = (bf16[1,512,512]{1,2,0:T(8,128)(2,1)S(1)}, bf16[1,512,512]{1,2,0:T(8,128)(2,1)}, u32[]{:S(2)}) copy-start(bf16[1,512,512]{1,2,0:T(8,128)(2,1)} %copy.50) | copy-start | bytes 1572868
  65.5 7.1 %slice-start = ((s8[8388608]{0:T(1024)(128)(4,1)}), s8[4194304]{0:T(1024)(128)(4,1)S(1)}, s32[]{:S(2)}) async-start(s8[8388608]{0:T(1024)(128)(4,1)} %bitcast.62), calls=%async_computation.2 | async-start | bytes 8388608
  70.3 2.3 %slice-start.1 = ((s8[8388608]{0:T(1024)(128)(4,1)}), s8[4194304]{0:T(1024)(128)(4,1)S(1)}, s32[]{:S(2)}) async-start(s8[8388608]{0:T(1024)(128)(4,1)} %bitcast.62), calls=%async_computation.3 | async-start | bytes 8388608
  74.5 8.5 %copy-start.1 = (bf16[4,512,1024]{1,2,0:T(8,128)(2,1)}, bf16[4,512,1024]{1,2,0:T(8,128)(2,1)S(1)}, u32[]{:S(2)}) copy-start(bf16[4,512,1024]{1,2,0:T(8,128)(2,1)S(1)} %fusion.1) | copy-start | bytes 12582916
  79.5 8.3 %collective-permute-start.2 = (bf16[256,1024]{1,0:T(8,128)(2,1)S(1)}, bf16[256,1024]{1,0:T(8,128)(2,1)S(1)}, u32[]{:S(2)}, u32[]{:S(2)}) collective-permute-start(bf16[256,1024]{1,0:T(8,128)(2,1)S(1)} %dynamic-slice_convert_fusion), channel_id=1, source_target_pairs={{0,128},{128,0},{1,129},{129,1},{2,130},{130,2},{3,131},{131,3},{4... | collective-permute-start | bytes 1572872 | tf_op jit(solution)/shard_map/ppermute | solution.py:40
  86.5 28.7 %collective-permute-start.1 = (bf16[512,576]{0,1:T(8,128)(2,1)}, bf16[512,576]{0,1:T(8,128)(2,1)}, u32[]{:S(2)}, u32[]{:S(2)}) collective-permute-start(bf16[512,576]{0,1:T(8,128)(2,1)} %fusion.16), channel_id=1, source_target_pairs={{32,0},{64,32},{96,64},{33,1},{65,33},{97,65},{34,2},{66,34},{98,6... | collective-permute-start | bytes 1769480 | tf_op jit(solution)/shard_map/ppermute | solution.py:22
  89.7 9.5 %collective-permute-start.3 = (bf16[64,1024]{1,0:T(8,128)(2,1)}, bf16[64,1024]{1,0:T(8,128)(2,1)}, u32[]{:S(2)}, u32[]{:S(2)}) collective-permute-start(bf16[64,1024]{1,0:T(8,128)(2,1)} %get-tuple-element.74), channel_id=1, source_target_pairs={{0,32},{32,64},{64,96},{96,0},{1,33},{33,65},{65,97},{97,1},{2,34}... | collective-permute-start | bytes 393224 | tf_op jit(solution)/shard_map/ppermute | solution.py:46
  92.7 10.3 %collective-permute-start.4 = (bf16[64,1024]{1,0:T(8,128)(2,1)}, bf16[64,1024]{1,0:T(8,128)(2,1)}, u32[]{:S(2)}, u32[]{:S(2)}) collective-permute-start(bf16[64,1024]{1,0:T(8,128)(2,1)} %get-tuple-element.76), channel_id=1, source_target_pairs={{0,64},{32,96},{64,0},{96,32},{1,65},{33,97},{65,1},{97,33},{2,66}... | collective-permute-start | bytes 393224 | tf_op jit(solution)/shard_map/ppermute | solution.py:46
  96.5 13.8 %collective-permute-start.5 = (bf16[64,1024]{1,0:T(8,128)(2,1)}, bf16[64,1024]{1,0:T(8,128)(2,1)}, u32[]{:S(2)}, u32[]{:S(2)}) collective-permute-start(bf16[64,1024]{1,0:T(8,128)(2,1)} %get-tuple-element.75), channel_id=1, source_target_pairs={{0,96},{32,0},{64,32},{96,64},{1,97},{33,1},{65,33},{97,65},{2,98}... | collective-permute-start | bytes 393224 | tf_op jit(solution)/shard_map/ppermute | solution.py:46
  112.2 13.5 %collective-permute-start.6 = (bf16[64,1024]{1,0:T(8,128)(2,1)}, bf16[64,1024]{1,0:T(8,128)(2,1)}, u32[]{:S(2)}, u32[]{:S(2)}) collective-permute-start(bf16[64,1024]{1,0:T(8,128)(2,1)} %add_convert_fusion), channel_id=1, source_target_pairs={{0,96},{32,0},{64,32},{96,64},{1,97},{33,1},{65,33},{97,65},{2,98}... | collective-permute-start | bytes 393224 | tf_op jit(solution)/shard_map/ppermute | solution.py:48
  113.1 13.5 %collective-permute-start.7 = (bf16[64,1024]{1,0:T(8,128)(2,1)}, bf16[64,1024]{1,0:T(8,128)(2,1)}, u32[]{:S(2)}, u32[]{:S(2)}) collective-permute-start(bf16[64,1024]{1,0:T(8,128)(2,1)} %add_convert_fusion), channel_id=1, source_target_pairs={{0,64},{32,96},{64,0},{96,32},{1,65},{33,97},{65,1},{97,33},{2,66}... | collective-permute-start | bytes 393224 | tf_op jit(solution)/shard_map/ppermute | solution.py:48
  119.4 25.5 %all-to-all-start.1 = ((bf16[32,16,576]{2,1,0:T(8,128)(2,1)}), bf16[32,16,576]{2,1,0:T(8,128)(2,1)S(1)}, u32[]{:S(2)}, u32[]{:S(2)}) async-start(bf16[32,16,576]{2,1,0:T(8,128)(2,1)} %bitcast.19), calls=%async_computation.1 | async-start | bytes 1310720 | tf_op jit(solution)/shard_map/all_to_all | solution.py:158
  124.9 5.3 %collective-permute-start.8 = (bf16[64,1024]{1,0:T(8,128)(2,1)}, bf16[64,1024]{1,0:T(8,128)(2,1)S(1)}, u32[]{:S(2)}, u32[]{:S(2)}) collective-permute-start(bf16[64,1024]{1,0:T(8,128)(2,1)} %add_convert_fusion), channel_id=1, source_target_pairs={{0,32},{32,64},{64,96},{96,0},{1,33},{33,65},{65,97},{97,1},{2,34}... | collective-permute-start | bytes 393224 | tf_op jit(solution)/shard_map/ppermute | solution.py:48
  131.2 8.2 %copy-start.4 = (bf16[1024,1024]{0,1:T(8,128)(2,1)S(1)}, bf16[1024,1024]{0,1:T(8,128)(2,1)}, u32[]{:S(2)}) copy-start(bf16[1024,1024]{0,1:T(8,128)(2,1)} %copy-done.3) | copy-start | bytes 6291460
  133.3 6.2 %copy-start.2 = (bf16[4,512,1024]{1,2,0:T(8,128)(2,1)S(1)}, bf16[4,512,1024]{1,2,0:T(8,128)(2,1)}, u32[]{:S(2)}) copy-start(bf16[4,512,1024]{1,2,0:T(8,128)(2,1)} %copy-done.1) | copy-start | bytes 12582916
  133.3 8.1 %collective-permute-start.9 = (bf16[256,1024]{1,0:T(8,128)(2,1)S(1)}, bf16[256,1024]{1,0:T(8,128)(2,1)}, u32[]{:S(2)}, u32[]{:S(2)}) collective-permute-start(bf16[256,1024]{1,0:T(8,128)(2,1)S(1)} %constant_dynamic-slice_fusion), channel_id=1, source_target_pairs={{0,128},{128,0},{1,129},{129,1},{2,130},{130,2},{3,131},{131,3},{4... | collective-permute-start | bytes 1572872 | tf_op jit(solution)/shard_map/ppermute | solution.py:51
  (2 other events, 2.9 us)

commit v2 on v1

v2 whole, which is shorter than its diff:
```python
import jax
import jax.numpy as jnp
from jax import lax
from jax.experimental import pallas as pl
from jax.experimental.pallas import tpu as pltpu
from jax.sharding import PartitionSpec as P

LATENT = 512
ROPE = 64
NOPE = 128
VDIM = 128
HEADS_DEV = 4
TOK_CTX = 512
DOC_MAX = 512
QUERIES = 256
KEYS = QUERIES + DOC_MAX
WINDOW = TOK_CTX + DOC_MAX
KV_WIDTH = NOPE + VDIM
FACTOR = (NOPE + ROPE) ** -0.5
LOG2E = 1.4426950408889634
N_CTX = 4
HEAD_DEVS = 32


def passed_along(array, axis, by):
    length = lax.axis_size(axis)
    pairs = [(i, i + by) for i in range(length) if 0 <= i + by < length]
    return lax.ppermute(array, axis, pairs)


def shift_pairs(by):
    return [(i, (i + by) % N_CTX) for i in range(N_CTX)]


def gathered_rows(rows):
    copies = jnp.broadcast_to(rows[None], (HEAD_DEVS, *rows.shape))
    return lax.all_to_all(copies, "head", 0, 0).reshape(-1, rows.shape[-1])


def summed_weight(part):
    core = lax.axis_index("dp")
    place = lax.axis_index("ctx")
    half, quarter = LATENT // 2, LATENT // 8
    swap = [(0, 1), (1, 0)]
    low = part
    other = lax.ppermute(lax.dynamic_slice_in_dim(low, (1 - core) * half, half), "dp", swap)
    mine = lax.dynamic_slice_in_dim(low, core * half, half).astype(jnp.float32)
    mine = mine + other.astype(jnp.float32)
    low = mine.astype(jnp.bfloat16)
    total = lax.dynamic_slice_in_dim(mine, place * quarter, quarter)
    for by in range(1, N_CTX):
        chunk = lax.dynamic_slice_in_dim(low, (place + by) % N_CTX * quarter, quarter)
        total = total + lax.ppermute(chunk, "ctx", shift_pairs(by)).astype(jnp.float32)
    low = total.astype(jnp.bfloat16)
    pieces = [low] + [lax.ppermute(low, "ctx", shift_pairs(by)) for by in range(1, N_CTX)]
    line = jnp.concatenate(pieces[::-1] + pieces[:0:-1], axis=0)
    mine = lax.dynamic_slice_in_dim(line, (N_CTX - 1 - place) * quarter, half)
    other = lax.ppermute(mine, "dp", swap)
    line = jnp.concatenate([mine, other, mine], axis=0)
    return lax.dynamic_slice_in_dim(line, core * half, LATENT).astype(jnp.float32)


NT = (((1,), (1,)), ((), ()))
NN = (((1,), (0,)), ((), ()))
TN = (((0,), (0,)), ((), ()))


def mm(left, right, dims):
    return lax.dot_general(left, right, dims, preferred_element_type=jnp.float32)


def attention_kernel(
    low_ref,
    prev_ref,
    own_ref,
    weight_ref,
    query_ref,
    grad_ref,
    d_query_ref,
    d_weight_ref,
    prev_term_ref,
    own_term_ref,
    bias_ref,
    turned_ref,
    term_ref,
    rope_ref,
):
    step = pl.program_id(0)
    low = jnp.bfloat16
    rows = jnp.concatenate([prev_ref[...], own_ref[...]], axis=0)
    latent = rows[:, :LATENT]
    key_rope = rows[:, LATENT:]
    blank = jnp.zeros((WINDOW, ROPE), low)

    @pl.when(step == 0)
    def _():
        turned_ref[...] = latent.T
        term_ref[...] = jnp.zeros_like(term_ref)
        rope_ref[...] = jnp.zeros_like(rope_ref)
        for tile in range(TOK_CTX // QUERIES):
            first = tile * QUERIES
            key = first + lax.broadcasted_iota(jnp.int32, (KEYS, QUERIES), 0)
            query = first + DOC_MAX + lax.broadcasted_iota(jnp.int32, (KEYS, QUERIES), 1)
            start = low_ref[:, first : first + QUERIES]
            allowed = (key >= start) & (key <= query)
            bias_ref[tile] = jnp.where(allowed, 0.0, -1e30)

    middle = []
    for head in range(2):
        head_weight = weight_ref[:, head * KV_WIDTH : (head + 1) * KV_WIDTH]
        kv_rows = mm(latent, head_weight, NN).astype(low)
        key_nope = kv_rows[:, :NOPE]
        value_rows = kv_rows[:, NOPE:]
        parts = [key_nope, key_rope, blank] if head == 0 else [blank, key_nope, key_rope]
        keys = jnp.concatenate(parts, axis=1)
        grads = []
        for tile in range(TOK_CTX // QUERIES):
            first = tile * QUERIES
            queries = query_ref[first : first + QUERIES, head * NOPE : head * NOPE + 2 * NOPE]
            upstream = grad_ref[first : first + QUERIES, head * VDIM : (head + 1) * VDIM]
            tile_keys = keys[first : first + KEYS]
            tile_values = value_rows[first : first + KEYS]
            scores = mm(tile_keys, queries, NT) * (FACTOR * LOG2E) + bias_ref[tile]
            weights = jnp.exp2(scores - jnp.max(scores, axis=0, keepdims=True))
            prob = weights * (1.0 / jnp.sum(weights, axis=0, keepdims=True))
            prob_low = prob.astype(low)
            dots = mm(tile_values, upstream, NT)
            delta = jnp.sum(prob_low.astype(jnp.float32) * dots, axis=0, keepdims=True)
            slope = (prob * (dots - delta)).astype(low)
            grads.append((mm(slope, queries, NN), mm(prob_low, upstream, NN)))
            d_query = mm(slope, tile_keys, TN) * FACTOR
            at = slice(first, first + QUERIES)
            if head == 0:
                d_query_ref[at, :NOPE] = d_query[:, :NOPE].astype(low)
                middle.append(d_query[:, NOPE:])
            else:
                d_query_ref[at, NOPE : 2 * NOPE] = (middle[tile] + d_query[:, :NOPE]).astype(low)
                d_query_ref[at, 2 * NOPE :] = d_query[:, NOPE:].astype(low)
        key_grad, value_grad = (
            jnp.concatenate(
                [one[:QUERIES], one[QUERIES:] + two[:-QUERIES], two[-QUERIES:]], axis=0
            )
            for one, two in zip(*grads)
        )
        key_grad = key_grad * FACTOR
        if head == 0:
            nope_grad, rope_grad = key_grad[:, :NOPE], key_grad[:, NOPE : NOPE + ROPE]
        else:
            nope_grad, rope_grad = key_grad[:, ROPE : ROPE + NOPE], key_grad[:, ROPE + NOPE :]
        rope_ref[...] += rope_grad
        kv_grad = jnp.concatenate([nope_grad.astype(low), value_grad.astype(low)], axis=1)
        d_weight_ref[:, head * KV_WIDTH : (head + 1) * KV_WIDTH] = mm(
            turned_ref[...], kv_grad, NN
        ).astype(low)
        term_ref[...] += mm(kv_grad, head_weight, NT)

    @pl.when(step == pl.num_programs(0) - 1)
    def _():
        prev_term_ref[:, :LATENT] = term_ref[:DOC_MAX].astype(low)
        prev_term_ref[:, LATENT:] = rope_ref[:DOC_MAX].astype(low)
        own_term_ref[:, :LATENT] = term_ref[DOC_MAX:]
        own_term_ref[:, LATENT:] = rope_ref[DOC_MAX:]


def attention(low_keys, prev_rows, own_rows, weight, query, grad_out):
    def whole(shape):
        return pl.BlockSpec(shape, lambda step: (0, 0))

    def columns(count, width):
        return pl.BlockSpec((count, width), lambda step: (0, step))

    columns_latent = LATENT + ROPE
    return pl.pallas_call(
        attention_kernel,
        grid=(HEADS_DEV // 2,),
        in_specs=[
            whole((1, TOK_CTX)),
            whole((DOC_MAX, columns_latent)),
            whole((TOK_CTX, columns_latent)),
            columns(LATENT, 2 * KV_WIDTH),
            columns(TOK_CTX, 2 * (NOPE + ROPE)),
            columns(TOK_CTX, 2 * VDIM),
        ],
        out_specs=[
            columns(TOK_CTX, 2 * (NOPE + ROPE)),
            columns(LATENT, 2 * KV_WIDTH),
            whole((DOC_MAX, columns_latent)),
            whole((TOK_CTX, columns_latent)),
        ],
        out_shape=[
            jax.ShapeDtypeStruct((TOK_CTX, HEADS_DEV * (NOPE + ROPE)), jnp.bfloat16),
            jax.ShapeDtypeStruct((LATENT, HEADS_DEV * KV_WIDTH), jnp.bfloat16),
            jax.ShapeDtypeStruct((DOC_MAX, columns_latent), jnp.bfloat16),
            jax.ShapeDtypeStruct((TOK_CTX, columns_latent), jnp.float32),
        ],
        scratch_shapes=[
            pltpu.VMEM((TOK_CTX // QUERIES, KEYS, QUERIES), jnp.float32),
            pltpu.VMEM((LATENT, WINDOW), jnp.bfloat16),
            pltpu.VMEM((WINDOW, LATENT), jnp.float32),
            pltpu.VMEM((WINDOW, ROPE), jnp.float32),
        ],
        compiler_params=pltpu.CompilerParams(vmem_limit_bytes=48 * 1024 * 1024),
        cost_estimate=pl.CostEstimate(
            flops=8_000_000_000, bytes_accessed=10_000_000, transcendentals=1_600_000
        ),
        name="attention",
    )(low_keys, prev_rows, own_rows, weight, query, grad_out)


def first_keys(lengths):
    starts = jnp.cumsum(lengths) - lengths
    base = lax.axis_index("ctx") * TOK_CTX
    positions = base + jnp.arange(TOK_CTX, dtype=jnp.int32)
    reached = jnp.where(starts[:, None] <= positions[None, :], starts[:, None], 0)
    return jnp.max(reached, axis=0, keepdims=True) - (base - DOC_MAX)


def on_device(query, kv_latent, kv_weight, grad_out, doc_lengths):
    own_rows = gathered_rows(kv_latent[0])
    prev_rows = passed_along(own_rows, "ctx", 1)
    d_query, weight_part, prev_term, own_term = attention(
        first_keys(doc_lengths[0]), prev_rows, own_rows, kv_weight, query[0], grad_out[0]
    )
    incoming = passed_along(prev_term, "ctx", -1)
    own_term = (own_term + incoming.astype(jnp.float32)).astype(jnp.bfloat16)
    terms = lax.all_to_all(own_term.reshape(HEAD_DEVS, -1, LATENT + ROPE), "head", 0, 0)
    d_latent = jnp.sum(terms.astype(jnp.float32), axis=0).astype(jnp.bfloat16)
    d_kv_weight = summed_weight(weight_part)
    return (d_query[None], d_latent[None], d_kv_weight)


def solution(mesh):
    return jax.shard_map(
        on_device,
        mesh=mesh,
        in_specs=(
            P("dp", "ctx", "head"),
            P("dp", ("ctx", "head"), None),
            P(None, "head"),
            P("dp", "ctx", "head"),
            P("dp", None),
        ),
        out_specs=(P("dp", "ctx", "head"), P("dp", ("ctx", "head"), None), P(None, "head")),
        check_vma=False,
    )
```

time: 146 us -> 125 us (0.86); the launches traced: 146 us -> 122 us
  matrix products: 32.3 us -> 0 us
  Pallas kernels: 0 us -> 14.8 us
  other arithmetic: 18.9 us -> 6.99 us
  waiting for transfers between devices: 38.4 us -> 50.3 us
  local copies, waits for them, and re-layouts: 15.1 us -> 7.88 us
  starting transfers between devices: 39.9 us -> 41.5 us
    dot_general x11 -> x0, matrix products: 21.3 us -> none  [the longest x1 4.54 us: attend(): jnp.einsum('qhd,khd->hqk', query_nope, key_nope, preferred_element_type=j...]
    pallas_call x0 -> x1, Pallas kernels: none -> 14.8 us  [attention(): pl.pallas_call(attention_kernel, grid=(HEADS_DEV // 2,), in_specs=[whole(...]
    ppermute x2, waiting for transfers between devices: 4.72 us -> 18.4 us  [passed_along(): return lax.ppermute(array, axis, pairs)]
    ppermute x3, waiting for transfers between devices: 13.8 us -> 1.35 us  [summed_weight(): lax.ppermute(chunk, 'ctx', shift_pairs(by)).astype(jnp.float32)]
    sub x1 -> x0, matrix products: 10.9 us -> none  [attend(): weights = jnp.where(allowed[None], jnp.exp(scores - top_score), 0.0)]
    unnamed x37 -> x16, local copies, waits for them, and re-layouts: 10 us -> 2.43 us
    convert_element_type x2 -> x1, other arithmetic: 6.82 us -> 0.96 us  [on_device(): own_term = (own_term + incoming.astype(jnp.float32)).astype(jnp.bfloat16)]
    all_to_all x1, waiting for transfers between devices: 0.01 us -> 5.36 us  [on_device(): lax.all_to_all(own_term.reshape(HEAD_DEVS, -1, LATENT + ROPE), 'head', 0, 0)]
  transfers between devices with their start and end apart: 12 -> 12, of which waited for: 6 -> 7; matrix products, arithmetic and copies ran while one was open for 21% -> 7% of each run, Pallas kernels for 0% -> 0%
where the time goes in v2:
time: 125 us; the launch traced here: 122 us
  waiting for transfers between devices  50.3 us (40%)
  starting transfers between devices  41.5 us (33%)
  Pallas kernels  14.8 us (12%)
  local copies, waits for them, and re-layouts  7.88 us (6%)
  other arithmetic  6.99 us (6%)
    all_to_all x1, waiting for transfers between devices, gathered_rows(): return lax.all_to_all(copies, 'head', 0, 0).reshape(-1, rows.shape[-1])  18.7 us
    ppermute x2, waiting for transfers between devices, passed_along(): return lax.ppermute(array, axis, pairs)  18.4 us
    pallas_call x1, Pallas kernels, attention(): pl.pallas_call(attention_kernel, grid=(HEADS_DEV // 2,), in_specs=[whole(...  14.8 us
    all_to_all x1, starting transfers between devices, gathered_rows(): return lax.all_to_all(copies, 'head', 0, 0).reshape(-1, rows.shape[-1])  12.2 us
    ppermute x3, starting transfers between devices, summed_weight(): lax.ppermute(low, 'ctx', shift_pairs(by))  7.12 us
    ppermute x3, starting transfers between devices, summed_weight(): lax.ppermute(chunk, 'ctx', shift_pairs(by)).astype(jnp.float32)  5.97 us
    all_to_all x1, starting transfers between devices, on_device(): lax.all_to_all(own_term.reshape(HEAD_DEVS, -1, LATENT + ROPE), 'head', 0, 0)  5.52 us
    all_to_all x1, waiting for transfers between devices, on_device(): lax.all_to_all(own_term.reshape(HEAD_DEVS, -1, LATENT + ROPE), 'head', 0, 0)  5.36 us
  transfers between devices with their start and end apart: 12, of which 7 were waited for; matrix products, arithmetic and copies ran while one was open for 7% of the time, Pallas kernels for 0%

profile of v2, /device:TPU:1, one launch (start us, length us, event | category | flops | bytes accessed | tf_op | source)
XLA Modules:
  0.0 122.4 jit_solution(15185289491126172343)
XLA Ops:
  0.6 1.6 %broadcast_in_dim.29 = bf16[32,16,576]{2,1,0:T(8,128)(2,1)} broadcast(bf16[16,576]{1,0:T(8,128)(2,1)} %bitcast.17), dimensions={1,2} | broadcast | bytes 608256 | tf_op jit(solution)/shard_map/broadcast_in_dim | solution.py:36
  2.3 12.2 %all-to-all-start = ((bf16[32,16,576]{2,1,0:T(8,128)(2,1)}), bf16[32,16,576]{2,1,0:T(8,128)(2,1)S(1)}, u32[]{:S(2)}, u32[]{:S(2)}) async-start(bf16[32,16,576]{2,1,0:T(8,128)(2,1)} %broadcast_in_dim.29), calls=%async_computation | async-start | bytes 1310720 | tf_op jit(solution)/shard_map/all_to_all | solution.py:37
  14.4 18.7 %all-to-all-done = bf16[32,16,576]{2,1,0:T(8,128)(2,1)S(1)} async-done(((bf16[32,16,576]{2,1,0:T(8,128)(2,1)}), bf16[32,16,576]{2,1,0:T(8,128)(2,1)S(1)}, u32[]{:S(2)}, u32[]{:S(2)}) %all-to-all-start) | async-done | bytes 589856 | tf_op jit(solution)/shard_map/all_to_all | solution.py:37
  33.4 3.2 %collective-permute-start = (bf16[512,576]{0,1:T(8,128)(2,1)S(1)}, bf16[512,576]{0,1:T(8,128)(2,1)S(1)}, u32[]{:S(2)}, u32[]{:S(2)}) collective-permute-start(bf16[512,576]{0,1:T(8,128)(2,1)S(1)} %copy.16), channel_id=1, source_target_pairs={{0,32},{32,64},{64,96},{1,33},{33,65},{65,97},{2,34},{34,66},{66,9... | collective-permute-start | bytes 1769480 | tf_op jit(solution)/shard_map/ppermute | solution.py:28
  36.9 9.7 %collective-permute-done = bf16[512,576]{0,1:T(8,128)(2,1)S(1)} collective-permute-done((bf16[512,576]{0,1:T(8,128)(2,1)S(1)}, bf16[512,576]{0,1:T(8,128)(2,1)S(1)}, u32[]{:S(2)}, u32[]{:S(2)}) %collective-permute-start) | collective-permute-done | bytes 589856 | tf_op jit(solution)/shard_map/ppermute | solution.py:28
  47.0 1.2 copy-done
  48.2 1.1 copy-done.1
  49.3 14.8 %attention.1 = (bf16[512,768]{1,0:T(8,128)(2,1)}, bf16[512,1024]{1,0:T(8,128)(2,1)S(1)}, bf16[512,576]{1,0:T(8,128)(2,1)S(1)}, f32[512,576]{1,0:T(8,128)}) custom-call(s32[1,512]{1,0:T(1,128)S(1)} %bitcast.13, bf16[512,576]{1,0:T(8,128)(2,1)S(1)} %copy.17.prev_ref, bf16[512,576]{1,0:T(8,128)(2,1)S(1)} %bitcast.12, bf16[512,1024]{1,0:T(8,128)(2,1)S(1)} %copy-done, ...), custom_call_target="tpu_custom_call" | custom-call | flops 8000000000 | bytes 10000000 | tf_op jit(solution)/shard_map/attention/pallas_call | solution.py:173
  64.2 3.5 %collective-permute-start.2 = (bf16[256,1024]{1,0:T(8,128)(2,1)S(1)}, bf16[256,1024]{1,0:T(8,128)(2,1)}, u32[]{:S(2)}, u32[]{:S(2)}) collective-permute-start(bf16[256,1024]{1,0:T(8,128)(2,1)S(1)} %constant_dynamic-slice_fusion.4), channel_id=1, source_target_pairs={{0,128},{128,0},{1,129},{129,1},{2,130},{130,2},{3,131},{131,3},{4... | collective-permute-start | bytes 1572872 | tf_op jit(solution)/shard_map/ppermute | solution.py:46
  67.6 1.1 copy.18
  68.7 1.3 %collective-permute-start.1 = (bf16[512,576]{0,1:T(8,128)(2,1)}, bf16[512,576]{0,1:T(8,128)(2,1)}, u32[]{:S(2)}, u32[]{:S(2)}) collective-permute-start(bf16[512,576]{0,1:T(8,128)(2,1)} %copy.18), channel_id=1, source_target_pairs={{32,0},{64,32},{96,64},{33,1},{65,33},{97,65},{34,2},{66,34},{98,6... | collective-permute-start | bytes 1769480 | tf_op jit(solution)/shard_map/ppermute | solution.py:28
  70.0 1.4 %fusion.3 = (bf16[256,1024]{1,0:T(8,128)(2,1)S(1)}, f32[256,1024]{1,0:T(8,128)S(1)}) fusion(bf16[256,1024]{1,0:T(8,128)(2,1)} %collective-permute-done.2, bf16[512,1024]{1,0:T(8,128)(2,1)S(1)} %get-tuple-element.10, s32[]{:T(128)S(6)} %select_n.44), kind=kLoop, calls=%fused_computation.25 | loop fusion | flops 1048576 | bytes 2621444 | tf_op jit(solution)/shard_map/convert_element_type | solution.py:49
  72.1 5.4 %collective-permute-start.5 = (bf16[64,1024]{1,0:T(8,128)(2,1)}, bf16[64,1024]{1,0:T(8,128)(2,1)S(1)}, u32[]{:S(2)}, u32[]{:S(2)}) collective-permute-start(bf16[64,1024]{1,0:T(8,128)(2,1)} %get-tuple-element.14), channel_id=1, source_target_pairs={{0,96},{32,0},{64,32},{96,64},{1,97},{33,1},{65,33},{97,65},{2,98}... | collective-permute-start | bytes 393224 | tf_op jit(solution)/shard_map/ppermute | solution.py:53
  78.1 8.7 %collective-permute-done.1 = bf16[512,576]{0,1:T(8,128)(2,1)} collective-permute-done((bf16[512,576]{0,1:T(8,128)(2,1)}, bf16[512,576]{0,1:T(8,128)(2,1)}, u32[]{:S(2)}, u32[]{:S(2)}) %collective-permute-start.1) | collective-permute-done | bytes 589856 | tf_op jit(solution)/shard_map/ppermute | solution.py:28
  86.8 1.4 %copy.19 = bf16[512,576]{1,0:T(8,128)(2,1)S(1)} copy(bf16[512,576]{0,1:T(8,128)(2,1)} %collective-permute-done.1) | data formatting | bytes 1179648 | tf_op jit(solution)/shard_map/ppermute | solution.py:28
  88.1 1.3 %collective-permute-done.5 = bf16[64,1024]{1,0:T(8,128)(2,1)S(1)} collective-permute-done((bf16[64,1024]{1,0:T(8,128)(2,1)}, bf16[64,1024]{1,0:T(8,128)(2,1)S(1)}, u32[]{:S(2)}, u32[]{:S(2)}) %collective-permute-start.5) | collective-permute-done | bytes 131104 | tf_op jit(solution)/shard_map/ppermute | solution.py:53
  90.5 5.5 %collective-permute-start.6 = (bf16[64,1024]{1,0:T(8,128)(2,1)S(1)}, bf16[64,1024]{1,0:T(8,128)(2,1)S(1)}, u32[]{:S(2)}, u32[]{:S(2)}) collective-permute-start(bf16[64,1024]{1,0:T(8,128)(2,1)S(1)} %add_convert_fusion.1), channel_id=1, source_target_pairs={{0,96},{32,0},{64,32},{96,64},{1,97},{33,1},{65,33},{97,65},{2,98}... | collective-permute-start | bytes 393224 | tf_op jit(solution)/shard_map/ppermute | solution.py:55
  95.9 1.6 %collective-permute-start.7 = (bf16[64,1024]{1,0:T(8,128)(2,1)S(1)}, bf16[64,1024]{1,0:T(8,128)(2,1)S(1)}, u32[]{:S(2)}, u32[]{:S(2)}) collective-permute-start(bf16[64,1024]{1,0:T(8,128)(2,1)S(1)} %add_convert_fusion.1), channel_id=1, source_target_pairs={{0,64},{32,96},{64,0},{96,32},{1,65},{33,97},{65,1},{97,33},{2,66}... | collective-permute-start | bytes 393224 | tf_op jit(solution)/shard_map/ppermute | solution.py:55
  98.5 5.5 %all-to-all-start.1 = ((bf16[32,16,576]{2,1,0:T(8,128)(2,1)}), bf16[32,16,576]{2,1,0:T(8,128)(2,1)S(1)}, u32[]{:S(2)}, u32[]{:S(2)}) async-start(bf16[32,16,576]{2,1,0:T(8,128)(2,1)} %bitcast.8), calls=%async_computation.1 | async-start | bytes 1310720 | tf_op jit(solution)/shard_map/all_to_all | solution.py:226
  104.1 5.0 %collective-permute-done.8 = bf16[64,1024]{1,0:T(8,128)(2,1)S(1)} collective-permute-done((bf16[64,1024]{1,0:T(8,128)(2,1)S(1)}, bf16[64,1024]{1,0:T(8,128)(2,1)S(1)}, u32[]{:S(2)}, u32[]{:S(2)}) %collective-permute-start.8) | collective-permute-done | bytes 131104 | tf_op jit(solution)/shard_map/ppermute | solution.py:55
  109.2 2.9 %collective-permute-start.9 = (bf16[256,1024]{1,0:T(8,128)(2,1)S(1)}, bf16[256,1024]{1,0:T(8,128)(2,1)S(1)}, u32[]{:S(2)}, u32[]{:S(2)}) collective-permute-start(bf16[256,1024]{1,0:T(8,128)(2,1)S(1)} %constant_dynamic-slice_fusion), channel_id=1, source_target_pairs={{0,128},{128,0},{1,129},{129,1},{2,130},{130,2},{3,131},{131,3},{4... | collective-permute-start | bytes 1572872 | tf_op jit(solution)/shard_map/ppermute | solution.py:58
  112.1 1.5 %collective-permute-done.9 = bf16[256,1024]{1,0:T(8,128)(2,1)S(1)} collective-permute-done((bf16[256,1024]{1,0:T(8,128)(2,1)S(1)}, bf16[256,1024]{1,0:T(8,128)(2,1)S(1)}, u32[]{:S(2)}, u32[]{:S(2)}) %collective-permute-start.9) | collective-permute-done | bytes 524320 | tf_op jit(solution)/shard_map/ppermute | solution.py:58
  113.6 2.7 %fusion.2 = f32[512,1024]{1,0:T(8,128)} fusion(s32[]{:T(128)S(6)} %select_n.54, bf16[256,1024]{1,0:T(8,128)(2,1)S(1)} %constant_dynamic-slice_fusion, bf16[256,1024]{1,0:T(8,128)(2,1)S(1)} %collective-permute-done.9), kind=kLoop, calls=%fused_computation.6 | loop fusion | flops 3145728 | bytes 3145732 | tf_op jit(solution)/shard_map/convert_element_type | solution.py:60
  116.4 5.4 %all-to-all-done.1 = bf16[32,16,576]{2,1,0:T(8,128)(2,1)S(1)} async-done(((bf16[32,16,576]{2,1,0:T(8,128)(2,1)}), bf16[32,16,576]{2,1,0:T(8,128)(2,1)S(1)}, u32[]{:S(2)}, u32[]{:S(2)}) %all-to-all-start.1) | async-done | bytes 589856 | tf_op jit(solution)/shard_map/all_to_all | solution.py:226
  (38 shorter events, 5.1 us)
Async XLA Ops:
  0.6 35.9 %copy-start.4 = (s32[1,16]{1,0:T(1,128)S(1)}, s32[1,16]{1,0:T(1,128)}, u32[]{:S(2)}) copy-start(s32[1,16]{1,0:T(1,128)} %param.9) | copy-start | bytes 196
  2.3 44.7 %copy-start.2 = (bf16[1,512,512]{2,1,0:T(8,128)(2,1)S(1)}, bf16[1,512,512]{2,1,0:T(8,128)(2,1)}, u32[]{:S(2)}) copy-start(bf16[1,512,512]{2,1,0:T(8,128)(2,1)} %param.8) | copy-start | bytes 1572868
  2.3 30.9 %all-to-all-start = ((bf16[32,16,576]{2,1,0:T(8,128)(2,1)}), bf16[32,16,576]{2,1,0:T(8,128)(2,1)S(1)}, u32[]{:S(2)}, u32[]{:S(2)}) async-start(bf16[32,16,576]{2,1,0:T(8,128)(2,1)} %broadcast_in_dim.29), calls=%async_computation | async-start | bytes 1310720 | tf_op jit(solution)/shard_map/all_to_all | solution.py:37
  33.4 13.3 %collective-permute-start = (bf16[512,576]{0,1:T(8,128)(2,1)S(1)}, bf16[512,576]{0,1:T(8,128)(2,1)S(1)}, u32[]{:S(2)}, u32[]{:S(2)}) collective-permute-start(bf16[512,576]{0,1:T(8,128)(2,1)S(1)} %copy.16), channel_id=1, source_target_pairs={{0,32},{32,64},{64,96},{1,33},{33,65},{65,97},{2,34},{34,66},{66,9... | collective-permute-start | bytes 1769480 | tf_op jit(solution)/shard_map/ppermute | solution.py:28
  47.0 1.2 %copy-start = (bf16[512,1024]{1,0:T(8,128)(2,1)S(1)}, bf16[512,1024]{1,0:T(8,128)(2,1)}, u32[]{:S(2)}) copy-start(bf16[512,1024]{1,0:T(8,128)(2,1)} %weight_ref.1) | copy-start | bytes 3145732
  48.2 1.1 copy-start.1
  64.2 5.9 %collective-permute-start.2 = (bf16[256,1024]{1,0:T(8,128)(2,1)S(1)}, bf16[256,1024]{1,0:T(8,128)(2,1)}, u32[]{:S(2)}, u32[]{:S(2)}) collective-permute-start(bf16[256,1024]{1,0:T(8,128)(2,1)S(1)} %constant_dynamic-slice_fusion.4), channel_id=1, source_target_pairs={{0,128},{128,0},{1,129},{129,1},{2,130},{130,2},{3,131},{131,3},{4... | collective-permute-start | bytes 1572872 | tf_op jit(solution)/shard_map/ppermute | solution.py:46
  68.7 18.1 %collective-permute-start.1 = (bf16[512,576]{0,1:T(8,128)(2,1)}, bf16[512,576]{0,1:T(8,128)(2,1)}, u32[]{:S(2)}, u32[]{:S(2)}) collective-permute-start(bf16[512,576]{0,1:T(8,128)(2,1)} %copy.18), channel_id=1, source_target_pairs={{32,0},{64,32},{96,64},{33,1},{65,33},{97,65},{34,2},{66,34},{98,6... | collective-permute-start | bytes 1769480 | tf_op jit(solution)/shard_map/ppermute | solution.py:28
  70.0 27.5 %copy-start.3 = (f32[512,576]{1,0:T(8,128)S(1)}, f32[512,576]{1,0:T(8,128)}, u32[]{:S(2)}) copy-start(f32[512,576]{1,0:T(8,128)} %get-tuple-element.8) | copy-start | bytes 3538948
  72.1 17.4 %collective-permute-start.5 = (bf16[64,1024]{1,0:T(8,128)(2,1)}, bf16[64,1024]{1,0:T(8,128)(2,1)S(1)}, u32[]{:S(2)}, u32[]{:S(2)}) collective-permute-start(bf16[64,1024]{1,0:T(8,128)(2,1)} %get-tuple-element.14), channel_id=1, source_target_pairs={{0,96},{32,0},{64,32},{96,64},{1,97},{33,1},{65,33},{97,65},{2,98}... | collective-permute-start | bytes 393224 | tf_op jit(solution)/shard_map/ppermute | solution.py:53
  77.5 12.0 %collective-permute-start.4 = (bf16[64,1024]{1,0:T(8,128)(2,1)S(1)}, bf16[64,1024]{1,0:T(8,128)(2,1)S(1)}, u32[]{:S(2)}, u32[]{:S(2)}) collective-permute-start(bf16[64,1024]{1,0:T(8,128)(2,1)S(1)} %get-tuple-element.15), channel_id=1, source_target_pairs={{0,64},{32,96},{64,0},{96,32},{1,65},{33,97},{65,1},{97,33},{2,66}... | collective-permute-start | bytes 393224 | tf_op jit(solution)/shard_map/ppermute | solution.py:53
  77.5 12.0 %collective-permute-start.3 = (bf16[64,1024]{1,0:T(8,128)(2,1)S(1)}, bf16[64,1024]{1,0:T(8,128)(2,1)}, u32[]{:S(2)}, u32[]{:S(2)}) collective-permute-start(bf16[64,1024]{1,0:T(8,128)(2,1)S(1)} %get-tuple-element.13), channel_id=1, source_target_pairs={{0,32},{32,64},{64,96},{96,0},{1,33},{33,65},{65,97},{97,1},{2,34}... | collective-permute-start | bytes 393224 | tf_op jit(solution)/shard_map/ppermute | solution.py:53
  90.5 13.6 %collective-permute-start.6 = (bf16[64,1024]{1,0:T(8,128)(2,1)S(1)}, bf16[64,1024]{1,0:T(8,128)(2,1)S(1)}, u32[]{:S(2)}, u32[]{:S(2)}) collective-permute-start(bf16[64,1024]{1,0:T(8,128)(2,1)S(1)} %add_convert_fusion.1), channel_id=1, source_target_pairs={{0,96},{32,0},{64,32},{96,64},{1,97},{33,1},{65,33},{97,65},{2,98}... | collective-permute-start | bytes 393224 | tf_op jit(solution)/shard_map/ppermute | solution.py:55
  95.9 8.2 %collective-permute-start.7 = (bf16[64,1024]{1,0:T(8,128)(2,1)S(1)}, bf16[64,1024]{1,0:T(8,128)(2,1)S(1)}, u32[]{:S(2)}, u32[]{:S(2)}) collective-permute-start(bf16[64,1024]{1,0:T(8,128)(2,1)S(1)} %add_convert_fusion.1), channel_id=1, source_target_pairs={{0,64},{32,96},{64,0},{96,32},{1,65},{33,97},{65,1},{97,33},{2,66}... | collective-permute-start | bytes 393224 | tf_op jit(solution)/shard_map/ppermute | solution.py:55
  98.5 23.2 %all-to-all-start.1 = ((bf16[32,16,576]{2,1,0:T(8,128)(2,1)}), bf16[32,16,576]{2,1,0:T(8,128)(2,1)S(1)}, u32[]{:S(2)}, u32[]{:S(2)}) async-start(bf16[32,16,576]{2,1,0:T(8,128)(2,1)} %bitcast.8), calls=%async_computation.1 | async-start | bytes 1310720 | tf_op jit(solution)/shard_map/all_to_all | solution.py:226
  104.0 5.1 %collective-permute-start.8 = (bf16[64,1024]{1,0:T(8,128)(2,1)S(1)}, bf16[64,1024]{1,0:T(8,128)(2,1)S(1)}, u32[]{:S(2)}, u32[]{:S(2)}) collective-permute-start(bf16[64,1024]{1,0:T(8,128)(2,1)S(1)} %add_convert_fusion.1), channel_id=1, source_target_pairs={{0,32},{32,64},{64,96},{96,0},{1,33},{33,65},{65,97},{97,1},{2,34}... | collective-permute-start | bytes 393224 | tf_op jit(solution)/shard_map/ppermute | solution.py:55
  109.2 4.4 %collective-permute-start.9 = (bf16[256,1024]{1,0:T(8,128)(2,1)S(1)}, bf16[256,1024]{1,0:T(8,128)(2,1)S(1)}, u32[]{:S(2)}, u32[]{:S(2)}) collective-permute-start(bf16[256,1024]{1,0:T(8,128)(2,1)S(1)} %constant_dynamic-slice_fusion), channel_id=1, source_target_pairs={{0,128},{128,0},{1,129},{129,1},{2,130},{130,2},{3,131},{131,3},{4... | collective-permute-start | bytes 1572872 | tf_op jit(solution)/shard_map/ppermute | solution.py:58

commit v3 on v2

v3 whole, which is shorter than its diff:
```python
import jax
import jax.numpy as jnp
from jax import lax
from jax.experimental import pallas as pl
from jax.experimental.pallas import tpu as pltpu
from jax.sharding import PartitionSpec as P

LATENT = 512
ROPE = 64
NOPE = 128
VDIM = 128
HEADS_DEV = 4
TOK_CTX = 512
DOC_MAX = 512
QUERIES = 256
KEYS = QUERIES + DOC_MAX
WINDOW = TOK_CTX + DOC_MAX
KV_WIDTH = NOPE + VDIM
FACTOR = (NOPE + ROPE) ** -0.5
LOG2E = 1.4426950408889634
N_CTX = 4
Y = 4
Z = 8
ROWS = 16
PART = LATENT // 8


def passed_along(array, by):
    pairs = [(i, i + by) for i in range(N_CTX) if 0 <= i + by < N_CTX]
    return lax.ppermute(array, "ctx", pairs)


def turned(array, axis, by):
    if axis == "ctx":
        return lax.ppermute(array, axis, [(i, (i + by) % N_CTX) for i in range(N_CTX)])
    pairs = [(i, i // Y * Y + (i + by) % Y) for i in range(Z * Y)]
    return lax.ppermute(array, axis, pairs)


def summed_weight(kept, given):
    low = jnp.bfloat16
    swap = [(0, 1), (1, 0)]
    other = lax.ppermute(given, "dp", swap)
    mine = [
        kept[by * PART : (by + 1) * PART].astype(jnp.float32)
        + other[by * PART : (by + 1) * PART].astype(jnp.float32)
        for by in range(N_CTX)
    ]
    total = mine[0]
    for by in range(1, N_CTX):
        total = total + turned(mine[by].astype(low), "ctx", by).astype(jnp.float32)
    total = total.astype(low)
    pieces = [total] + [turned(total, "ctx", by) for by in range(1, N_CTX)]
    pieces = jnp.stack(pieces)
    return placed(pieces, lax.ppermute(pieces, "dp", swap))


def place_kernel(core_ref, place_ref, mine_ref, other_ref, out_ref):
    core, place = core_ref[0], place_ref[0]
    for by in range(N_CTX):
        at = lax.rem(place - by + N_CTX, N_CTX)
        out_ref[core * N_CTX + at] = mine_ref[by].astype(jnp.float32)
        out_ref[(1 - core) * N_CTX + at] = other_ref[by].astype(jnp.float32)


def place_of(axis):
    return lax.axis_index(axis).astype(jnp.int32).reshape(1)


def placed(mine, other):
    vmem = pl.BlockSpec(memory_space=pltpu.VMEM)
    smem = pl.BlockSpec(memory_space=pltpu.SMEM)
    whole = pl.pallas_call(
        place_kernel,
        in_specs=[smem, smem, vmem, vmem],
        out_specs=vmem,
        out_shape=jax.ShapeDtypeStruct((2 * N_CTX, *mine.shape[1:]), jnp.float32),
        compiler_params=pltpu.CompilerParams(vmem_limit_bytes=16 * 1024 * 1024),
        name="placed",
    )(place_of("dp"), place_of("ctx"), mine, other)
    return whole.reshape(LATENT, -1)


NT = (((1,), (1,)), ((), ()))
NN = (((1,), (0,)), ((), ()))
TN = (((0,), (0,)), ((), ()))


def mm(left, right, dims):
    return lax.dot_general(left, right, dims, preferred_element_type=jnp.float32)


def attention_kernel(
    spot_ref,
    low_ref,
    piece0_ref,
    piece1_ref,
    piece2_ref,
    piece3_ref,
    weight_ref,
    query_ref,
    grad_ref,
    d_query_ref,
    kept_ref,
    given_ref,
    term0_ref,
    term1_ref,
    term2_ref,
    term3_ref,
    rows_ref,
    bias_ref,
    plain_ref,
    turned_ref,
    term_ref,
    rope_ref,
):
    step = pl.program_id(0)
    low = jnp.bfloat16
    core, place, spot = spot_ref[0], spot_ref[1], spot_ref[2]

    @pl.when(step == 0)
    def _():
        for by, piece in enumerate([piece0_ref, piece1_ref, piece2_ref, piece3_ref]):
            at = lax.rem(spot - by + Y, Y)
            rows_ref[:Z, at] = piece[:, 0]
            rows_ref[Z:, at] = piece[:, 1]

    rows = rows_ref[...].reshape(WINDOW, LATENT + ROPE)
    latent = rows[:, :LATENT]
    key_rope = rows[:, LATENT:]
    blank = jnp.zeros((WINDOW, ROPE), low)

    @pl.when(step == 0)
    def _():
        plain_ref[...] = latent.T.reshape(2 * N_CTX, PART, WINDOW)
        for by in range(N_CTX):
            at = lax.rem(place + by, N_CTX)
            turned_ref[by] = plain_ref[core * N_CTX + at]
            turned_ref[N_CTX + by] = plain_ref[(1 - core) * N_CTX + at]
        term_ref[...] = jnp.zeros_like(term_ref)
        rope_ref[...] = jnp.zeros_like(rope_ref)
        for tile in range(TOK_CTX // QUERIES):
            first = tile * QUERIES
            key = first + lax.broadcasted_iota(jnp.int32, (KEYS, QUERIES), 0)
            query = first + DOC_MAX + lax.broadcasted_iota(jnp.int32, (KEYS, QUERIES), 1)
            start = low_ref[:, first : first + QUERIES]
            allowed = (key >= start) & (key <= query)
            bias_ref[tile] = jnp.where(allowed, 0.0, -1e30)

    middle = []
    for head in range(2):
        head_weight = weight_ref[:, head * KV_WIDTH : (head + 1) * KV_WIDTH]
        kv_rows = mm(latent, head_weight, NN).astype(low)
        key_nope = kv_rows[:, :NOPE]
        value_rows = kv_rows[:, NOPE:]
        parts = [key_nope, key_rope, blank] if head == 0 else [blank, key_nope, key_rope]
        keys = jnp.concatenate(parts, axis=1)
        grads = []
        for tile in range(TOK_CTX // QUERIES):
            first = tile * QUERIES
            queries = query_ref[first : first + QUERIES, head * NOPE : head * NOPE + 2 * NOPE]
            upstream = grad_ref[first : first + QUERIES, head * VDIM : (head + 1) * VDIM]
            tile_keys = keys[first : first + KEYS]
            tile_values = value_rows[first : first + KEYS]
            scores = mm(tile_keys, queries, NT) * (FACTOR * LOG2E) + bias_ref[tile]
            weights = jnp.exp2(scores - jnp.max(scores, axis=0, keepdims=True))
            prob = weights * (1.0 / jnp.sum(weights, axis=0, keepdims=True))
            prob_low = prob.astype(low)
            dots = mm(tile_values, upstream, NT)
            delta = jnp.sum(prob_low.astype(jnp.float32) * dots, axis=0, keepdims=True)
            slope = (prob * (dots - delta)).astype(low)
            grads.append((mm(slope, queries, NN), mm(prob_low, upstream, NN)))
            d_query = mm(slope, tile_keys, TN) * FACTOR
            at = slice(first, first + QUERIES)
            if head == 0:
                d_query_ref[at, :NOPE] = d_query[:, :NOPE].astype(low)
                middle.append(d_query[:, NOPE:])
            else:
                d_query_ref[at, NOPE : 2 * NOPE] = (middle[tile] + d_query[:, :NOPE]).astype(low)
                d_query_ref[at, 2 * NOPE :] = d_query[:, NOPE:].astype(low)
        key_grad, value_grad = (
            jnp.concatenate(
                [one[:QUERIES], one[QUERIES:] + two[:-QUERIES], two[-QUERIES:]], axis=0
            )
            for one, two in zip(*grads)
        )
        key_grad = key_grad * FACTOR
        if head == 0:
            nope_grad, rope_grad = key_grad[:, :NOPE], key_grad[:, NOPE : NOPE + ROPE]
        else:
            nope_grad, rope_grad = key_grad[:, ROPE : ROPE + NOPE], key_grad[:, ROPE + NOPE :]
        rope_ref[...] += rope_grad.reshape(rope_ref.shape)
        kv_grad = jnp.concatenate([nope_grad.astype(low), value_grad.astype(low)], axis=1)
        part = mm(turned_ref[...].reshape(LATENT, WINDOW), kv_grad, NN).astype(low)
        kept_ref[:, head * KV_WIDTH : (head + 1) * KV_WIDTH] = part[: LATENT // 2]
        given_ref[:, head * KV_WIDTH : (head + 1) * KV_WIDTH] = part[LATENT // 2 :]
        term_ref[...] += mm(kv_grad, head_weight, NT).reshape(term_ref.shape)

    @pl.when(step == pl.num_programs(0) - 1)
    def _():
        for by, out in enumerate([term0_ref, term1_ref, term2_ref, term3_ref]):
            at = lax.rem(spot + by, Y)
            term, rope = term_ref[:, at].astype(out.dtype), rope_ref[:, at].astype(out.dtype)
            for half in range(2):
                out[:, half, :, :LATENT] = term[half * Z : (half + 1) * Z]
                out[:, half, :, LATENT:] = rope[half * Z : (half + 1) * Z]


def attention(spot, low_keys, pieces, weight, query, grad_out):
    def whole(shape):
        return pl.BlockSpec(shape, lambda step: (0,) * len(shape))

    def columns(count, width):
        return pl.BlockSpec((count, width), lambda step: (0, step))

    piece = (Z, 2, ROWS, LATENT + ROPE)
    return pl.pallas_call(
        attention_kernel,
        grid=(HEADS_DEV // 2,),
        in_specs=[
            pl.BlockSpec(memory_space=pltpu.SMEM),
            whole((1, TOK_CTX)),
            *[whole(piece)] * Y,
            columns(LATENT, 2 * KV_WIDTH),
            columns(TOK_CTX, 2 * (NOPE + ROPE)),
            columns(TOK_CTX, 2 * VDIM),
        ],
        out_specs=[
            columns(TOK_CTX, 2 * (NOPE + ROPE)),
            columns(LATENT // 2, 2 * KV_WIDTH),
            columns(LATENT // 2, 2 * KV_WIDTH),
            *[whole(piece)] * Y,
        ],
        out_shape=[
            jax.ShapeDtypeStruct((TOK_CTX, HEADS_DEV * (NOPE + ROPE)), jnp.bfloat16),
            jax.ShapeDtypeStruct((LATENT // 2, HEADS_DEV * KV_WIDTH), jnp.bfloat16),
            jax.ShapeDtypeStruct((LATENT // 2, HEADS_DEV * KV_WIDTH), jnp.bfloat16),
            jax.ShapeDtypeStruct(piece, jnp.float32),
            *[jax.ShapeDtypeStruct(piece, jnp.bfloat16)] * (Y - 1),
        ],
        scratch_shapes=[
            pltpu.VMEM((2 * Z, Y, ROWS, LATENT + ROPE), jnp.bfloat16),
            pltpu.VMEM((TOK_CTX // QUERIES, KEYS, QUERIES), jnp.float32),
            pltpu.VMEM((2 * N_CTX, PART, WINDOW), jnp.bfloat16),
            pltpu.VMEM((2 * N_CTX, PART, WINDOW), jnp.bfloat16),
            pltpu.VMEM((2 * Z, Y, ROWS, LATENT), jnp.float32),
            pltpu.VMEM((2 * Z, Y, ROWS, ROPE), jnp.float32),
        ],
        compiler_params=pltpu.CompilerParams(vmem_limit_bytes=48 * 1024 * 1024),
        cost_estimate=pl.CostEstimate(
            flops=8_000_000_000, bytes_accessed=10_000_000, transcendentals=1_600_000
        ),
        name="attention",
    )(spot, low_keys, *pieces, weight, query, grad_out)


def first_keys(lengths):
    starts = jnp.cumsum(lengths) - lengths
    base = lax.axis_index("ctx") * TOK_CTX
    positions = base + jnp.arange(TOK_CTX, dtype=jnp.int32)
    reached = jnp.where(starts[:, None] <= positions[None, :], starts[:, None], 0)
    return jnp.max(reached, axis=0, keepdims=True) - (base - DOC_MAX)


def on_device(query, kv_latent, kv_weight, grad_out, doc_lengths):
    along_z = [[z * Y + y for z in range(Z)] for y in range(Y)]
    rows = jnp.stack([passed_along(kv_latent[0], 1), kv_latent[0]])
    rows = lax.all_gather(rows, "head", axis_index_groups=along_z)
    pieces = [rows] + [turned(rows, "head", by) for by in range(1, Y)]
    spot = jnp.stack(
        [lax.axis_index("dp"), lax.axis_index("ctx"), lax.axis_index("head") % Y]
    ).astype(jnp.int32)
    d_query, kept, given, *terms = attention(
        spot, first_keys(doc_lengths[0]), pieces, kv_weight, query[0], grad_out[0]
    )
    term = terms[0]
    for by in range(1, Y):
        term = term + turned(terms[by], "head", by).astype(jnp.float32)
    shares = lax.all_to_all(
        term.astype(jnp.bfloat16), "head", 0, 0, axis_index_groups=along_z
    )
    share = jnp.sum(shares.astype(jnp.float32), axis=0)
    d_latent = share[1] + passed_along(share[0].astype(jnp.bfloat16), -1).astype(jnp.float32)
    d_kv_weight = summed_weight(kept, given)
    return (d_query[None], d_latent.astype(jnp.bfloat16)[None], d_kv_weight)


def solution(mesh):
    return jax.shard_map(
        on_device,
        mesh=mesh,
        in_specs=(
            P("dp", "ctx", "head"),
            P("dp", ("ctx", "head"), None),
            P(None, "head"),
            P("dp", "ctx", "head"),
            P("dp", None),
        ),
        out_specs=(P("dp", "ctx", "head"), P("dp", ("ctx", "head"), None), P(None, "head")),
        check_vma=False,
    )
```

time: 125 us -> 116 us (0.928)
  blocking collectives: 0 us -> 22.7 us
  waiting for transfers between devices: 50.3 us -> 31.1 us
  starting transfers between devices: 41.5 us -> 36 us
  local copies, waits for them, and re-layouts: 7.88 us -> 2.91 us
  other arithmetic: 6.99 us -> 3.55 us
  Pallas kernels: 14.8 us -> 16.7 us
    all_to_all x2 -> x1, waiting for transfers between devices: 24 us -> 0.01 us  [on_device(): lax.all_to_all(term.astype(jnp.bfloat16), 'head', 0, 0, axis_index_groups...]
    all_gather x0 -> x1, blocking collectives: none -> 22.7 us  [on_device(): rows = lax.all_gather(rows, 'head', axis_index_groups=along_z)]
    all_to_all x2 -> x1, starting transfers between devices: 17.7 us -> 4.54 us  [on_device(): lax.all_to_all(term.astype(jnp.bfloat16), 'head', 0, 0, axis_index_groups...]
    ppermute x10 -> x16, starting transfers between devices: 23.9 us -> 31.4 us  [the longest x6 8.89 us: turned(): lax.ppermute(array, axis, [(i, (i + by) % N_CTX) for i in range(N_CTX)])]
    convert_element_type x4 -> x3, other arithmetic: 5.99 us -> 1.09 us  [the longest x1 0.87 us: on_device(): term.astype(jnp.bfloat16)]
    ppermute x10 -> x16, waiting for transfers between devices: 26.3 us -> 31.1 us  [the longest x6 21.3 us: turned(): return lax.ppermute(array, axis, pairs)]
    pallas_call x1 -> x2, Pallas kernels: 14.8 us -> 16.7 us  [the longest x1 15.3 us: attention(): pl.pallas_call(attention_kernel, grid=(HEADS_DEV // 2,), in_specs=[pl.Blo...]
    ppermute x2 -> x0, local copies, waits for them, and re-layouts: 1.65 us -> none  [passed_along(): return lax.ppermute(array, axis, pairs)]
  transfers between devices with their start and end apart: 12 -> 17, of which waited for: 7 -> 7; matrix products, arithmetic and copies ran while one was open for 7% -> 3% of each run, Pallas kernels for 0% -> 0%
where the time goes in v3:
time: 116 us; the launch traced here: 114 us
  starting transfers between devices  36 us (31%)
  waiting for transfers between devices  31.1 us (27%)
  blocking collectives  22.7 us (20%)
  Pallas kernels  16.7 us (14%)
  other arithmetic  3.55 us (3%)
  local copies, waits for them, and re-layouts  2.91 us (3%)
    all_gather x1, blocking collectives, on_device(): rows = lax.all_gather(rows, 'head', axis_index_groups=along_z)  22.7 us
    ppermute x6, waiting for transfers between devices, turned(): return lax.ppermute(array, axis, pairs)  21.3 us
    pallas_call x1, Pallas kernels, attention(): pl.pallas_call(attention_kernel, grid=(HEADS_DEV // 2,), in_specs=[pl.Blo...  15.3 us
    ppermute x6, starting transfers between devices, turned(): lax.ppermute(array, axis, [(i, (i + by) % N_CTX) for i in range(N_CTX)])  8.89 us
    ppermute x1, starting transfers between devices, summed_weight(): other = lax.ppermute(given, 'dp', swap)  8.34 us
    ppermute x6, waiting for transfers between devices, turned(): lax.ppermute(array, axis, [(i, (i + by) % N_CTX) for i in range(N_CTX)])  6.55 us
    ppermute x6, starting transfers between devices, turned(): return lax.ppermute(array, axis, pairs)  6.45 us
    ppermute x2, starting transfers between devices, passed_along(): return lax.ppermute(array, 'ctx', pairs)  5.24 us
  transfers between devices with their start and end apart: 17, of which 7 were waited for; matrix products, arithmetic and copies ran while one was open for 3% of the time, Pallas kernels for 0%

profile of v3, /device:TPU:1, one launch (start us, length us, event | category | flops | bytes accessed | tf_op | source)
XLA Modules:
  0.0 113.7 jit_solution(17084285742313664115)
XLA Ops:
  0.6 3.9 %collective-permute-start = (bf16[16,576]{1,0:T(8,128)(2,1)}, bf16[16,576]{1,0:T(8,128)(2,1)S(1)}, u32[]{:S(2)}, u32[]{:S(2)}) collective-permute-start(bf16[16,576]{1,0:T(8,128)(2,1)} %bitcast.42), channel_id=1, source_target_pairs={{0,32},{32,64},{64,96},{1,33},{33,65},{65,97},{2,34},{34,66},{66,9... | collective-permute-start | bytes 55304 | tf_op jit(solution)/shard_map/ppermute | solution.py:30
  7.0 22.7 %all-gather = bf16[16,16,576]{2,1,0:T(8,128)(2,1)S(1)} all-gather(bf16[2,16,576]{2,1,0:T(8,128)(2,1)S(1)} %pad_maximum_fusion.1), channel_id=2, replica_groups={{0,4,8,12,16,20,24,28},{1,5,9,13,17,21,25,29},{2,6,10,14,18,22,26,30},{..., dimensions={0}, use_global_device_ids=true | all-gather | bytes 331776 | tf_op jit(solution)/shard_map/all_gather | solution.py:268
  29.7 2.7 %collective-permute-start.3 = (bf16[8,2,16,576]{3,2,1,0:T(8,128)(2,1)S(1)}, bf16[8,2,16,576]{3,2,1,0:T(8,128)(2,1)S(1)}, u32[]{:S(2)}, u32[]{:S(2)}) collective-permute-start(bf16[8,2,16,576]{3,2,1,0:T(8,128)(2,1)S(1)} %bitcast.30), channel_id=1, source_target_pairs={{0,3},{1,0},{2,1},{3,2},{4,7},{5,4},{6,5},{7,6},{8,11},{9,8},{10,9... | collective-permute-start | bytes 884744 | tf_op jit(solution)/shard_map/ppermute | solution.py:37
  33.6 6.4 %collective-permute-done.3.piece3_ref = bf16[8,2,16,576]{3,2,1,0:T(8,128)(2,1)S(1)} collective-permute-done((bf16[8,2,16,576]{3,2,1,0:T(8,128)(2,1)S(1)}, bf16[8,2,16,576]{3,2,1,0:T(8,128)(2,1)S(1)}, u32[]{:S(2)}, u32[]{:S(2)}) %collective-permute-start.3) | collective-permute-done | bytes 294944 | tf_op jit(solution)/shard_map/ppermute | solution.py:37
  40.0 3.4 %collective-permute-done.1.piece1_ref = bf16[8,2,16,576]{3,2,1,0:T(8,128)(2,1)S(1)} collective-permute-done((bf16[8,2,16,576]{3,2,1,0:T(8,128)(2,1)S(1)}, bf16[8,2,16,576]{3,2,1,0:T(8,128)(2,1)S(1)}, u32[]{:S(2)}, u32[]{:S(2)}) %collective-permute-start.1) | collective-permute-done | bytes 294944 | tf_op jit(solution)/shard_map/ppermute | solution.py:37
  43.4 1.1 copy-done
  44.6 1.0 copy-done.1
  45.6 15.3 %attention.1 = (bf16[512,768]{1,0:T(8,128)(2,1)}, bf16[256,1024]{1,0:T(8,128)(2,1)S(1)}, bf16[256,1024]{1,0:T(8,128)(2,1)S(1)}, f32[8,2,16,576]{3,2,1,0:T(8,128)...) custom-call(s32[3]{0:T(128)S(1)} %pad_add_fusion.spot_ref, ...), custom_call_target="tpu_custom_call" | custom-call | flops 8000000000 | bytes 10000000 | tf_op jit(solution)/shard_map/attention/pallas_call | solution.py:217
  60.9 8.3 %collective-permute-start.8 = (bf16[256,1024]{1,0:T(8,128)(2,1)S(1)}, bf16[256,1024]{1,0:T(8,128)(2,1)S(1)}, u32[]{:S(2)}, u32[]{:S(2)}) collective-permute-start(bf16[256,1024]{1,0:T(8,128)(2,1)S(1)} %get-tuple-element.16), channel_id=1, source_target_pairs={{0,128},{128,0},{1,129},{129,1},{2,130},{130,2},{3,131},{131,3},{4... | collective-permute-start | bytes 1572872 | tf_op jit(solution)/shard_map/ppermute | solution.py:43
  69.2 1.5 %collective-permute-start.5 = (bf16[8,2,16,576]{3,2,1,0:T(8,128)(2,1)S(1)}, bf16[8,2,16,576]{3,2,1,0:T(8,128)(2,1)S(1)}, u32[]{:S(2)}, u32[]{:S(2)}) collective-permute-start(bf16[8,2,16,576]{3,2,1,0:T(8,128)(2,1)S(1)} %get-tuple-element.13), channel_id=1, source_target_pairs={{0,2},{1,3},{2,0},{3,1},{4,6},{5,7},{6,4},{7,5},{8,10},{9,11},{10,... | collective-permute-start | bytes 884744 | tf_op jit(solution)/shard_map/ppermute | solution.py:37
  70.7 1.2 %collective-permute-start.6 = (bf16[8,2,16,576]{3,2,1,0:T(8,128)(2,1)S(1)}, bf16[8,2,16,576]{3,2,1,0:T(8,128)(2,1)S(1)}, u32[]{:S(2)}, u32[]{:S(2)}) collective-permute-start(bf16[8,2,16,576]{3,2,1,0:T(8,128)(2,1)S(1)} %get-tuple-element.14), channel_id=1, source_target_pairs={{0,3},{1,0},{2,1},{3,2},{4,7},{5,4},{6,5},{7,6},{8,11},{9,8},{10,9... | collective-permute-start | bytes 884744 | tf_op jit(solution)/shard_map/ppermute | solution.py:37
  72.0 2.0 %collective-permute-start.9 = (bf16[64,1024]{1,0:T(8,128)(2,1)S(1)}, bf16[64,1024]{1,0:T(8,128)(2,1)S(1)}, u32[]{:S(2)}, u32[]{:S(2)}) collective-permute-start(bf16[64,1024]{1,0:T(8,128)(2,1)S(1)} %get-tuple-element.17), channel_id=1, source_target_pairs={{0,32},{32,64},{64,96},{96,0},{1,33},{33,65},{65,97},{97,1},{2,34}... | collective-permute-start | bytes 393224 | tf_op jit(solution)/shard_map/ppermute | solution.py:35
  74.1 1.3 %collective-permute-start.11 = (bf16[64,1024]{1,0:T(8,128)(2,1)S(1)}, bf16[64,1024]{1,0:T(8,128)(2,1)S(1)}, u32[]{:S(2)}, u32[]{:S(2)}) collective-permute-start(bf16[64,1024]{1,0:T(8,128)(2,1)S(1)} %get-tuple-element.18), channel_id=1, source_target_pairs={{0,96},{32,0},{64,32},{96,64},{1,97},{33,1},{65,33},{97,65},{2,98}... | collective-permute-start | bytes 393224 | tf_op jit(solution)/shard_map/ppermute | solution.py:35
  75.3 11.4 %collective-permute-done.4 = bf16[8,2,16,576]{3,2,1,0:T(8,128)(2,1)S(1)} collective-permute-done((bf16[8,2,16,576]{3,2,1,0:T(8,128)(2,1)S(1)}, bf16[8,2,16,576]{3,2,1,0:T(8,128)(2,1)S(1)}, u32[]{:S(2)}, u32[]{:S(2)}) %collective-permute-start.4) | collective-permute-done | bytes 294944 | tf_op jit(solution)/shard_map/ppermute | solution.py:37
  86.8 3.4 %collective-permute-start.10 = (bf16[64,1024]{1,0:T(8,128)(2,1)S(1)}, bf16[64,1024]{1,0:T(8,128)(2,1)S(1)}, u32[]{:S(2)}, u32[]{:S(2)}) collective-permute-start(bf16[64,1024]{1,0:T(8,128)(2,1)S(1)} %get-tuple-element.19), channel_id=1, source_target_pairs={{0,64},{32,96},{64,0},{96,32},{1,65},{33,97},{65,1},{97,33},{2,66}... | collective-permute-start | bytes 393224 | tf_op jit(solution)/shard_map/ppermute | solution.py:35
  91.1 4.5 %all-to-all-start = ((bf16[8,2,16,576]{3,2,1,0:T(8,128)(2,1)}), bf16[8,2,16,576]{3,2,1,0:T(8,128)(2,1)S(1)}, u32[]{:S(2)}, u32[]{:S(2)}) async-start(bf16[8,2,16,576]{3,2,1,0:T(8,128)(2,1)} %add_convert_fusion), calls=%async_computation | async-start | bytes 655360 | tf_op jit(solution)/shard_map/all_to_all | solution.py:279
  96.7 1.2 %collective-permute-start.13 = (bf16[64,1024]{1,0:T(8,128)(2,1)S(1)}, bf16[64,1024]{1,0:T(8,128)(2,1)S(1)}, u32[]{:S(2)}, u32[]{:S(2)}) collective-permute-start(bf16[64,1024]{1,0:T(8,128)(2,1)S(1)} %add_convert_fusion.1), channel_id=1, source_target_pairs={{0,64},{32,96},{64,0},{96,32},{1,65},{33,97},{65,1},{97,33},{2,66}... | collective-permute-start | bytes 393224 | tf_op jit(solution)/shard_map/ppermute | solution.py:35
  97.9 1.7 %collective-permute-done.14 = bf16[64,1024]{1,0:T(8,128)(2,1)S(1)} collective-permute-done((bf16[64,1024]{1,0:T(8,128)(2,1)S(1)}, bf16[64,1024]{1,0:T(8,128)(2,1)S(1)}, u32[]{:S(2)}, u32[]{:S(2)}) %collective-permute-start.14) | collective-permute-done | bytes 131104 | tf_op jit(solution)/shard_map/ppermute | solution.py:35
  99.6 2.4 %collective-permute-done.13 = bf16[64,1024]{1,0:T(8,128)(2,1)S(1)} collective-permute-done((bf16[64,1024]{1,0:T(8,128)(2,1)S(1)}, bf16[64,1024]{1,0:T(8,128)(2,1)S(1)}, u32[]{:S(2)}, u32[]{:S(2)}) %collective-permute-start.13) | collective-permute-done | bytes 131104 | tf_op jit(solution)/shard_map/ppermute | solution.py:35
  102.1 2.4 %collective-permute-done.12 = bf16[64,1024]{1,0:T(8,128)(2,1)S(1)} collective-permute-done((bf16[64,1024]{1,0:T(8,128)(2,1)S(1)}, bf16[64,1024]{1,0:T(8,128)(2,1)S(1)}, u32[]{:S(2)}, u32[]{:S(2)}) %collective-permute-start.12) | collective-permute-done | bytes 131104 | tf_op jit(solution)/shard_map/ppermute | solution.py:35
  104.5 2.5 %collective-permute-start.15 = (bf16[4,64,1024]{2,1,0:T(8,128)(2,1)S(1)}, bf16[4,64,1024]{2,1,0:T(8,128)(2,1)S(1)}, u32[]{:S(2)}, u32[]{:S(2)}) collective-permute-start(bf16[4,64,1024]{2,1,0:T(8,128)(2,1)S(1)} %pad_maximum_fusion.mine_ref), channel_id=1, source_target_pairs={{0,128},{128,0},{1,129},{129,1},{2,130},{130,2},{3,131},{131,3},{4... | collective-permute-start | bytes 1572872 | tf_op jit(solution)/shard_map/ppermute | solution.py:55
  107.1 1.3 %collective-permute-start.7 = (bf16[16,576]{1,0:T(8,128)(2,1)S(1)}, bf16[16,576]{1,0:T(8,128)(2,1)S(1)}, u32[]{:S(2)}, u32[]{:S(2)}) collective-permute-start(bf16[16,576]{1,0:T(8,128)(2,1)S(1)} %fusion.3), channel_id=1, source_target_pairs={{32,0},{64,32},{96,64},{33,1},{65,33},{97,65},{34,2},{66,34},{98,6... | collective-permute-start | bytes 55304 | tf_op jit(solution)/shard_map/ppermute | solution.py:30
  108.4 3.2 %collective-permute-done.7 = bf16[16,576]{1,0:T(8,128)(2,1)S(1)} collective-permute-done((bf16[16,576]{1,0:T(8,128)(2,1)S(1)}, bf16[16,576]{1,0:T(8,128)(2,1)S(1)}, u32[]{:S(2)}, u32[]{:S(2)}) %collective-permute-start.7) | collective-permute-done | bytes 18464 | tf_op jit(solution)/shard_map/ppermute | solution.py:30
  112.3 1.5 %placed.1 = f32[8,64,1024]{2,1,0:T(8,128)} custom-call(s32[1]{0:T(128)} %bitcast.core_ref, s32[1]{0:T(128)} %bitcast.1.place_ref, bf16[4,64,1024]{2,1,0:T(8,128)(2,1)S(1)} %pad_maximum_fusion.mine_ref, bf16[4,64,1024]{2,1,0:T(8,128)(2,1)S(1)} %collective-permute-done.15.other_ref), custom_call_target="tpu_custom_call" | custom-call | tf_op jit(solution)/shard_map/placed/pallas_call | solution.py:73
  (33 shorter events, 6.3 us)
Async XLA Ops:
  0.6 5.6 %collective-permute-start = (bf16[16,576]{1,0:T(8,128)(2,1)}, bf16[16,576]{1,0:T(8,128)(2,1)S(1)}, u32[]{:S(2)}, u32[]{:S(2)}) collective-permute-start(bf16[16,576]{1,0:T(8,128)(2,1)} %bitcast.42), channel_id=1, source_target_pairs={{0,32},{32,64},{64,96},{1,33},{33,65},{65,97},{2,34},{34,66},{66,9... | collective-permute-start | bytes 55304 | tf_op jit(solution)/shard_map/ppermute | solution.py:30
  29.7 10.3 %collective-permute-start.3 = (bf16[8,2,16,576]{3,2,1,0:T(8,128)(2,1)S(1)}, bf16[8,2,16,576]{3,2,1,0:T(8,128)(2,1)S(1)}, u32[]{:S(2)}, u32[]{:S(2)}) collective-permute-start(bf16[8,2,16,576]{3,2,1,0:T(8,128)(2,1)S(1)} %bitcast.30), channel_id=1, source_target_pairs={{0,3},{1,0},{2,1},{3,2},{4,7},{5,4},{6,5},{7,6},{8,11},{9,8},{10,9... | collective-permute-start | bytes 884744 | tf_op jit(solution)/shard_map/ppermute | solution.py:37
  32.5 7.5 %collective-permute-start.2 = (bf16[8,2,16,576]{3,2,1,0:T(8,128)(2,1)S(1)}, bf16[8,2,16,576]{3,2,1,0:T(8,128)(2,1)S(1)}, u32[]{:S(2)}, u32[]{:S(2)}) collective-permute-start(bf16[8,2,16,576]{3,2,1,0:T(8,128)(2,1)S(1)} %bitcast.31), channel_id=1, source_target_pairs={{0,2},{1,3},{2,0},{3,1},{4,6},{5,7},{6,4},{7,5},{8,10},{9,11},{10,... | collective-permute-start | bytes 884744 | tf_op jit(solution)/shard_map/ppermute | solution.py:37
  32.8 10.6 %collective-permute-start.1 = (bf16[8,2,16,576]{3,2,1,0:T(8,128)(2,1)S(1)}, bf16[8,2,16,576]{3,2,1,0:T(8,128)(2,1)S(1)}, u32[]{:S(2)}, u32[]{:S(2)}) collective-permute-start(bf16[8,2,16,576]{3,2,1,0:T(8,128)(2,1)S(1)} %bitcast.32), channel_id=1, source_target_pairs={{0,1},{1,2},{2,3},{3,0},{4,5},{5,6},{6,7},{7,4},{8,9},{9,10},{10,1... | collective-permute-start | bytes 884744 | tf_op jit(solution)/shard_map/ppermute | solution.py:37
  43.4 1.1 copy-start
  44.6 1.0 copy-start.1
  60.9 11.0 %collective-permute-start.8 = (bf16[256,1024]{1,0:T(8,128)(2,1)S(1)}, bf16[256,1024]{1,0:T(8,128)(2,1)S(1)}, u32[]{:S(2)}, u32[]{:S(2)}) collective-permute-start(bf16[256,1024]{1,0:T(8,128)(2,1)S(1)} %get-tuple-element.16), channel_id=1, source_target_pairs={{0,128},{128,0},{1,129},{129,1},{2,130},{130,2},{3,131},{131,3},{4... | collective-permute-start | bytes 1572872 | tf_op jit(solution)/shard_map/ppermute | solution.py:43
  69.2 17.6 %collective-permute-start.4 = (bf16[8,2,16,576]{3,2,1,0:T(8,128)(2,1)S(1)}, bf16[8,2,16,576]{3,2,1,0:T(8,128)(2,1)S(1)}, u32[]{:S(2)}, u32[]{:S(2)}) collective-permute-start(bf16[8,2,16,576]{3,2,1,0:T(8,128)(2,1)S(1)} %get-tuple-element.12), channel_id=1, source_target_pairs={{0,1},{1,2},{2,3},{3,0},{4,5},{5,6},{6,7},{7,4},{8,9},{9,10},{10,1... | collective-permute-start | bytes 884744 | tf_op jit(solution)/shard_map/ppermute | solution.py:37
  69.2 21.0 %collective-permute-start.5 = (bf16[8,2,16,576]{3,2,1,0:T(8,128)(2,1)S(1)}, bf16[8,2,16,576]{3,2,1,0:T(8,128)(2,1)S(1)}, u32[]{:S(2)}, u32[]{:S(2)}) collective-permute-start(bf16[8,2,16,576]{3,2,1,0:T(8,128)(2,1)S(1)} %get-tuple-element.13), channel_id=1, source_target_pairs={{0,2},{1,3},{2,0},{3,1},{4,6},{5,7},{6,4},{7,5},{8,10},{9,11},{10,... | collective-permute-start | bytes 884744 | tf_op jit(solution)/shard_map/ppermute | solution.py:37
  70.7 19.5 %collective-permute-start.6 = (bf16[8,2,16,576]{3,2,1,0:T(8,128)(2,1)S(1)}, bf16[8,2,16,576]{3,2,1,0:T(8,128)(2,1)S(1)}, u32[]{:S(2)}, u32[]{:S(2)}) collective-permute-start(bf16[8,2,16,576]{3,2,1,0:T(8,128)(2,1)S(1)} %get-tuple-element.14), channel_id=1, source_target_pairs={{0,3},{1,0},{2,1},{3,2},{4,7},{5,4},{6,5},{7,6},{8,11},{9,8},{10,9... | collective-permute-start | bytes 884744 | tf_op jit(solution)/shard_map/ppermute | solution.py:37
  72.0 23.6 %collective-permute-start.9 = (bf16[64,1024]{1,0:T(8,128)(2,1)S(1)}, bf16[64,1024]{1,0:T(8,128)(2,1)S(1)}, u32[]{:S(2)}, u32[]{:S(2)}) collective-permute-start(bf16[64,1024]{1,0:T(8,128)(2,1)S(1)} %get-tuple-element.17), channel_id=1, source_target_pairs={{0,32},{32,64},{64,96},{96,0},{1,33},{33,65},{65,97},{97,1},{2,34}... | collective-permute-start | bytes 393224 | tf_op jit(solution)/shard_map/ppermute | solution.py:35
  74.1 21.6 %collective-permute-start.11 = (bf16[64,1024]{1,0:T(8,128)(2,1)S(1)}, bf16[64,1024]{1,0:T(8,128)(2,1)S(1)}, u32[]{:S(2)}, u32[]{:S(2)}) collective-permute-start(bf16[64,1024]{1,0:T(8,128)(2,1)S(1)} %get-tuple-element.18), channel_id=1, source_target_pairs={{0,96},{32,0},{64,32},{96,64},{1,97},{33,1},{65,33},{97,65},{2,98}... | collective-permute-start | bytes 393224 | tf_op jit(solution)/shard_map/ppermute | solution.py:35
  86.8 8.8 %collective-permute-start.10 = (bf16[64,1024]{1,0:T(8,128)(2,1)S(1)}, bf16[64,1024]{1,0:T(8,128)(2,1)S(1)}, u32[]{:S(2)}, u32[]{:S(2)}) collective-permute-start(bf16[64,1024]{1,0:T(8,128)(2,1)S(1)} %get-tuple-element.19), channel_id=1, source_target_pairs={{0,64},{32,96},{64,0},{96,32},{1,65},{33,97},{65,1},{97,33},{2,66}... | collective-permute-start | bytes 393224 | tf_op jit(solution)/shard_map/ppermute | solution.py:35
  91.1 16.0 %all-to-all-start = ((bf16[8,2,16,576]{3,2,1,0:T(8,128)(2,1)}), bf16[8,2,16,576]{3,2,1,0:T(8,128)(2,1)S(1)}, u32[]{:S(2)}, u32[]{:S(2)}) async-start(bf16[8,2,16,576]{3,2,1,0:T(8,128)(2,1)} %add_convert_fusion), calls=%async_computation | async-start | bytes 655360 | tf_op jit(solution)/shard_map/all_to_all | solution.py:279
  95.7 3.9 %collective-permute-start.14 = (bf16[64,1024]{1,0:T(8,128)(2,1)S(1)}, bf16[64,1024]{1,0:T(8,128)(2,1)S(1)}, u32[]{:S(2)}, u32[]{:S(2)}) collective-permute-start(bf16[64,1024]{1,0:T(8,128)(2,1)S(1)} %add_convert_fusion.1), channel_id=1, source_target_pairs={{0,96},{32,0},{64,32},{96,64},{1,97},{33,1},{65,33},{97,65},{2,98}... | collective-permute-start | bytes 393224 | tf_op jit(solution)/shard_map/ppermute | solution.py:35
  96.7 5.4 %collective-permute-start.13 = (bf16[64,1024]{1,0:T(8,128)(2,1)S(1)}, bf16[64,1024]{1,0:T(8,128)(2,1)S(1)}, u32[]{:S(2)}, u32[]{:S(2)}) collective-permute-start(bf16[64,1024]{1,0:T(8,128)(2,1)S(1)} %add_convert_fusion.1), channel_id=1, source_target_pairs={{0,64},{32,96},{64,0},{96,32},{1,65},{33,97},{65,1},{97,33},{2,66}... | collective-permute-start | bytes 393224 | tf_op jit(solution)/shard_map/ppermute | solution.py:35
  97.9 6.5 %collective-permute-start.12 = (bf16[64,1024]{1,0:T(8,128)(2,1)S(1)}, bf16[64,1024]{1,0:T(8,128)(2,1)S(1)}, u32[]{:S(2)}, u32[]{:S(2)}) collective-permute-start(bf16[64,1024]{1,0:T(8,128)(2,1)S(1)} %add_convert_fusion.1), channel_id=1, source_target_pairs={{0,32},{32,64},{64,96},{96,0},{1,33},{33,65},{65,97},{97,1},{2,34}... | collective-permute-start | bytes 393224 | tf_op jit(solution)/shard_map/ppermute | solution.py:35
  104.5 7.7 %collective-permute-start.15 = (bf16[4,64,1024]{2,1,0:T(8,128)(2,1)S(1)}, bf16[4,64,1024]{2,1,0:T(8,128)(2,1)S(1)}, u32[]{:S(2)}, u32[]{:S(2)}) collective-permute-start(bf16[4,64,1024]{2,1,0:T(8,128)(2,1)S(1)} %pad_maximum_fusion.mine_ref), channel_id=1, source_target_pairs={{0,128},{128,0},{1,129},{129,1},{2,130},{130,2},{3,131},{131,3},{4... | collective-permute-start | bytes 1572872 | tf_op jit(solution)/shard_map/ppermute | solution.py:55
  107.1 4.5 %collective-permute-start.7 = (bf16[16,576]{1,0:T(8,128)(2,1)S(1)}, bf16[16,576]{1,0:T(8,128)(2,1)S(1)}, u32[]{:S(2)}, u32[]{:S(2)}) collective-permute-start(bf16[16,576]{1,0:T(8,128)(2,1)S(1)} %fusion.3), channel_id=1, source_target_pairs={{32,0},{64,32},{96,64},{33,1},{65,33},{97,65},{34,2},{66,34},{98,6... | collective-permute-start | bytes 55304 | tf_op jit(solution)/shard_map/ppermute | solution.py:30

commit v4 on v3

--- a/solution.py
+++ b/solution.py
@@ -37,22 +37,50 @@
     return lax.ppermute(array, axis, pairs)
 
 
-def summed_weight(kept, given):
-    low = jnp.bfloat16
+def first_sum_kernel(kept_ref, other_ref, after_ref, mine_ref, *out_refs):
+    for by, out in enumerate([mine_ref, *out_refs]):
+        at = slice(by * PART, (by + 1) * PART)
+        total = kept_ref[at].astype(jnp.float32) + other_ref[at].astype(jnp.float32)
+        out[...] = total.astype(out.dtype)
+
+
+def second_sum_kernel(mine_ref, one_ref, two_ref, three_ref, after_ref, out_ref):
+    total = mine_ref[...]
+    for ref in (one_ref, two_ref, three_ref):
+        total = total + ref[...].astype(jnp.float32)
+    out_ref[...] = total.astype(out_ref.dtype)
+
+
+def stack_kernel(one_ref, two_ref, three_ref, four_ref, after_ref, out_ref):
+    for by, ref in enumerate((one_ref, two_ref, three_ref, four_ref)):
+        out_ref[by] = ref[...]
+
+
+def small_call(kernel, out_shape, name, *operands, after):
+    vmem = pl.BlockSpec(memory_space=pltpu.VMEM)
+    return pl.pallas_call(
+        kernel,
+        in_specs=[vmem] * len(operands) + [pl.BlockSpec(memory_space=pl.ANY)],
+        out_specs=jax.tree.map(lambda _: vmem, out_shape),
+        out_shape=out_shape,
+        compiler_params=pltpu.CompilerParams(vmem_limit_bytes=16 * 1024 * 1024),
+        name=name,
+    )(*operands, after)
+
+
+def summed_weight(kept, given, first_after, second_after):
     swap = [(0, 1), (1, 0)]
     other = lax.ppermute(given, "dp", swap)
-    mine = [
-        kept[by * PART : (by + 1) * PART].astype(jnp.float32)
-        + other[by * PART : (by + 1) * PART].astype(jnp.float32)
-        for by in range(N_CTX)
-    ]
-    total = mine[0]
-    for by in range(1, N_CTX):
-        total = total + turned(mine[by].astype(low), "ctx", by).astype(jnp.float32)
-    total = total.astype(low)
+    shape = (PART, given.shape[1])
+    full = jax.ShapeDtypeStruct(shape, jnp.float32)
+    low = jax.ShapeDtypeStruct(shape, jnp.bfloat16)
+    mine, *rest = small_call(
+        first_sum_kernel, [full, low, low, low], "first_sum", kept, other, after=first_after
+    )
+    rest = [turned(part, "ctx", by + 1) for by, part in enumerate(rest)]
+    total = small_call(second_sum_kernel, low, "second_sum", mine, *rest, after=second_after)
     pieces = [total] + [turned(total, "ctx", by) for by in range(1, N_CTX)]
-    pieces = jnp.stack(pieces)
-    return placed(pieces, lax.ppermute(pieces, "dp", swap))
+    return pieces
 
 
 def place_kernel(core_ref, place_ref, mine_ref, other_ref, out_ref):
@@ -90,40 +118,21 @@
     return lax.dot_general(left, right, dims, preferred_element_type=jnp.float32)
 
 
-def attention_kernel(
-    spot_ref,
-    low_ref,
-    piece0_ref,
-    piece1_ref,
-    piece2_ref,
-    piece3_ref,
-    weight_ref,
-    query_ref,
-    grad_ref,
-    d_query_ref,
-    kept_ref,
-    given_ref,
-    term0_ref,
-    term1_ref,
-    term2_ref,
-    term3_ref,
-    rows_ref,
-    bias_ref,
-    plain_ref,
-    turned_ref,
-    term_ref,
-    rope_ref,
-):
+def attention_kernel(spot_ref, low_ref, *refs):
+    own_pieces, prev_pieces, refs = refs[:Y], refs[Y : 2 * Y], refs[2 * Y :]
+    weight_ref, query_ref, grad_ref, d_query_ref, kept_ref, given_ref, *refs = refs
+    own_terms, prev_terms, refs = refs[:Y], refs[Y : 2 * Y], refs[2 * Y :]
+    rows_ref, bias_ref, plain_ref, turned_ref, term_ref, rope_ref = refs
     step = pl.program_id(0)
     low = jnp.bfloat16
     core, place, spot = spot_ref[0], spot_ref[1], spot_ref[2]
 
     @pl.when(step == 0)
     def _():
-        for by, piece in enumerate([piece0_ref, piece1_ref, piece2_ref, piece3_ref]):
+        for by in range(Y):
             at = lax.rem(spot - by + Y, Y)
-            rows_ref[:Z, at] = piece[:, 0]
-            rows_ref[Z:, at] = piece[:, 1]
+            rows_ref[:Z, at] = prev_pieces[by][...]
+            rows_ref[Z:, at] = own_pieces[by][...]
 
     rows = rows_ref[...].reshape(WINDOW, LATENT + ROPE)
     latent = rows[:, :LATENT]
@@ -198,29 +207,29 @@
 
     @pl.when(step == pl.num_programs(0) - 1)
     def _():
-        for by, out in enumerate([term0_ref, term1_ref, term2_ref, term3_ref]):
+        for by in range(Y):
             at = lax.rem(spot + by, Y)
-            term, rope = term_ref[:, at].astype(out.dtype), rope_ref[:, at].astype(out.dtype)
-            for half in range(2):
-                out[:, half, :, :LATENT] = term[half * Z : (half + 1) * Z]
-                out[:, half, :, LATENT:] = rope[half * Z : (half + 1) * Z]
-
-
-def attention(spot, low_keys, pieces, weight, query, grad_out):
+            for outs, first in ((prev_terms, 0), (own_terms, Z)):
+                out = outs[by]
+                out[:, :, :LATENT] = term_ref[first : first + Z, at].astype(out.dtype)
+                out[:, :, LATENT:] = rope_ref[first : first + Z, at].astype(out.dtype)
+
+
+def attention(spot, low_keys, own_pieces, prev_pieces, weight, query, grad_out):
     def whole(shape):
         return pl.BlockSpec(shape, lambda step: (0,) * len(shape))
 
     def columns(count, width):
         return pl.BlockSpec((count, width), lambda step: (0, step))
 
-    piece = (Z, 2, ROWS, LATENT + ROPE)
+    piece = (Z, ROWS, LATENT + ROPE)
     return pl.pallas_call(
         attention_kernel,
         grid=(HEADS_DEV // 2,),
         in_specs=[
             pl.BlockSpec(memory_space=pltpu.SMEM),
             whole((1, TOK_CTX)),
-            *[whole(piece)] * Y,
+            *[whole(piece)] * (2 * Y),
             columns(LATENT, 2 * KV_WIDTH),
             columns(TOK_CTX, 2 * (NOPE + ROPE)),
             columns(TOK_CTX, 2 * VDIM),
@@ -229,14 +238,13 @@
             columns(TOK_CTX, 2 * (NOPE + ROPE)),
             columns(LATENT // 2, 2 * KV_WIDTH),
             columns(LATENT // 2, 2 * KV_WIDTH),
-            *[whole(piece)] * Y,
+            *[whole(piece)] * (2 * Y),
         ],
         out_shape=[
             jax.ShapeDtypeStruct((TOK_CTX, HEADS_DEV * (NOPE + ROPE)), jnp.bfloat16),
             jax.ShapeDtypeStruct((LATENT // 2, HEADS_DEV * KV_WIDTH), jnp.bfloat16),
             jax.ShapeDtypeStruct((LATENT // 2, HEADS_DEV * KV_WIDTH), jnp.bfloat16),
-            jax.ShapeDtypeStruct(piece, jnp.float32),
-            *[jax.ShapeDtypeStruct(piece, jnp.bfloat16)] * (Y - 1),
+            *[jax.ShapeDtypeStruct(piece, jnp.float32 if by == 0 else jnp.bfloat16) for by in range(Y)] * 2,
         ],
         scratch_shapes=[
             pltpu.VMEM((2 * Z, Y, ROWS, LATENT + ROPE), jnp.bfloat16),
@@ -251,7 +259,7 @@
             flops=8_000_000_000, bytes_accessed=10_000_000, transcendentals=1_600_000
         ),
         name="attention",
-    )(spot, low_keys, *pieces, weight, query, grad_out)
+    )(spot, low_keys, *own_pieces, *prev_pieces, weight, query, grad_out)
 
 
 def first_keys(lengths):
@@ -262,27 +270,42 @@
     return jnp.max(reached, axis=0, keepdims=True) - (base - DOC_MAX)
 
 
+def summed_over_y(terms):
+    total = terms[0]
+    for by in range(1, Y):
+        total = total + turned(terms[by], "head", by).astype(jnp.float32)
+    return total
+
+
 def on_device(query, kv_latent, kv_weight, grad_out, doc_lengths):
     along_z = [[z * Y + y for z in range(Z)] for y in range(Y)]
-    rows = jnp.stack([passed_along(kv_latent[0], 1), kv_latent[0]])
-    rows = lax.all_gather(rows, "head", axis_index_groups=along_z)
-    pieces = [rows] + [turned(rows, "head", by) for by in range(1, Y)]
+    block = jnp.broadcast_to(kv_latent, (Z, ROWS, LATENT + ROPE))
+    block = lax.all_to_all(block, "head", 0, 0, axis_index_groups=along_z)
+    prev_block = passed_along(block, 1)
+    own_pieces = [block] + [turned(block, "head", by) for by in range(1, Y)]
+    prev_pieces = [prev_block] + [turned(prev_block, "head", by) for by in range(1, Y)]
     spot = jnp.stack(
         [lax.axis_index("dp"), lax.axis_index("ctx"), lax.axis_index("head") % Y]
     ).astype(jnp.int32)
     d_query, kept, given, *terms = attention(
-        spot, first_keys(doc_lengths[0]), pieces, kv_weight, query[0], grad_out[0]
+        spot,
+        first_keys(doc_lengths[0]),
+        own_pieces,
+        prev_pieces,
+        kv_weight,
+        query[0],
+        grad_out[0],
     )
-    term = terms[0]
-    for by in range(1, Y):
-        term = term + turned(terms[by], "head", by).astype(jnp.float32)
-    shares = lax.all_to_all(
-        term.astype(jnp.bfloat16), "head", 0, 0, axis_index_groups=along_z
-    )
-    share = jnp.sum(shares.astype(jnp.float32), axis=0)
-    d_latent = share[1] + passed_along(share[0].astype(jnp.bfloat16), -1).astype(jnp.float32)
-    d_kv_weight = summed_weight(kept, given)
-    return (d_query[None], d_latent.astype(jnp.bfloat16)[None], d_kv_weight)
+    prev_term = summed_over_y(terms[Y:]).astype(jnp.bfloat16)
+    term = summed_over_y(terms[:Y]) + passed_along(prev_term, -1).astype(jnp.float32)
+    term = term.astype(jnp.bfloat16)
+    parts = summed_weight(kept, given, prev_term, term)
+    shares = lax.all_to_all(term, "head", 0, 0, axis_index_groups=along_z)
+    d_latent = jnp.sum(shares.astype(jnp.float32), axis=0).astype(jnp.bfloat16)
+    stacked = jax.ShapeDtypeStruct((N_CTX, *parts[0].shape), jnp.bfloat16)
+    parts = small_call(stack_kernel, stacked, "stacked", *parts, after=d_latent)
+    d_kv_weight = placed(parts, lax.ppermute(parts, "dp", [(0, 1), (1, 0)]))
+    return (d_query[None], d_latent[None], d_kv_weight)
 
 
 def solution(mesh):

time: 116 us -> 100 us (0.86); the launches traced: 114 us -> 99.7 us
  blocking collectives: 22.7 us -> 0 us
  starting transfers between devices: 36 us -> 50.5 us
  waiting for transfers between devices: 31.1 us -> 25.2 us
  other arithmetic: 3.55 us -> 1.89 us
  local copies, waits for them, and re-layouts: 2.91 us -> 4.32 us
    all_gather x1 -> x0, blocking collectives: 22.7 us -> none  [on_device(): rows = lax.all_gather(rows, 'head', axis_index_groups=along_z)]
    all_to_all x1 -> x2, waiting for transfers between devices: 0.01 us -> 11.2 us  [the longest x1 6.6 us: on_device(): block = lax.all_to_all(block, 'head', 0, 0, axis_index_groups=along_z)]
    ppermute x6 -> x12, waiting for transfers between devices: 21.3 us -> 11.5 us  [turned(): return lax.ppermute(array, axis, pairs)]
    ppermute x6 -> x12, starting transfers between devices: 6.45 us -> 14.7 us  [turned(): return lax.ppermute(array, axis, pairs)]
    all_to_all x1 -> x2, starting transfers between devices: 4.54 us -> 12.4 us  [the longest x1 9.01 us: on_device(): block = lax.all_to_all(block, 'head', 0, 0, axis_index_groups=along_z)]
    ppermute x6, waiting for transfers between devices: 6.55 us -> 1.01 us  [turned(): lax.ppermute(array, axis, [(i, (i + by) % N_CTX) for i in range(N_CTX)])]
    ppermute x1, starting transfers between devices: 8.34 us -> 4.52 us  [summed_weight(): other = lax.ppermute(given, 'dp', swap)]
    ppermute x2, waiting for transfers between devices: 3.23 us -> 0.01 us  [passed_along(): return lax.ppermute(array, 'ctx', pairs)]
  transfers between devices with their start and end apart: 17 -> 24, of which waited for: 7 -> 11; matrix products, arithmetic and copies ran while one was open for 3% -> 3% of each run, Pallas kernels for 0% -> 0%
where the time goes in v4:
time: 100 us; the launch traced here: 99.7 us
  starting transfers between devices  50.5 us (50%)
  waiting for transfers between devices  25.2 us (25%)
  Pallas kernels  16.9 us (17%)
  local copies, waits for them, and re-layouts  4.32 us (4%)
  other arithmetic  1.89 us (2%)
    pallas_call x1, Pallas kernels, attention(): pl.pallas_call(attention_kernel, grid=(HEADS_DEV // 2,), in_specs=[pl.Blo...  15.3 us
    ppermute x12, starting transfers between devices, turned(): return lax.ppermute(array, axis, pairs)  14.7 us
    ppermute x12, waiting for transfers between devices, turned(): return lax.ppermute(array, axis, pairs)  11.5 us
    ppermute x6, starting transfers between devices, turned(): lax.ppermute(array, axis, [(i, (i + by) % N_CTX) for i in range(N_CTX)])  9.11 us
    all_to_all x1, starting transfers between devices, on_device(): block = lax.all_to_all(block, 'head', 0, 0, axis_index_groups=along_z)  9.01 us
    all_to_all x1, waiting for transfers between devices, on_device(): block = lax.all_to_all(block, 'head', 0, 0, axis_index_groups=along_z)  6.6 us
    ppermute x1, starting transfers between devices, on_device(): d_kv_weight = placed(parts, lax.ppermute(parts, 'dp', [(0, 1), (1, 0)]))  5.38 us
    all_to_all x1, waiting for transfers between devices, on_device(): shares = lax.all_to_all(term, 'head', 0, 0, axis_index_groups=along_z)  4.6 us
  transfers between devices with their start and end apart: 24, of which 11 were waited for; matrix products, arithmetic and copies ran while one was open for 3% of the time, Pallas kernels for 0%

profile of v4, /device:TPU:1, one launch (start us, length us, event | category | flops | bytes accessed | tf_op | source)
XLA Modules:
  0.0 99.7 jit_solution(17675458181533186495)
XLA Ops:
  0.6 1.4 %broadcast_in_dim.29 = bf16[8,16,576]{2,1,0:T(8,128)(2,1)} broadcast(bf16[16,576]{1,0:T(8,128)(2,1)} %bitcast.18), dimensions={1,2} | broadcast | bytes 165888 | tf_op jit(solution)/shard_map/broadcast_in_dim | solution.py:282
  2.0 9.0 %all-to-all-start = ((bf16[8,16,576]{2,1,0:T(8,128)(2,1)}), bf16[8,16,576]{2,1,0:T(8,128)(2,1)S(1)}, u32[]{:S(2)}, u32[]{:S(2)}) async-start(bf16[8,16,576]{2,1,0:T(8,128)(2,1)} %broadcast_in_dim.29), calls=%async_computation | async-start | bytes 327680 | tf_op jit(solution)/shard_map/all_to_all | solution.py:283
  12.6 6.6 %all-to-all-done.refs_0_ = bf16[8,16,576]{2,1,0:T(8,128)(2,1)S(1)} async-done(((bf16[8,16,576]{2,1,0:T(8,128)(2,1)}), bf16[8,16,576]{2,1,0:T(8,128)(2,1)S(1)}, u32[]{:S(2)}, u32[]{:S(2)}) %all-to-all-start) | async-done | bytes 147488 | tf_op jit(solution)/shard_map/all_to_all | solution.py:283
  19.2 3.1 %collective-permute-start.3 = (bf16[8,16,576]{2,1,0:T(8,128)(2,1)S(1)}, bf16[8,16,576]{2,1,0:T(8,128)(2,1)S(1)}, u32[]{:S(2)}, u32[]{:S(2)}) collective-permute-start(bf16[8,16,576]{2,1,0:T(8,128)(2,1)S(1)} %all-to-all-done.refs_0_), channel_id=1, source_target_pairs={{0,32},{32,64},{64,96},{1,33},{33,65},{65,97},{2,34},{34,66},{66,9... | collective-permute-start | bytes 442376 | tf_op jit(solution)/shard_map/ppermute | solution.py:30
  22.3 2.8 %collective-permute-start.2 = (bf16[8,16,576]{2,1,0:T(8,128)(2,1)S(1)}, bf16[8,16,576]{2,1,0:T(8,128)(2,1)S(1)}, u32[]{:S(2)}, u32[]{:S(2)}) collective-permute-start(bf16[8,16,576]{2,1,0:T(8,128)(2,1)S(1)} %all-to-all-done.refs_0_), channel_id=1, source_target_pairs={{0,3},{1,0},{2,1},{3,2},{4,7},{5,4},{6,5},{7,6},{8,11},{9,8},{10,9... | collective-permute-start | bytes 442376 | tf_op jit(solution)/shard_map/ppermute | solution.py:37
  26.4 2.0 %collective-permute-start.6 = (bf16[8,16,576]{2,1,0:T(8,128)(2,1)S(1)}, bf16[8,16,576]{2,1,0:T(8,128)(2,1)S(1)}, u32[]{:S(2)}, u32[]{:S(2)}) collective-permute-start(bf16[8,16,576]{2,1,0:T(8,128)(2,1)S(1)} %collective-permute-done.3.refs_4_), channel_id=1, source_target_pairs={{0,3},{1,0},{2,1},{3,2},{4,7},{5,4},{6,5},{7,6},{8,11},{9,8},{10,9... | collective-permute-start | bytes 442376 | tf_op jit(solution)/shard_map/ppermute | solution.py:37
  28.3 1.4 %collective-permute-start.5 = (bf16[8,16,576]{2,1,0:T(8,128)(2,1)S(1)}, bf16[8,16,576]{2,1,0:T(8,128)(2,1)S(1)}, u32[]{:S(2)}, u32[]{:S(2)}) collective-permute-start(bf16[8,16,576]{2,1,0:T(8,128)(2,1)S(1)} %collective-permute-done.3.refs_4_), channel_id=1, source_target_pairs={{0,2},{1,3},{2,0},{3,1},{4,6},{5,7},{6,4},{7,5},{8,10},{9,11},{10,... | collective-permute-start | bytes 442376 | tf_op jit(solution)/shard_map/ppermute | solution.py:37
  31.1 1.7 %collective-permute-done.refs_1_ = bf16[8,16,576]{2,1,0:T(8,128)(2,1)S(1)} collective-permute-done((bf16[8,16,576]{2,1,0:T(8,128)(2,1)S(1)}, bf16[8,16,576]{2,1,0:T(8,128)(2,1)S(1)}, u32[]{:S(2)}, u32[]{:S(2)}) %collective-permute-start) | collective-permute-done | bytes 147488 | tf_op jit(solution)/shard_map/ppermute | solution.py:37
  32.7 2.7 %collective-permute-done.6.refs_7_ = bf16[8,16,576]{2,1,0:T(8,128)(2,1)S(1)} collective-permute-done((bf16[8,16,576]{2,1,0:T(8,128)(2,1)S(1)}, bf16[8,16,576]{2,1,0:T(8,128)(2,1)S(1)}, u32[]{:S(2)}, u32[]{:S(2)}) %collective-permute-start.6) | collective-permute-done | bytes 147488 | tf_op jit(solution)/shard_map/ppermute | solution.py:37
  36.5 3.6 %collective-permute-done.4.refs_5_ = bf16[8,16,576]{2,1,0:T(8,128)(2,1)S(1)} collective-permute-done((bf16[8,16,576]{2,1,0:T(8,128)(2,1)S(1)}, bf16[8,16,576]{2,1,0:T(8,128)(2,1)S(1)}, u32[]{:S(2)}, u32[]{:S(2)}) %collective-permute-start.4) | collective-permute-done | bytes 147488 | tf_op jit(solution)/shard_map/ppermute | solution.py:37
  42.2 15.3 %attention.1 = (bf16[512,768]{1,0:T(8,128)(2,1)}, bf16[256,1024]{1,0:T(8,128)(2,1)S(1)}, bf16[256,1024]{1,0:T(8,128)(2,1)S(1)}, f32[8,16,576]{2,1,0:T(8,128)S(1)...) custom-call(s32[3]{0:T(128)S(1)} %pad_add_fusion.spot_ref, ...), custom_call_target="tpu_custom_call" | custom-call | flops 8000000000 | bytes 10000000 | tf_op jit(solution)/shard_map/attention/pallas_call | solution.py:226
  57.5 1.4 %collective-permute-start.11 = (bf16[8,16,576]{2,1,0:T(8,128)(2,1)S(1)}, bf16[8,16,576]{2,1,0:T(8,128)(2,1)S(1)}, u32[]{:S(2)}, u32[]{:S(2)}) collective-permute-start(bf16[8,16,576]{2,1,0:T(8,128)(2,1)S(1)} %get-tuple-element.25), channel_id=1, source_target_pairs={{0,2},{1,3},{2,0},{3,1},{4,6},{5,7},{6,4},{7,5},{8,10},{9,11},{10,... | collective-permute-start | bytes 442376 | tf_op jit(solution)/shard_map/ppermute | solution.py:37
  58.9 1.3 %collective-permute-start.12 = (bf16[8,16,576]{2,1,0:T(8,128)(2,1)S(1)}, bf16[8,16,576]{2,1,0:T(8,128)(2,1)S(1)}, u32[]{:S(2)}, u32[]{:S(2)}) collective-permute-start(bf16[8,16,576]{2,1,0:T(8,128)(2,1)S(1)} %get-tuple-element.26), channel_id=1, source_target_pairs={{0,3},{1,0},{2,1},{3,2},{4,7},{5,4},{6,5},{7,6},{8,11},{9,8},{10,9... | collective-permute-start | bytes 442376 | tf_op jit(solution)/shard_map/ppermute | solution.py:37
  60.2 4.5 %collective-permute-start.14 = (bf16[256,1024]{1,0:T(8,128)(2,1)S(1)}, bf16[256,1024]{1,0:T(8,128)(2,1)S(1)}, u32[]{:S(2)}, u32[]{:S(2)}) collective-permute-start(bf16[256,1024]{1,0:T(8,128)(2,1)S(1)} %get-tuple-element.28), channel_id=1, source_target_pairs={{0,128},{128,0},{1,129},{129,1},{2,130},{130,2},{3,131},{131,3},{4... | collective-permute-start | bytes 1572872 | tf_op jit(solution)/shard_map/ppermute | solution.py:73
  66.1 1.3 %collective-permute-start.8 = (bf16[8,16,576]{2,1,0:T(8,128)(2,1)S(1)}, bf16[8,16,576]{2,1,0:T(8,128)(2,1)S(1)}, u32[]{:S(2)}, u32[]{:S(2)}) collective-permute-start(bf16[8,16,576]{2,1,0:T(8,128)(2,1)S(1)} %get-tuple-element.21), channel_id=1, source_target_pairs={{0,2},{1,3},{2,0},{3,1},{4,6},{5,7},{6,4},{7,5},{8,10},{9,11},{10,... | collective-permute-start | bytes 442376 | tf_op jit(solution)/shard_map/ppermute | solution.py:37
  67.4 2.1 %collective-permute-start.9 = (bf16[8,16,576]{2,1,0:T(8,128)(2,1)S(1)}, bf16[8,16,576]{2,1,0:T(8,128)(2,1)S(1)}, u32[]{:S(2)}, u32[]{:S(2)}) collective-permute-start(bf16[8,16,576]{2,1,0:T(8,128)(2,1)S(1)} %get-tuple-element.22), channel_id=1, source_target_pairs={{0,3},{1,0},{2,1},{3,2},{4,7},{5,4},{6,5},{7,6},{8,11},{9,8},{10,9... | collective-permute-start | bytes 442376 | tf_op jit(solution)/shard_map/ppermute | solution.py:37
  71.0 2.2 %collective-permute-start.15 = (bf16[64,1024]{1,0:T(8,128)(2,1)S(1)}, bf16[64,1024]{1,0:T(8,128)(2,1)S(1)}, u32[]{:S(2)}, u32[]{:S(2)}) collective-permute-start(bf16[64,1024]{1,0:T(8,128)(2,1)S(1)} %get-tuple-element.30), channel_id=1, source_target_pairs={{0,32},{32,64},{64,96},{96,0},{1,33},{33,65},{65,97},{97,1},{2,34}... | collective-permute-start | bytes 393224 | tf_op jit(solution)/shard_map/ppermute | solution.py:35
  74.4 2.4 %collective-permute-start.16 = (bf16[64,1024]{1,0:T(8,128)(2,1)S(1)}, bf16[64,1024]{1,0:T(8,128)(2,1)S(1)}, u32[]{:S(2)}, u32[]{:S(2)}) collective-permute-start(bf16[64,1024]{1,0:T(8,128)(2,1)S(1)} %get-tuple-element.31), channel_id=1, source_target_pairs={{0,64},{32,96},{64,0},{96,32},{1,65},{33,97},{65,1},{97,33},{2,66}... | collective-permute-start | bytes 393224 | tf_op jit(solution)/shard_map/ppermute | solution.py:35
  78.8 3.4 %all-to-all-start.1 = ((bf16[8,16,576]{2,1,0:T(8,128)(2,1)}), bf16[8,16,576]{2,1,0:T(8,128)(2,1)S(1)}, u32[]{:S(2)}, u32[]{:S(2)}) async-start(bf16[8,16,576]{2,1,0:T(8,128)(2,1)} %add_convert_fusion.after_ref), calls=%async_computation.1 | async-start | bytes 327680 | tf_op jit(solution)/shard_map/all_to_all | solution.py:303
  82.5 1.7 %collective-permute-start.20 = (bf16[64,1024]{1,0:T(8,128)(2,1)S(1)}, bf16[64,1024]{1,0:T(8,128)(2,1)S(1)}, u32[]{:S(2)}, u32[]{:S(2)}) collective-permute-start(bf16[64,1024]{1,0:T(8,128)(2,1)S(1)} %second_sum.1.one_ref), channel_id=1, source_target_pairs={{0,96},{32,0},{64,32},{96,64},{1,97},{33,1},{65,33},{97,65},{2,98}... | collective-permute-start | bytes 393224 | tf_op jit(solution)/shard_map/ppermute | solution.py:35
  85.9 4.6 %all-to-all-done.1 = bf16[8,16,576]{2,1,0:T(8,128)(2,1)S(1)} async-done(((bf16[8,16,576]{2,1,0:T(8,128)(2,1)}), bf16[8,16,576]{2,1,0:T(8,128)(2,1)S(1)}, u32[]{:S(2)}, u32[]{:S(2)}) %all-to-all-start.1) | async-done | bytes 147488 | tf_op jit(solution)/shard_map/all_to_all | solution.py:303
  91.3 5.4 %collective-permute-start.21 = (bf16[4,64,1024]{2,1,0:T(8,128)(2,1)S(1)}, bf16[4,64,1024]{2,1,0:T(8,128)(2,1)S(1)}, u32[]{:S(2)}, u32[]{:S(2)}) collective-permute-start(bf16[4,64,1024]{2,1,0:T(8,128)(2,1)S(1)} %stacked.1.mine_ref), channel_id=1, source_target_pairs={{0,128},{128,0},{1,129},{129,1},{2,130},{130,2},{3,131},{131,3},{4... | collective-permute-start | bytes 1572872 | tf_op jit(solution)/shard_map/ppermute | solution.py:307
  96.7 1.5 %collective-permute-done.21.other_ref = bf16[4,64,1024]{2,1,0:T(8,128)(2,1)S(1)} collective-permute-done((bf16[4,64,1024]{2,1,0:T(8,128)(2,1)S(1)}, bf16[4,64,1024]{2,1,0:T(8,128)(2,1)S(1)}, u32[]{:S(2)}, u32[]{:S(2)}) %collective-permute-start.21) | collective-permute-done | bytes 524320 | tf_op jit(solution)/shard_map/ppermute | solution.py:307
  98.2 1.5 %placed.1 = f32[8,64,1024]{2,1,0:T(8,128)} custom-call(s32[1]{0:T(128)} %bitcast.core_ref, s32[1]{0:T(128)} %bitcast.1.place_ref, bf16[4,64,1024]{2,1,0:T(8,128)(2,1)S(1)} %stacked.1.mine_ref, bf16[4,64,1024]{2,1,0:T(8,128)(2,1)S(1)} %collective-permute-done.21.other_ref), custom_call_target="tpu_custom_call" | custom-call | tf_op jit(solution)/shard_map/placed/pallas_call | solution.py:101
  (47 shorter events, 16.1 us)
Async XLA Ops:
  2.0 17.2 %all-to-all-start = ((bf16[8,16,576]{2,1,0:T(8,128)(2,1)}), bf16[8,16,576]{2,1,0:T(8,128)(2,1)S(1)}, u32[]{:S(2)}, u32[]{:S(2)}) async-start(bf16[8,16,576]{2,1,0:T(8,128)(2,1)} %broadcast_in_dim.29), calls=%async_computation | async-start | bytes 327680 | tf_op jit(solution)/shard_map/all_to_all | solution.py:283
  19.2 7.2 %collective-permute-start.3 = (bf16[8,16,576]{2,1,0:T(8,128)(2,1)S(1)}, bf16[8,16,576]{2,1,0:T(8,128)(2,1)S(1)}, u32[]{:S(2)}, u32[]{:S(2)}) collective-permute-start(bf16[8,16,576]{2,1,0:T(8,128)(2,1)S(1)} %all-to-all-done.refs_0_), channel_id=1, source_target_pairs={{0,32},{32,64},{64,96},{1,33},{33,65},{65,97},{2,34},{34,66},{66,9... | collective-permute-start | bytes 442376 | tf_op jit(solution)/shard_map/ppermute | solution.py:30
  22.3 7.4 %collective-permute-start.2 = (bf16[8,16,576]{2,1,0:T(8,128)(2,1)S(1)}, bf16[8,16,576]{2,1,0:T(8,128)(2,1)S(1)}, u32[]{:S(2)}, u32[]{:S(2)}) collective-permute-start(bf16[8,16,576]{2,1,0:T(8,128)(2,1)S(1)} %all-to-all-done.refs_0_), channel_id=1, source_target_pairs={{0,3},{1,0},{2,1},{3,2},{4,7},{5,4},{6,5},{7,6},{8,11},{9,8},{10,9... | collective-permute-start | bytes 442376 | tf_op jit(solution)/shard_map/ppermute | solution.py:37
  25.2 5.9 %collective-permute-start.1 = (bf16[8,16,576]{2,1,0:T(8,128)(2,1)S(1)}, bf16[8,16,576]{2,1,0:T(8,128)(2,1)S(1)}, u32[]{:S(2)}, u32[]{:S(2)}) collective-permute-start(bf16[8,16,576]{2,1,0:T(8,128)(2,1)S(1)} %all-to-all-done.refs_0_), channel_id=1, source_target_pairs={{0,2},{1,3},{2,0},{3,1},{4,6},{5,7},{6,4},{7,5},{8,10},{9,11},{10,... | collective-permute-start | bytes 442376 | tf_op jit(solution)/shard_map/ppermute | solution.py:37
  25.7 7.1 %collective-permute-start = (bf16[8,16,576]{2,1,0:T(8,128)(2,1)S(1)}, bf16[8,16,576]{2,1,0:T(8,128)(2,1)S(1)}, u32[]{:S(2)}, u32[]{:S(2)}) collective-permute-start(bf16[8,16,576]{2,1,0:T(8,128)(2,1)S(1)} %all-to-all-done.refs_0_), channel_id=1, source_target_pairs={{0,1},{1,2},{2,3},{3,0},{4,5},{5,6},{6,7},{7,4},{8,9},{9,10},{10,1... | collective-permute-start | bytes 442376 | tf_op jit(solution)/shard_map/ppermute | solution.py:37
  26.4 9.1 %collective-permute-start.6 = (bf16[8,16,576]{2,1,0:T(8,128)(2,1)S(1)}, bf16[8,16,576]{2,1,0:T(8,128)(2,1)S(1)}, u32[]{:S(2)}, u32[]{:S(2)}) collective-permute-start(bf16[8,16,576]{2,1,0:T(8,128)(2,1)S(1)} %collective-permute-done.3.refs_4_), channel_id=1, source_target_pairs={{0,3},{1,0},{2,1},{3,2},{4,7},{5,4},{6,5},{7,6},{8,11},{9,8},{10,9... | collective-permute-start | bytes 442376 | tf_op jit(solution)/shard_map/ppermute | solution.py:37
  28.3 8.1 %collective-permute-start.5 = (bf16[8,16,576]{2,1,0:T(8,128)(2,1)S(1)}, bf16[8,16,576]{2,1,0:T(8,128)(2,1)S(1)}, u32[]{:S(2)}, u32[]{:S(2)}) collective-permute-start(bf16[8,16,576]{2,1,0:T(8,128)(2,1)S(1)} %collective-permute-done.3.refs_4_), channel_id=1, source_target_pairs={{0,2},{1,3},{2,0},{3,1},{4,6},{5,7},{6,4},{7,5},{8,10},{9,11},{10,... | collective-permute-start | bytes 442376 | tf_op jit(solution)/shard_map/ppermute | solution.py:37
  29.8 10.3 %collective-permute-start.4 = (bf16[8,16,576]{2,1,0:T(8,128)(2,1)S(1)}, bf16[8,16,576]{2,1,0:T(8,128)(2,1)S(1)}, u32[]{:S(2)}, u32[]{:S(2)}) collective-permute-start(bf16[8,16,576]{2,1,0:T(8,128)(2,1)S(1)} %collective-permute-done.3.refs_4_), channel_id=1, source_target_pairs={{0,1},{1,2},{2,3},{3,0},{4,5},{5,6},{6,7},{7,4},{8,9},{9,10},{10,1... | collective-permute-start | bytes 442376 | tf_op jit(solution)/shard_map/ppermute | solution.py:37
  57.5 8.6 %collective-permute-start.10 = (bf16[8,16,576]{2,1,0:T(8,128)(2,1)S(1)}, bf16[8,16,576]{2,1,0:T(8,128)(2,1)S(1)}, u32[]{:S(2)}, u32[]{:S(2)}) collective-permute-start(bf16[8,16,576]{2,1,0:T(8,128)(2,1)S(1)} %get-tuple-element.24), channel_id=1, source_target_pairs={{0,1},{1,2},{2,3},{3,0},{4,5},{5,6},{6,7},{7,4},{8,9},{9,10},{10,1... | collective-permute-start | bytes 442376 | tf_op jit(solution)/shard_map/ppermute | solution.py:37
  57.5 9.9 %collective-permute-start.11 = (bf16[8,16,576]{2,1,0:T(8,128)(2,1)S(1)}, bf16[8,16,576]{2,1,0:T(8,128)(2,1)S(1)}, u32[]{:S(2)}, u32[]{:S(2)}) collective-permute-start(bf16[8,16,576]{2,1,0:T(8,128)(2,1)S(1)} %get-tuple-element.25), channel_id=1, source_target_pairs={{0,2},{1,3},{2,0},{3,1},{4,6},{5,7},{6,4},{7,5},{8,10},{9,11},{10,... | collective-permute-start | bytes 442376 | tf_op jit(solution)/shard_map/ppermute | solution.py:37
  58.9 10.5 %collective-permute-start.12 = (bf16[8,16,576]{2,1,0:T(8,128)(2,1)S(1)}, bf16[8,16,576]{2,1,0:T(8,128)(2,1)S(1)}, u32[]{:S(2)}, u32[]{:S(2)}) collective-permute-start(bf16[8,16,576]{2,1,0:T(8,128)(2,1)S(1)} %get-tuple-element.26), channel_id=1, source_target_pairs={{0,3},{1,0},{2,1},{3,2},{4,7},{5,4},{6,5},{7,6},{8,11},{9,8},{10,9... | collective-permute-start | bytes 442376 | tf_op jit(solution)/shard_map/ppermute | solution.py:37
  60.2 10.6 %collective-permute-start.14 = (bf16[256,1024]{1,0:T(8,128)(2,1)S(1)}, bf16[256,1024]{1,0:T(8,128)(2,1)S(1)}, u32[]{:S(2)}, u32[]{:S(2)}) collective-permute-start(bf16[256,1024]{1,0:T(8,128)(2,1)S(1)} %get-tuple-element.28), channel_id=1, source_target_pairs={{0,128},{128,0},{1,129},{129,1},{2,130},{130,2},{3,131},{131,3},{4... | collective-permute-start | bytes 1572872 | tf_op jit(solution)/shard_map/ppermute | solution.py:73
  64.8 9.6 %collective-permute-start.7 = (bf16[8,16,576]{2,1,0:T(8,128)(2,1)S(1)}, bf16[8,16,576]{2,1,0:T(8,128)(2,1)S(1)}, u32[]{:S(2)}, u32[]{:S(2)}) collective-permute-start(bf16[8,16,576]{2,1,0:T(8,128)(2,1)S(1)} %get-tuple-element.20), channel_id=1, source_target_pairs={{0,1},{1,2},{2,3},{3,0},{4,5},{5,6},{6,7},{7,4},{8,9},{9,10},{10,1... | collective-permute-start | bytes 442376 | tf_op jit(solution)/shard_map/ppermute | solution.py:37
  66.1 10.8 %collective-permute-start.8 = (bf16[8,16,576]{2,1,0:T(8,128)(2,1)S(1)}, bf16[8,16,576]{2,1,0:T(8,128)(2,1)S(1)}, u32[]{:S(2)}, u32[]{:S(2)}) collective-permute-start(bf16[8,16,576]{2,1,0:T(8,128)(2,1)S(1)} %get-tuple-element.21), channel_id=1, source_target_pairs={{0,2},{1,3},{2,0},{3,1},{4,6},{5,7},{6,4},{7,5},{8,10},{9,11},{10,... | collective-permute-start | bytes 442376 | tf_op jit(solution)/shard_map/ppermute | solution.py:37
  67.4 10.6 %collective-permute-start.9 = (bf16[8,16,576]{2,1,0:T(8,128)(2,1)S(1)}, bf16[8,16,576]{2,1,0:T(8,128)(2,1)S(1)}, u32[]{:S(2)}, u32[]{:S(2)}) collective-permute-start(bf16[8,16,576]{2,1,0:T(8,128)(2,1)S(1)} %get-tuple-element.22), channel_id=1, source_target_pairs={{0,3},{1,0},{2,1},{3,2},{4,7},{5,4},{6,5},{7,6},{8,11},{9,8},{10,9... | collective-permute-start | bytes 442376 | tf_op jit(solution)/shard_map/ppermute | solution.py:37
  69.5 8.5 %collective-permute-start.13 = (bf16[8,16,576]{2,1,0:T(8,128)(2,1)S(1)}, bf16[8,16,576]{2,1,0:T(8,128)(2,1)S(1)}, u32[]{:S(2)}, u32[]{:S(2)}) collective-permute-start(bf16[8,16,576]{2,1,0:T(8,128)(2,1)S(1)} %add_convert_fusion.1.after_ref), channel_id=1, source_target_pairs={{32,0},{64,32},{96,64},{33,1},{65,33},{97,65},{34,2},{66,34},{98,6... | collective-permute-start | bytes 442376 | tf_op jit(solution)/shard_map/ppermute | solution.py:30
  71.0 11.2 %collective-permute-start.15 = (bf16[64,1024]{1,0:T(8,128)(2,1)S(1)}, bf16[64,1024]{1,0:T(8,128)(2,1)S(1)}, u32[]{:S(2)}, u32[]{:S(2)}) collective-permute-start(bf16[64,1024]{1,0:T(8,128)(2,1)S(1)} %get-tuple-element.30), channel_id=1, source_target_pairs={{0,32},{32,64},{64,96},{96,0},{1,33},{33,65},{65,97},{97,1},{2,34}... | collective-permute-start | bytes 393224 | tf_op jit(solution)/shard_map/ppermute | solution.py:35
  74.4 7.8 %collective-permute-start.16 = (bf16[64,1024]{1,0:T(8,128)(2,1)S(1)}, bf16[64,1024]{1,0:T(8,128)(2,1)S(1)}, u32[]{:S(2)}, u32[]{:S(2)}) collective-permute-start(bf16[64,1024]{1,0:T(8,128)(2,1)S(1)} %get-tuple-element.31), channel_id=1, source_target_pairs={{0,64},{32,96},{64,0},{96,32},{1,65},{33,97},{65,1},{97,33},{2,66}... | collective-permute-start | bytes 393224 | tf_op jit(solution)/shard_map/ppermute | solution.py:35
  76.8 5.6 %collective-permute-start.17 = (bf16[64,1024]{1,0:T(8,128)(2,1)S(1)}, bf16[64,1024]{1,0:T(8,128)(2,1)S(1)}, u32[]{:S(2)}, u32[]{:S(2)}) collective-permute-start(bf16[64,1024]{1,0:T(8,128)(2,1)S(1)} %get-tuple-element.32), channel_id=1, source_target_pairs={{0,96},{32,0},{64,32},{96,64},{1,97},{33,1},{65,33},{97,65},{2,98}... | collective-permute-start | bytes 393224 | tf_op jit(solution)/shard_map/ppermute | solution.py:35
  78.8 11.7 %all-to-all-start.1 = ((bf16[8,16,576]{2,1,0:T(8,128)(2,1)}), bf16[8,16,576]{2,1,0:T(8,128)(2,1)S(1)}, u32[]{:S(2)}, u32[]{:S(2)}) async-start(bf16[8,16,576]{2,1,0:T(8,128)(2,1)} %add_convert_fusion.after_ref), calls=%async_computation.1 | async-start | bytes 327680 | tf_op jit(solution)/shard_map/all_to_all | solution.py:303
  82.5 8.0 %collective-permute-start.20 = (bf16[64,1024]{1,0:T(8,128)(2,1)S(1)}, bf16[64,1024]{1,0:T(8,128)(2,1)S(1)}, u32[]{:S(2)}, u32[]{:S(2)}) collective-permute-start(bf16[64,1024]{1,0:T(8,128)(2,1)S(1)} %second_sum.1.one_ref), channel_id=1, source_target_pairs={{0,96},{32,0},{64,32},{96,64},{1,97},{33,1},{65,33},{97,65},{2,98}... | collective-permute-start | bytes 393224 | tf_op jit(solution)/shard_map/ppermute | solution.py:35
  84.3 6.3 %collective-permute-start.19 = (bf16[64,1024]{1,0:T(8,128)(2,1)S(1)}, bf16[64,1024]{1,0:T(8,128)(2,1)S(1)}, u32[]{:S(2)}, u32[]{:S(2)}) collective-permute-start(bf16[64,1024]{1,0:T(8,128)(2,1)S(1)} %second_sum.1.one_ref), channel_id=1, source_target_pairs={{0,64},{32,96},{64,0},{96,32},{1,65},{33,97},{65,1},{97,33},{2,66}... | collective-permute-start | bytes 393224 | tf_op jit(solution)/shard_map/ppermute | solution.py:35
  85.1 6.1 %collective-permute-start.18 = (bf16[64,1024]{1,0:T(8,128)(2,1)S(1)}, bf16[64,1024]{1,0:T(8,128)(2,1)S(1)}, u32[]{:S(2)}, u32[]{:S(2)}) collective-permute-start(bf16[64,1024]{1,0:T(8,128)(2,1)S(1)} %second_sum.1.one_ref), channel_id=1, source_target_pairs={{0,32},{32,64},{64,96},{96,0},{1,33},{33,65},{65,97},{97,1},{2,34}... | collective-permute-start | bytes 393224 | tf_op jit(solution)/shard_map/ppermute | solution.py:35
  91.3 6.9 %collective-permute-start.21 = (bf16[4,64,1024]{2,1,0:T(8,128)(2,1)S(1)}, bf16[4,64,1024]{2,1,0:T(8,128)(2,1)S(1)}, u32[]{:S(2)}, u32[]{:S(2)}) collective-permute-start(bf16[4,64,1024]{2,1,0:T(8,128)(2,1)S(1)} %stacked.1.mine_ref), channel_id=1, source_target_pairs={{0,128},{128,0},{1,129},{129,1},{2,130},{130,2},{3,131},{131,3},{4... | collective-permute-start | bytes 1572872 | tf_op jit(solution)/shard_map/ppermute | solution.py:307
  (3 other events, 11.4 us)

commit v5 on v4

--- a/solution.py
+++ b/solution.py
@@ -13,6 +13,8 @@
 TOK_CTX = 512
 DOC_MAX = 512
 QUERIES = 256
+AHEAD = 1
+BEHIND = 1
 KEYS = QUERIES + DOC_MAX
 WINDOW = TOK_CTX + DOC_MAX
 KV_WIDTH = NOPE + VDIM
@@ -120,19 +122,43 @@
 
 def attention_kernel(spot_ref, low_ref, *refs):
     own_pieces, prev_pieces, refs = refs[:Y], refs[Y : 2 * Y], refs[2 * Y :]
-    weight_ref, query_ref, grad_ref, d_query_ref, kept_ref, given_ref, *refs = refs
+    weight_ref, query_in, grad_in, d_query_ref, kept_ref, given_ref, *refs = refs
     own_terms, prev_terms, refs = refs[:Y], refs[Y : 2 * Y], refs[2 * Y :]
-    rows_ref, bias_ref, plain_ref, turned_ref, term_ref, rope_ref = refs
+    rows_ref, bias_ref, plain_ref, turned_ref, term_ref, rope_ref, *refs = refs
+    query_all, grad_all, copied = refs
     step = pl.program_id(0)
     low = jnp.bfloat16
     core, place, spot = spot_ref[0], spot_ref[1], spot_ref[2]
 
+    def copies(pair):
+        wide, narrow = 2 * (NOPE + ROPE), 2 * VDIM
+        return (
+            pltpu.make_async_copy(
+                query_in.at[:, pair * wide : (pair + 1) * wide], query_all.at[pair], copied.at[pair]
+            ),
+            pltpu.make_async_copy(
+                grad_in.at[:, pair * narrow : (pair + 1) * narrow],
+                grad_all.at[pair],
+                copied.at[2 + pair],
+            ),
+        )
+
     @pl.when(step == 0)
     def _():
+        for pair in range(2):
+            for copy in copies(pair):
+                copy.start()
         for by in range(Y):
             at = lax.rem(spot - by + Y, Y)
             rows_ref[:Z, at] = prev_pieces[by][...]
             rows_ref[Z:, at] = own_pieces[by][...]
+
+    for pair in range(2):
+
+        @pl.when(step == pair)
+        def _():
+            for copy in copies(pair):
+                copy.wait()
 
     rows = rows_ref[...].reshape(WINDOW, LATENT + ROPE)
     latent = rows[:, :LATENT]
@@ -156,54 +182,78 @@
             allowed = (key >= start) & (key <= query)
             bias_ref[tile] = jnp.where(allowed, 0.0, -1e30)
 
-    middle = []
+    kv_rows = mm(latent, weight_ref[...], NN).astype(low)
+    keys, values = [], []
     for head in range(2):
-        head_weight = weight_ref[:, head * KV_WIDTH : (head + 1) * KV_WIDTH]
-        kv_rows = mm(latent, head_weight, NN).astype(low)
-        key_nope = kv_rows[:, :NOPE]
-        value_rows = kv_rows[:, NOPE:]
+        key_nope = kv_rows[:, head * KV_WIDTH : head * KV_WIDTH + NOPE]
         parts = [key_nope, key_rope, blank] if head == 0 else [blank, key_nope, key_rope]
-        keys = jnp.concatenate(parts, axis=1)
-        grads = []
-        for tile in range(TOK_CTX // QUERIES):
-            first = tile * QUERIES
-            queries = query_ref[first : first + QUERIES, head * NOPE : head * NOPE + 2 * NOPE]
-            upstream = grad_ref[first : first + QUERIES, head * VDIM : (head + 1) * VDIM]
-            tile_keys = keys[first : first + KEYS]
-            tile_values = value_rows[first : first + KEYS]
-            scores = mm(tile_keys, queries, NT) * (FACTOR * LOG2E) + bias_ref[tile]
-            weights = jnp.exp2(scores - jnp.max(scores, axis=0, keepdims=True))
-            prob = weights * (1.0 / jnp.sum(weights, axis=0, keepdims=True))
-            prob_low = prob.astype(low)
-            dots = mm(tile_values, upstream, NT)
-            delta = jnp.sum(prob_low.astype(jnp.float32) * dots, axis=0, keepdims=True)
-            slope = (prob * (dots - delta)).astype(low)
-            grads.append((mm(slope, queries, NN), mm(prob_low, upstream, NN)))
-            d_query = mm(slope, tile_keys, TN) * FACTOR
-            at = slice(first, first + QUERIES)
-            if head == 0:
-                d_query_ref[at, :NOPE] = d_query[:, :NOPE].astype(low)
-                middle.append(d_query[:, NOPE:])
-            else:
-                d_query_ref[at, NOPE : 2 * NOPE] = (middle[tile] + d_query[:, :NOPE]).astype(low)
-                d_query_ref[at, 2 * NOPE :] = d_query[:, NOPE:].astype(low)
+        keys.append(jnp.concatenate(parts, axis=1))
+        values.append(kv_rows[:, head * KV_WIDTH + NOPE : (head + 1) * KV_WIDTH])
+    spans = [(head, tile * QUERIES) for head in range(2) for tile in range(TOK_CTX // QUERIES)]
+
+    def operands(head, first):
+        rows_at = slice(first, first + QUERIES)
+        queries = query_all[step, rows_at, head * NOPE : head * NOPE + 2 * NOPE]
+        return queries, grad_all[step, rows_at, head * VDIM : (head + 1) * VDIM]
+
+    def products(head, first):
+        queries, upstream = operands(head, first)
+        scores = mm(keys[head][first : first + KEYS], queries, NT)
+        return scores, mm(values[head][first : first + KEYS], upstream, NT)
+
+    def slopes(first, scores, dots):
+        scores = scores * (FACTOR * LOG2E) + bias_ref[first // QUERIES]
+        weights = jnp.exp2(scores - jnp.max(scores, axis=0, keepdims=True))
+        prob = weights * (1.0 / jnp.sum(weights, axis=0, keepdims=True))
+        prob_low = prob.astype(low)
+        delta = jnp.sum(prob_low.astype(jnp.float32) * dots, axis=0, keepdims=True)
+        return prob_low, (prob * (dots - delta)).astype(low)
+
+    def gradients(head, first, prob_low, slope):
+        queries, upstream = operands(head, first)
+        d_query = mm(slope, keys[head][first : first + KEYS], TN) * FACTOR
+        at = slice(first, first + QUERIES)
+        if head == 0:
+            d_query_ref[at, :NOPE] = d_query[:, :NOPE].astype(low)
+            middle.append(d_query[:, NOPE:])
+        else:
+            whole = middle[first // QUERIES] + d_query[:, :NOPE]
+            d_query_ref[at, NOPE : 2 * NOPE] = whole.astype(low)
+            d_query_ref[at, 2 * NOPE :] = d_query[:, NOPE:].astype(low)
+        return mm(slope, queries, NN), mm(prob_low, upstream, NN)
+
+    middle, grads = [], []
+    made, held = {}, {}
+    count = len(spans)
+    for turn in range(-AHEAD, count + BEHIND):
+        if turn + AHEAD < count:
+            made[turn + AHEAD] = products(*spans[turn + AHEAD])
+        if 0 <= turn < count:
+            held[turn] = slopes(spans[turn][1], *made.pop(turn))
+        if 0 <= turn - BEHIND:
+            grads.append(gradients(*spans[turn - BEHIND], *held.pop(turn - BEHIND)))
+
+    kv_grads, rope_grads = [], []
+    for head in range(2):
         key_grad, value_grad = (
             jnp.concatenate(
                 [one[:QUERIES], one[QUERIES:] + two[:-QUERIES], two[-QUERIES:]], axis=0
             )
-            for one, two in zip(*grads)
+            for one, two in zip(*grads[2 * head : 2 * head + 2])
         )
         key_grad = key_grad * FACTOR
         if head == 0:
             nope_grad, rope_grad = key_grad[:, :NOPE], key_grad[:, NOPE : NOPE + ROPE]
         else:
             nope_grad, rope_grad = key_grad[:, ROPE : ROPE + NOPE], key_grad[:, ROPE + NOPE :]
-        rope_ref[...] += rope_grad.reshape(rope_ref.shape)
-        kv_grad = jnp.concatenate([nope_grad.astype(low), value_grad.astype(low)], axis=1)
-        part = mm(turned_ref[...].reshape(LATENT, WINDOW), kv_grad, NN).astype(low)
-        kept_ref[:, head * KV_WIDTH : (head + 1) * KV_WIDTH] = part[: LATENT // 2]
-        given_ref[:, head * KV_WIDTH : (head + 1) * KV_WIDTH] = part[LATENT // 2 :]
-        term_ref[...] += mm(kv_grad, head_weight, NT).reshape(term_ref.shape)
+        rope_grads.append(rope_grad)
+        kv_grads += [nope_grad.astype(low), value_grad.astype(low)]
+    kv_grad = jnp.concatenate(kv_grads, axis=1)
+    rope_ref[...] += (rope_grads[0] + rope_grads[1]).reshape(rope_ref.shape)
+    part = mm(turned_ref[...].reshape(LATENT, WINDOW), kv_grad, NN).astype(low)
+    kept_ref[...] = part[: LATENT // 2]
+    given_ref[...] = part[LATENT // 2 :]
+    term_ref[...] += mm(kv_grad, weight_ref[...], NT).reshape(term_ref.shape)
 
     @pl.when(step == pl.num_programs(0) - 1)
     def _():
@@ -231,8 +281,8 @@
             whole((1, TOK_CTX)),
             *[whole(piece)] * (2 * Y),
             columns(LATENT, 2 * KV_WIDTH),
-            columns(TOK_CTX, 2 * (NOPE + ROPE)),
-            columns(TOK_CTX, 2 * VDIM),
+            pl.BlockSpec(memory_space=pltpu.HBM),
+            pl.BlockSpec(memory_space=pltpu.HBM),
         ],
         out_specs=[
             columns(TOK_CTX, 2 * (NOPE + ROPE)),
@@ -253,13 +303,24 @@
             pltpu.VMEM((2 * N_CTX, PART, WINDOW), jnp.bfloat16),
             pltpu.VMEM((2 * Z, Y, ROWS, LATENT), jnp.float32),
             pltpu.VMEM((2 * Z, Y, ROWS, ROPE), jnp.float32),
+            pltpu.VMEM((HEADS_DEV // 2, TOK_CTX, 2 * (NOPE + ROPE)), jnp.bfloat16),
+            pltpu.VMEM((HEADS_DEV // 2, TOK_CTX, 2 * VDIM), jnp.bfloat16),
+            pltpu.SemaphoreType.DMA((4,)),
         ],
         compiler_params=pltpu.CompilerParams(vmem_limit_bytes=48 * 1024 * 1024),
         cost_estimate=pl.CostEstimate(
             flops=8_000_000_000, bytes_accessed=10_000_000, transcendentals=1_600_000
         ),
         name="attention",
-    )(spot, low_keys, *own_pieces, *prev_pieces, weight, query, grad_out)
+    )(
+        spot,
+        low_keys,
+        *own_pieces,
+        *prev_pieces,
+        pltpu.with_memory_space_constraint(weight, pltpu.HBM),
+        pltpu.with_memory_space_constraint(query, pltpu.HBM),
+        pltpu.with_memory_space_constraint(grad_out, pltpu.HBM),
+    )
 
 
 def first_keys(lengths):

time: 100 us -> 96.1 us (0.961)
  local copies, waits for them, and re-layouts: 4.32 us -> 2.14 us
  Pallas kernels: 16.9 us -> 15 us
    unnamed x6 -> x2, local copies, waits for them, and re-layouts: 2.18 us -> 0.01 us
    pallas_call x1, Pallas kernels: 15.3 us -> 13.4 us  [attention(): pl.pallas_call(attention_kernel, grid=(HEADS_DEV // 2,), in_specs=[pl.Blo...]
where the time goes in v5:
time: 96.1 us; the launch traced here: 95.7 us
  starting transfers between devices  50.6 us (53%)
  waiting for transfers between devices  25.2 us (26%)
  Pallas kernels  15 us (16%)
  local copies, waits for them, and re-layouts  2.14 us (2%)
  other arithmetic  1.88 us (2%)
    ppermute x12, starting transfers between devices, turned(): return lax.ppermute(array, axis, pairs)  14.8 us
    pallas_call x1, Pallas kernels, attention(): pl.pallas_call(attention_kernel, grid=(HEADS_DEV // 2,), in_specs=[pl.Blo...  13.4 us
    ppermute x12, waiting for transfers between devices, turned(): return lax.ppermute(array, axis, pairs)  11.5 us
    ppermute x6, starting transfers between devices, turned(): lax.ppermute(array, axis, [(i, (i + by) % N_CTX) for i in range(N_CTX)])  9.12 us
    all_to_all x1, starting transfers between devices, on_device(): block = lax.all_to_all(block, 'head', 0, 0, axis_index_groups=along_z)  9.01 us
    all_to_all x1, waiting for transfers between devices, on_device(): block = lax.all_to_all(block, 'head', 0, 0, axis_index_groups=along_z)  6.6 us
    ppermute x1, starting transfers between devices, on_device(): d_kv_weight = placed(parts, lax.ppermute(parts, 'dp', [(0, 1), (1, 0)]))  5.38 us
    ppermute x1, starting transfers between devices, summed_weight(): other = lax.ppermute(given, 'dp', swap)  4.52 us
  transfers between devices with their start and end apart: 24, of which 11 were waited for; matrix products, arithmetic and copies ran while one was open for 3% of the time, Pallas kernels for 0%

profile of v5, /device:TPU:1, one launch (start us, length us, event | category | flops | bytes accessed | tf_op | source)
XLA Modules:
  0.0 95.7 jit_solution(7752048654953814515)
XLA Ops:
  0.6 1.4 %broadcast_in_dim.29 = bf16[8,16,576]{2,1,0:T(8,128)(2,1)} broadcast(bf16[16,576]{1,0:T(8,128)(2,1)} %bitcast.16), dimensions={1,2} | broadcast | bytes 165888 | tf_op jit(solution)/shard_map/broadcast_in_dim | solution.py:343
  2.0 9.0 %all-to-all-start = ((bf16[8,16,576]{2,1,0:T(8,128)(2,1)}), bf16[8,16,576]{2,1,0:T(8,128)(2,1)S(1)}, u32[]{:S(2)}, u32[]{:S(2)}) async-start(bf16[8,16,576]{2,1,0:T(8,128)(2,1)} %broadcast_in_dim.29), calls=%async_computation | async-start | bytes 327680 | tf_op jit(solution)/shard_map/all_to_all | solution.py:344
  12.6 6.6 %all-to-all-done.refs_0_ = bf16[8,16,576]{2,1,0:T(8,128)(2,1)S(1)} async-done(((bf16[8,16,576]{2,1,0:T(8,128)(2,1)}), bf16[8,16,576]{2,1,0:T(8,128)(2,1)S(1)}, u32[]{:S(2)}, u32[]{:S(2)}) %all-to-all-start) | async-done | bytes 147488 | tf_op jit(solution)/shard_map/all_to_all | solution.py:344
  19.2 3.1 %collective-permute-start.3 = (bf16[8,16,576]{2,1,0:T(8,128)(2,1)S(1)}, bf16[8,16,576]{2,1,0:T(8,128)(2,1)S(1)}, u32[]{:S(2)}, u32[]{:S(2)}) collective-permute-start(bf16[8,16,576]{2,1,0:T(8,128)(2,1)S(1)} %all-to-all-done.refs_0_), channel_id=1, source_target_pairs={{0,32},{32,64},{64,96},{1,33},{33,65},{65,97},{2,34},{34,66},{66,9... | collective-permute-start | bytes 442376 | tf_op jit(solution)/shard_map/ppermute | solution.py:32
  22.3 2.8 %collective-permute-start.2 = (bf16[8,16,576]{2,1,0:T(8,128)(2,1)S(1)}, bf16[8,16,576]{2,1,0:T(8,128)(2,1)S(1)}, u32[]{:S(2)}, u32[]{:S(2)}) collective-permute-start(bf16[8,16,576]{2,1,0:T(8,128)(2,1)S(1)} %all-to-all-done.refs_0_), channel_id=1, source_target_pairs={{0,3},{1,0},{2,1},{3,2},{4,7},{5,4},{6,5},{7,6},{8,11},{9,8},{10,9... | collective-permute-start | bytes 442376 | tf_op jit(solution)/shard_map/ppermute | solution.py:39
  26.4 2.0 %collective-permute-start.6 = (bf16[8,16,576]{2,1,0:T(8,128)(2,1)S(1)}, bf16[8,16,576]{2,1,0:T(8,128)(2,1)S(1)}, u32[]{:S(2)}, u32[]{:S(2)}) collective-permute-start(bf16[8,16,576]{2,1,0:T(8,128)(2,1)S(1)} %collective-permute-done.3.refs_4_), channel_id=1, source_target_pairs={{0,3},{1,0},{2,1},{3,2},{4,7},{5,4},{6,5},{7,6},{8,11},{9,8},{10,9... | collective-permute-start | bytes 442376 | tf_op jit(solution)/shard_map/ppermute | solution.py:39
  28.3 1.4 %collective-permute-start.5 = (bf16[8,16,576]{2,1,0:T(8,128)(2,1)S(1)}, bf16[8,16,576]{2,1,0:T(8,128)(2,1)S(1)}, u32[]{:S(2)}, u32[]{:S(2)}) collective-permute-start(bf16[8,16,576]{2,1,0:T(8,128)(2,1)S(1)} %collective-permute-done.3.refs_4_), channel_id=1, source_target_pairs={{0,2},{1,3},{2,0},{3,1},{4,6},{5,7},{6,4},{7,5},{8,10},{9,11},{10,... | collective-permute-start | bytes 442376 | tf_op jit(solution)/shard_map/ppermute | solution.py:39
  31.1 1.7 %collective-permute-done.refs_1_ = bf16[8,16,576]{2,1,0:T(8,128)(2,1)S(1)} collective-permute-done((bf16[8,16,576]{2,1,0:T(8,128)(2,1)S(1)}, bf16[8,16,576]{2,1,0:T(8,128)(2,1)S(1)}, u32[]{:S(2)}, u32[]{:S(2)}) %collective-permute-start) | collective-permute-done | bytes 147488 | tf_op jit(solution)/shard_map/ppermute | solution.py:39
  32.7 2.7 %collective-permute-done.6.refs_7_ = bf16[8,16,576]{2,1,0:T(8,128)(2,1)S(1)} collective-permute-done((bf16[8,16,576]{2,1,0:T(8,128)(2,1)S(1)}, bf16[8,16,576]{2,1,0:T(8,128)(2,1)S(1)}, u32[]{:S(2)}, u32[]{:S(2)}) %collective-permute-start.6) | collective-permute-done | bytes 147488 | tf_op jit(solution)/shard_map/ppermute | solution.py:39
  36.5 3.6 %collective-permute-done.4.refs_5_ = bf16[8,16,576]{2,1,0:T(8,128)(2,1)S(1)} collective-permute-done((bf16[8,16,576]{2,1,0:T(8,128)(2,1)S(1)}, bf16[8,16,576]{2,1,0:T(8,128)(2,1)S(1)}, u32[]{:S(2)}, u32[]{:S(2)}) %collective-permute-start.4) | collective-permute-done | bytes 147488 | tf_op jit(solution)/shard_map/ppermute | solution.py:39
  40.1 13.4 %attention.1 = (bf16[512,768]{1,0:T(8,128)(2,1)}, bf16[256,1024]{1,0:T(8,128)(2,1)S(1)}, bf16[256,1024]{1,0:T(8,128)(2,1)S(1)}, f32[8,16,576]{2,1,0:T(8,128)S(1)...) custom-call(s32[3]{0:T(128)S(1)} %pad_add_fusion.spot_ref, ...), custom_call_target="tpu_custom_call" | custom-call | flops 8000000000 | bytes 10000000 | tf_op jit(solution)/shard_map/attention/pallas_call | solution.py:276
  53.5 1.4 %collective-permute-start.11 = (bf16[8,16,576]{2,1,0:T(8,128)(2,1)S(1)}, bf16[8,16,576]{2,1,0:T(8,128)(2,1)S(1)}, u32[]{:S(2)}, u32[]{:S(2)}) collective-permute-start(bf16[8,16,576]{2,1,0:T(8,128)(2,1)S(1)} %get-tuple-element.25), channel_id=1, source_target_pairs={{0,2},{1,3},{2,0},{3,1},{4,6},{5,7},{6,4},{7,5},{8,10},{9,11},{10,... | collective-permute-start | bytes 442376 | tf_op jit(solution)/shard_map/ppermute | solution.py:39
  54.9 1.3 %collective-permute-start.12 = (bf16[8,16,576]{2,1,0:T(8,128)(2,1)S(1)}, bf16[8,16,576]{2,1,0:T(8,128)(2,1)S(1)}, u32[]{:S(2)}, u32[]{:S(2)}) collective-permute-start(bf16[8,16,576]{2,1,0:T(8,128)(2,1)S(1)} %get-tuple-element.26), channel_id=1, source_target_pairs={{0,3},{1,0},{2,1},{3,2},{4,7},{5,4},{6,5},{7,6},{8,11},{9,8},{10,9... | collective-permute-start | bytes 442376 | tf_op jit(solution)/shard_map/ppermute | solution.py:39
  56.2 4.5 %collective-permute-start.14 = (bf16[256,1024]{1,0:T(8,128)(2,1)S(1)}, bf16[256,1024]{1,0:T(8,128)(2,1)S(1)}, u32[]{:S(2)}, u32[]{:S(2)}) collective-permute-start(bf16[256,1024]{1,0:T(8,128)(2,1)S(1)} %get-tuple-element.28), channel_id=1, source_target_pairs={{0,128},{128,0},{1,129},{129,1},{2,130},{130,2},{3,131},{131,3},{4... | collective-permute-start | bytes 1572872 | tf_op jit(solution)/shard_map/ppermute | solution.py:75
  62.0 1.3 %collective-permute-start.8 = (bf16[8,16,576]{2,1,0:T(8,128)(2,1)S(1)}, bf16[8,16,576]{2,1,0:T(8,128)(2,1)S(1)}, u32[]{:S(2)}, u32[]{:S(2)}) collective-permute-start(bf16[8,16,576]{2,1,0:T(8,128)(2,1)S(1)} %get-tuple-element.21), channel_id=1, source_target_pairs={{0,2},{1,3},{2,0},{3,1},{4,6},{5,7},{6,4},{7,5},{8,10},{9,11},{10,... | collective-permute-start | bytes 442376 | tf_op jit(solution)/shard_map/ppermute | solution.py:39
  63.4 2.1 %collective-permute-start.9 = (bf16[8,16,576]{2,1,0:T(8,128)(2,1)S(1)}, bf16[8,16,576]{2,1,0:T(8,128)(2,1)S(1)}, u32[]{:S(2)}, u32[]{:S(2)}) collective-permute-start(bf16[8,16,576]{2,1,0:T(8,128)(2,1)S(1)} %get-tuple-element.22), channel_id=1, source_target_pairs={{0,3},{1,0},{2,1},{3,2},{4,7},{5,4},{6,5},{7,6},{8,11},{9,8},{10,9... | collective-permute-start | bytes 442376 | tf_op jit(solution)/shard_map/ppermute | solution.py:39
  67.0 2.2 %collective-permute-start.15 = (bf16[64,1024]{1,0:T(8,128)(2,1)S(1)}, bf16[64,1024]{1,0:T(8,128)(2,1)S(1)}, u32[]{:S(2)}, u32[]{:S(2)}) collective-permute-start(bf16[64,1024]{1,0:T(8,128)(2,1)S(1)} %get-tuple-element.30), channel_id=1, source_target_pairs={{0,32},{32,64},{64,96},{96,0},{1,33},{33,65},{65,97},{97,1},{2,34}... | collective-permute-start | bytes 393224 | tf_op jit(solution)/shard_map/ppermute | solution.py:37
  70.4 2.4 %collective-permute-start.16 = (bf16[64,1024]{1,0:T(8,128)(2,1)S(1)}, bf16[64,1024]{1,0:T(8,128)(2,1)S(1)}, u32[]{:S(2)}, u32[]{:S(2)}) collective-permute-start(bf16[64,1024]{1,0:T(8,128)(2,1)S(1)} %get-tuple-element.31), channel_id=1, source_target_pairs={{0,64},{32,96},{64,0},{96,32},{1,65},{33,97},{65,1},{97,33},{2,66}... | collective-permute-start | bytes 393224 | tf_op jit(solution)/shard_map/ppermute | solution.py:37
  74.8 3.4 %all-to-all-start.1 = ((bf16[8,16,576]{2,1,0:T(8,128)(2,1)}), bf16[8,16,576]{2,1,0:T(8,128)(2,1)S(1)}, u32[]{:S(2)}, u32[]{:S(2)}) async-start(bf16[8,16,576]{2,1,0:T(8,128)(2,1)} %add_convert_fusion.after_ref), calls=%async_computation.1 | async-start | bytes 327680 | tf_op jit(solution)/shard_map/all_to_all | solution.py:364
  78.5 1.7 %collective-permute-start.20 = (bf16[64,1024]{1,0:T(8,128)(2,1)S(1)}, bf16[64,1024]{1,0:T(8,128)(2,1)S(1)}, u32[]{:S(2)}, u32[]{:S(2)}) collective-permute-start(bf16[64,1024]{1,0:T(8,128)(2,1)S(1)} %second_sum.1.one_ref), channel_id=1, source_target_pairs={{0,96},{32,0},{64,32},{96,64},{1,97},{33,1},{65,33},{97,65},{2,98}... | collective-permute-start | bytes 393224 | tf_op jit(solution)/shard_map/ppermute | solution.py:37
  81.9 4.5 %all-to-all-done.1 = bf16[8,16,576]{2,1,0:T(8,128)(2,1)S(1)} async-done(((bf16[8,16,576]{2,1,0:T(8,128)(2,1)}), bf16[8,16,576]{2,1,0:T(8,128)(2,1)S(1)}, u32[]{:S(2)}, u32[]{:S(2)}) %all-to-all-start.1) | async-done | bytes 147488 | tf_op jit(solution)/shard_map/all_to_all | solution.py:364
  87.3 5.4 %collective-permute-start.21 = (bf16[4,64,1024]{2,1,0:T(8,128)(2,1)S(1)}, bf16[4,64,1024]{2,1,0:T(8,128)(2,1)S(1)}, u32[]{:S(2)}, u32[]{:S(2)}) collective-permute-start(bf16[4,64,1024]{2,1,0:T(8,128)(2,1)S(1)} %stacked.1.mine_ref), channel_id=1, source_target_pairs={{0,128},{128,0},{1,129},{129,1},{2,130},{130,2},{3,131},{131,3},{4... | collective-permute-start | bytes 1572872 | tf_op jit(solution)/shard_map/ppermute | solution.py:368
  92.7 1.5 %collective-permute-done.21.other_ref = bf16[4,64,1024]{2,1,0:T(8,128)(2,1)S(1)} collective-permute-done((bf16[4,64,1024]{2,1,0:T(8,128)(2,1)S(1)}, bf16[4,64,1024]{2,1,0:T(8,128)(2,1)S(1)}, u32[]{:S(2)}, u32[]{:S(2)}) %collective-permute-start.21) | collective-permute-done | bytes 524320 | tf_op jit(solution)/shard_map/ppermute | solution.py:368
  94.2 1.5 %placed.1 = f32[8,64,1024]{2,1,0:T(8,128)} custom-call(s32[1]{0:T(128)} %bitcast.core_ref, s32[1]{0:T(128)} %bitcast.1.place_ref, bf16[4,64,1024]{2,1,0:T(8,128)(2,1)S(1)} %stacked.1.mine_ref, bf16[4,64,1024]{2,1,0:T(8,128)(2,1)S(1)} %collective-permute-done.21.other_ref), custom_call_target="tpu_custom_call" | custom-call | tf_op jit(solution)/shard_map/placed/pallas_call | solution.py:103
  (43 shorter events, 14.1 us)
Async XLA Ops:
  2.0 17.2 %all-to-all-start = ((bf16[8,16,576]{2,1,0:T(8,128)(2,1)}), bf16[8,16,576]{2,1,0:T(8,128)(2,1)S(1)}, u32[]{:S(2)}, u32[]{:S(2)}) async-start(bf16[8,16,576]{2,1,0:T(8,128)(2,1)} %broadcast_in_dim.29), calls=%async_computation | async-start | bytes 327680 | tf_op jit(solution)/shard_map/all_to_all | solution.py:344
  19.2 7.2 %collective-permute-start.3 = (bf16[8,16,576]{2,1,0:T(8,128)(2,1)S(1)}, bf16[8,16,576]{2,1,0:T(8,128)(2,1)S(1)}, u32[]{:S(2)}, u32[]{:S(2)}) collective-permute-start(bf16[8,16,576]{2,1,0:T(8,128)(2,1)S(1)} %all-to-all-done.refs_0_), channel_id=1, source_target_pairs={{0,32},{32,64},{64,96},{1,33},{33,65},{65,97},{2,34},{34,66},{66,9... | collective-permute-start | bytes 442376 | tf_op jit(solution)/shard_map/ppermute | solution.py:32
  22.3 7.4 %collective-permute-start.2 = (bf16[8,16,576]{2,1,0:T(8,128)(2,1)S(1)}, bf16[8,16,576]{2,1,0:T(8,128)(2,1)S(1)}, u32[]{:S(2)}, u32[]{:S(2)}) collective-permute-start(bf16[8,16,576]{2,1,0:T(8,128)(2,1)S(1)} %all-to-all-done.refs_0_), channel_id=1, source_target_pairs={{0,3},{1,0},{2,1},{3,2},{4,7},{5,4},{6,5},{7,6},{8,11},{9,8},{10,9... | collective-permute-start | bytes 442376 | tf_op jit(solution)/shard_map/ppermute | solution.py:39
  25.2 5.9 %collective-permute-start.1 = (bf16[8,16,576]{2,1,0:T(8,128)(2,1)S(1)}, bf16[8,16,576]{2,1,0:T(8,128)(2,1)S(1)}, u32[]{:S(2)}, u32[]{:S(2)}) collective-permute-start(bf16[8,16,576]{2,1,0:T(8,128)(2,1)S(1)} %all-to-all-done.refs_0_), channel_id=1, source_target_pairs={{0,2},{1,3},{2,0},{3,1},{4,6},{5,7},{6,4},{7,5},{8,10},{9,11},{10,... | collective-permute-start | bytes 442376 | tf_op jit(solution)/shard_map/ppermute | solution.py:39
  25.7 7.1 %collective-permute-start = (bf16[8,16,576]{2,1,0:T(8,128)(2,1)S(1)}, bf16[8,16,576]{2,1,0:T(8,128)(2,1)S(1)}, u32[]{:S(2)}, u32[]{:S(2)}) collective-permute-start(bf16[8,16,576]{2,1,0:T(8,128)(2,1)S(1)} %all-to-all-done.refs_0_), channel_id=1, source_target_pairs={{0,1},{1,2},{2,3},{3,0},{4,5},{5,6},{6,7},{7,4},{8,9},{9,10},{10,1... | collective-permute-start | bytes 442376 | tf_op jit(solution)/shard_map/ppermute | solution.py:39
  26.4 9.1 %collective-permute-start.6 = (bf16[8,16,576]{2,1,0:T(8,128)(2,1)S(1)}, bf16[8,16,576]{2,1,0:T(8,128)(2,1)S(1)}, u32[]{:S(2)}, u32[]{:S(2)}) collective-permute-start(bf16[8,16,576]{2,1,0:T(8,128)(2,1)S(1)} %collective-permute-done.3.refs_4_), channel_id=1, source_target_pairs={{0,3},{1,0},{2,1},{3,2},{4,7},{5,4},{6,5},{7,6},{8,11},{9,8},{10,9... | collective-permute-start | bytes 442376 | tf_op jit(solution)/shard_map/ppermute | solution.py:39
  28.3 8.1 %collective-permute-start.5 = (bf16[8,16,576]{2,1,0:T(8,128)(2,1)S(1)}, bf16[8,16,576]{2,1,0:T(8,128)(2,1)S(1)}, u32[]{:S(2)}, u32[]{:S(2)}) collective-permute-start(bf16[8,16,576]{2,1,0:T(8,128)(2,1)S(1)} %collective-permute-done.3.refs_4_), channel_id=1, source_target_pairs={{0,2},{1,3},{2,0},{3,1},{4,6},{5,7},{6,4},{7,5},{8,10},{9,11},{10,... | collective-permute-start | bytes 442376 | tf_op jit(solution)/shard_map/ppermute | solution.py:39
  29.8 10.3 %collective-permute-start.4 = (bf16[8,16,576]{2,1,0:T(8,128)(2,1)S(1)}, bf16[8,16,576]{2,1,0:T(8,128)(2,1)S(1)}, u32[]{:S(2)}, u32[]{:S(2)}) collective-permute-start(bf16[8,16,576]{2,1,0:T(8,128)(2,1)S(1)} %collective-permute-done.3.refs_4_), channel_id=1, source_target_pairs={{0,1},{1,2},{2,3},{3,0},{4,5},{5,6},{6,7},{7,4},{8,9},{9,10},{10,1... | collective-permute-start | bytes 442376 | tf_op jit(solution)/shard_map/ppermute | solution.py:39
  53.4 8.6 %collective-permute-start.10 = (bf16[8,16,576]{2,1,0:T(8,128)(2,1)S(1)}, bf16[8,16,576]{2,1,0:T(8,128)(2,1)S(1)}, u32[]{:S(2)}, u32[]{:S(2)}) collective-permute-start(bf16[8,16,576]{2,1,0:T(8,128)(2,1)S(1)} %get-tuple-element.24), channel_id=1, source_target_pairs={{0,1},{1,2},{2,3},{3,0},{4,5},{5,6},{6,7},{7,4},{8,9},{9,10},{10,1... | collective-permute-start | bytes 442376 | tf_op jit(solution)/shard_map/ppermute | solution.py:39
  53.5 9.9 %collective-permute-start.11 = (bf16[8,16,576]{2,1,0:T(8,128)(2,1)S(1)}, bf16[8,16,576]{2,1,0:T(8,128)(2,1)S(1)}, u32[]{:S(2)}, u32[]{:S(2)}) collective-permute-start(bf16[8,16,576]{2,1,0:T(8,128)(2,1)S(1)} %get-tuple-element.25), channel_id=1, source_target_pairs={{0,2},{1,3},{2,0},{3,1},{4,6},{5,7},{6,4},{7,5},{8,10},{9,11},{10,... | collective-permute-start | bytes 442376 | tf_op jit(solution)/shard_map/ppermute | solution.py:39
  54.9 10.5 %collective-permute-start.12 = (bf16[8,16,576]{2,1,0:T(8,128)(2,1)S(1)}, bf16[8,16,576]{2,1,0:T(8,128)(2,1)S(1)}, u32[]{:S(2)}, u32[]{:S(2)}) collective-permute-start(bf16[8,16,576]{2,1,0:T(8,128)(2,1)S(1)} %get-tuple-element.26), channel_id=1, source_target_pairs={{0,3},{1,0},{2,1},{3,2},{4,7},{5,4},{6,5},{7,6},{8,11},{9,8},{10,9... | collective-permute-start | bytes 442376 | tf_op jit(solution)/shard_map/ppermute | solution.py:39
  56.2 10.6 %collective-permute-start.14 = (bf16[256,1024]{1,0:T(8,128)(2,1)S(1)}, bf16[256,1024]{1,0:T(8,128)(2,1)S(1)}, u32[]{:S(2)}, u32[]{:S(2)}) collective-permute-start(bf16[256,1024]{1,0:T(8,128)(2,1)S(1)} %get-tuple-element.28), channel_id=1, source_target_pairs={{0,128},{128,0},{1,129},{129,1},{2,130},{130,2},{3,131},{131,3},{4... | collective-permute-start | bytes 1572872 | tf_op jit(solution)/shard_map/ppermute | solution.py:75
  60.8 9.6 %collective-permute-start.7 = (bf16[8,16,576]{2,1,0:T(8,128)(2,1)S(1)}, bf16[8,16,576]{2,1,0:T(8,128)(2,1)S(1)}, u32[]{:S(2)}, u32[]{:S(2)}) collective-permute-start(bf16[8,16,576]{2,1,0:T(8,128)(2,1)S(1)} %get-tuple-element.20), channel_id=1, source_target_pairs={{0,1},{1,2},{2,3},{3,0},{4,5},{5,6},{6,7},{7,4},{8,9},{9,10},{10,1... | collective-permute-start | bytes 442376 | tf_op jit(solution)/shard_map/ppermute | solution.py:39
  62.0 10.8 %collective-permute-start.8 = (bf16[8,16,576]{2,1,0:T(8,128)(2,1)S(1)}, bf16[8,16,576]{2,1,0:T(8,128)(2,1)S(1)}, u32[]{:S(2)}, u32[]{:S(2)}) collective-permute-start(bf16[8,16,576]{2,1,0:T(8,128)(2,1)S(1)} %get-tuple-element.21), channel_id=1, source_target_pairs={{0,2},{1,3},{2,0},{3,1},{4,6},{5,7},{6,4},{7,5},{8,10},{9,11},{10,... | collective-permute-start | bytes 442376 | tf_op jit(solution)/shard_map/ppermute | solution.py:39
  63.4 10.6 %collective-permute-start.9 = (bf16[8,16,576]{2,1,0:T(8,128)(2,1)S(1)}, bf16[8,16,576]{2,1,0:T(8,128)(2,1)S(1)}, u32[]{:S(2)}, u32[]{:S(2)}) collective-permute-start(bf16[8,16,576]{2,1,0:T(8,128)(2,1)S(1)} %get-tuple-element.22), channel_id=1, source_target_pairs={{0,3},{1,0},{2,1},{3,2},{4,7},{5,4},{6,5},{7,6},{8,11},{9,8},{10,9... | collective-permute-start | bytes 442376 | tf_op jit(solution)/shard_map/ppermute | solution.py:39
  65.5 8.5 %collective-permute-start.13 = (bf16[8,16,576]{2,1,0:T(8,128)(2,1)S(1)}, bf16[8,16,576]{2,1,0:T(8,128)(2,1)S(1)}, u32[]{:S(2)}, u32[]{:S(2)}) collective-permute-start(bf16[8,16,576]{2,1,0:T(8,128)(2,1)S(1)} %add_convert_fusion.1.after_ref), channel_id=1, source_target_pairs={{32,0},{64,32},{96,64},{33,1},{65,33},{97,65},{34,2},{66,34},{98,6... | collective-permute-start | bytes 442376 | tf_op jit(solution)/shard_map/ppermute | solution.py:32
  67.0 11.2 %collective-permute-start.15 = (bf16[64,1024]{1,0:T(8,128)(2,1)S(1)}, bf16[64,1024]{1,0:T(8,128)(2,1)S(1)}, u32[]{:S(2)}, u32[]{:S(2)}) collective-permute-start(bf16[64,1024]{1,0:T(8,128)(2,1)S(1)} %get-tuple-element.30), channel_id=1, source_target_pairs={{0,32},{32,64},{64,96},{96,0},{1,33},{33,65},{65,97},{97,1},{2,34}... | collective-permute-start | bytes 393224 | tf_op jit(solution)/shard_map/ppermute | solution.py:37
  70.4 7.8 %collective-permute-start.16 = (bf16[64,1024]{1,0:T(8,128)(2,1)S(1)}, bf16[64,1024]{1,0:T(8,128)(2,1)S(1)}, u32[]{:S(2)}, u32[]{:S(2)}) collective-permute-start(bf16[64,1024]{1,0:T(8,128)(2,1)S(1)} %get-tuple-element.31), channel_id=1, source_target_pairs={{0,64},{32,96},{64,0},{96,32},{1,65},{33,97},{65,1},{97,33},{2,66}... | collective-permute-start | bytes 393224 | tf_op jit(solution)/shard_map/ppermute | solution.py:37
  72.8 5.6 %collective-permute-start.17 = (bf16[64,1024]{1,0:T(8,128)(2,1)S(1)}, bf16[64,1024]{1,0:T(8,128)(2,1)S(1)}, u32[]{:S(2)}, u32[]{:S(2)}) collective-permute-start(bf16[64,1024]{1,0:T(8,128)(2,1)S(1)} %get-tuple-element.32), channel_id=1, source_target_pairs={{0,96},{32,0},{64,32},{96,64},{1,97},{33,1},{65,33},{97,65},{2,98}... | collective-permute-start | bytes 393224 | tf_op jit(solution)/shard_map/ppermute | solution.py:37
  74.8 11.6 %all-to-all-start.1 = ((bf16[8,16,576]{2,1,0:T(8,128)(2,1)}), bf16[8,16,576]{2,1,0:T(8,128)(2,1)S(1)}, u32[]{:S(2)}, u32[]{:S(2)}) async-start(bf16[8,16,576]{2,1,0:T(8,128)(2,1)} %add_convert_fusion.after_ref), calls=%async_computation.1 | async-start | bytes 327680 | tf_op jit(solution)/shard_map/all_to_all | solution.py:364
  78.5 7.9 %collective-permute-start.20 = (bf16[64,1024]{1,0:T(8,128)(2,1)S(1)}, bf16[64,1024]{1,0:T(8,128)(2,1)S(1)}, u32[]{:S(2)}, u32[]{:S(2)}) collective-permute-start(bf16[64,1024]{1,0:T(8,128)(2,1)S(1)} %second_sum.1.one_ref), channel_id=1, source_target_pairs={{0,96},{32,0},{64,32},{96,64},{1,97},{33,1},{65,33},{97,65},{2,98}... | collective-permute-start | bytes 393224 | tf_op jit(solution)/shard_map/ppermute | solution.py:37
  80.2 6.2 %collective-permute-start.19 = (bf16[64,1024]{1,0:T(8,128)(2,1)S(1)}, bf16[64,1024]{1,0:T(8,128)(2,1)S(1)}, u32[]{:S(2)}, u32[]{:S(2)}) collective-permute-start(bf16[64,1024]{1,0:T(8,128)(2,1)S(1)} %second_sum.1.one_ref), channel_id=1, source_target_pairs={{0,64},{32,96},{64,0},{96,32},{1,65},{33,97},{65,1},{97,33},{2,66}... | collective-permute-start | bytes 393224 | tf_op jit(solution)/shard_map/ppermute | solution.py:37
  81.1 6.1 %collective-permute-start.18 = (bf16[64,1024]{1,0:T(8,128)(2,1)S(1)}, bf16[64,1024]{1,0:T(8,128)(2,1)S(1)}, u32[]{:S(2)}, u32[]{:S(2)}) collective-permute-start(bf16[64,1024]{1,0:T(8,128)(2,1)S(1)} %second_sum.1.one_ref), channel_id=1, source_target_pairs={{0,32},{32,64},{64,96},{96,0},{1,33},{33,65},{65,97},{97,1},{2,34}... | collective-permute-start | bytes 393224 | tf_op jit(solution)/shard_map/ppermute | solution.py:37
  87.3 6.9 %collective-permute-start.21 = (bf16[4,64,1024]{2,1,0:T(8,128)(2,1)S(1)}, bf16[4,64,1024]{2,1,0:T(8,128)(2,1)S(1)}, u32[]{:S(2)}, u32[]{:S(2)}) collective-permute-start(bf16[4,64,1024]{2,1,0:T(8,128)(2,1)S(1)} %stacked.1.mine_ref), channel_id=1, source_target_pairs={{0,128},{128,0},{1,129},{129,1},{2,130},{130,2},{3,131},{131,3},{4... | collective-permute-start | bytes 1572872 | tf_op jit(solution)/shard_map/ppermute | solution.py:368
  (1 other events, 9.3 us)

commit v6 on v5

--- a/solution.py
+++ b/solution.py
@@ -122,79 +122,52 @@
 
 def attention_kernel(spot_ref, low_ref, *refs):
     own_pieces, prev_pieces, refs = refs[:Y], refs[Y : 2 * Y], refs[2 * Y :]
-    weight_ref, query_in, grad_in, d_query_ref, kept_ref, given_ref, *refs = refs
+    weight_in, query_in, grad_in, d_query_ref, kept_ref, given_ref, *refs = refs
     own_terms, prev_terms, refs = refs[:Y], refs[Y : 2 * Y], refs[2 * Y :]
-    rows_ref, bias_ref, plain_ref, turned_ref, term_ref, rope_ref, *refs = refs
-    query_all, grad_all, copied = refs
-    step = pl.program_id(0)
+    rows_ref, plain_ref, turned_ref, term_ref, rope_ref, *refs = refs
+    weight_ref, query_ref, grad_ref, copied = refs
     low = jnp.bfloat16
     core, place, spot = spot_ref[0], spot_ref[1], spot_ref[2]
-
-    def copies(pair):
-        wide, narrow = 2 * (NOPE + ROPE), 2 * VDIM
-        return (
-            pltpu.make_async_copy(
-                query_in.at[:, pair * wide : (pair + 1) * wide], query_all.at[pair], copied.at[pair]
-            ),
-            pltpu.make_async_copy(
-                grad_in.at[:, pair * narrow : (pair + 1) * narrow],
-                grad_all.at[pair],
-                copied.at[2 + pair],
-            ),
+    copies = [
+        pltpu.make_async_copy(source, target, copied.at[at])
+        for at, (source, target) in enumerate(
+            ((weight_in, weight_ref), (query_in, query_ref), (grad_in, grad_ref))
         )
-
-    @pl.when(step == 0)
-    def _():
-        for pair in range(2):
-            for copy in copies(pair):
-                copy.start()
-        for by in range(Y):
-            at = lax.rem(spot - by + Y, Y)
-            rows_ref[:Z, at] = prev_pieces[by][...]
-            rows_ref[Z:, at] = own_pieces[by][...]
-
-    for pair in range(2):
-
-        @pl.when(step == pair)
-        def _():
-            for copy in copies(pair):
-                copy.wait()
-
+    ]
+    for copy in copies:
+        copy.start()
+
+    for by in range(Y):
+        at = lax.rem(spot - by + Y, Y)
+        rows_ref[:Z, at] = prev_pieces[by][...]
+        rows_ref[Z:, at] = own_pieces[by][...]
     rows = rows_ref[...].reshape(WINDOW, LATENT + ROPE)
     latent = rows[:, :LATENT]
     key_rope = rows[:, LATENT:]
     blank = jnp.zeros((WINDOW, ROPE), low)
-
-    @pl.when(step == 0)
-    def _():
-        plain_ref[...] = latent.T.reshape(2 * N_CTX, PART, WINDOW)
-        for by in range(N_CTX):
-            at = lax.rem(place + by, N_CTX)
-            turned_ref[by] = plain_ref[core * N_CTX + at]
-            turned_ref[N_CTX + by] = plain_ref[(1 - core) * N_CTX + at]
-        term_ref[...] = jnp.zeros_like(term_ref)
-        rope_ref[...] = jnp.zeros_like(rope_ref)
-        for tile in range(TOK_CTX // QUERIES):
-            first = tile * QUERIES
-            key = first + lax.broadcasted_iota(jnp.int32, (KEYS, QUERIES), 0)
-            query = first + DOC_MAX + lax.broadcasted_iota(jnp.int32, (KEYS, QUERIES), 1)
-            start = low_ref[:, first : first + QUERIES]
-            allowed = (key >= start) & (key <= query)
-            bias_ref[tile] = jnp.where(allowed, 0.0, -1e30)
+    biases = []
+    for first in range(0, TOK_CTX, QUERIES):
+        key = first + lax.broadcasted_iota(jnp.int32, (KEYS, QUERIES), 0)
+        query = first + DOC_MAX + lax.broadcasted_iota(jnp.int32, (KEYS, QUERIES), 1)
+        start = low_ref[:, first : first + QUERIES]
+        biases.append(jnp.where((key >= start) & (key <= query), 0.0, -1e30))
+    for copy in copies:
+        copy.wait()
 
     kv_rows = mm(latent, weight_ref[...], NN).astype(low)
     keys, values = [], []
-    for head in range(2):
+    for head in range(HEADS_DEV):
         key_nope = kv_rows[:, head * KV_WIDTH : head * KV_WIDTH + NOPE]
-        parts = [key_nope, key_rope, blank] if head == 0 else [blank, key_nope, key_rope]
+        parts = [key_nope, key_rope, blank] if head % 2 == 0 else [blank, key_nope, key_rope]
         keys.append(jnp.concatenate(parts, axis=1))
         values.append(kv_rows[:, head * KV_WIDTH + NOPE : (head + 1) * KV_WIDTH])
-    spans = [(head, tile * QUERIES) for head in range(2) for tile in range(TOK_CTX // QUERIES)]
+    spans = [(head, first) for head in range(HEADS_DEV) for first in range(0, TOK_CTX, QUERIES)]
 
     def operands(head, first):
         rows_at = slice(first, first + QUERIES)
-        queries = query_all[step, rows_at, head * NOPE : head * NOPE + 2 * NOPE]
-        return queries, grad_all[step, rows_at, head * VDIM : (head + 1) * VDIM]
+        left = head // 2 * 2 * (NOPE + ROPE) + head % 2 * NOPE
+        queries = query_ref[rows_at, left : left + 2 * NOPE]
+        return queries, grad_ref[rows_at, head * VDIM : (head + 1) * VDIM]
 
     def products(head, first):
         queries, upstream = operands(head, first)
@@ -202,7 +175,7 @@
         return scores, mm(values[head][first : first + KEYS], upstream, NT)
 
     def slopes(first, scores, dots):
-        scores = scores * (FACTOR * LOG2E) + bias_ref[first // QUERIES]
+        scores = scores * (FACTOR * LOG2E) + biases[first // QUERIES]
         weights = jnp.exp2(scores - jnp.max(scores, axis=0, keepdims=True))
         prob = weights * (1.0 / jnp.sum(weights, axis=0, keepdims=True))
         prob_low = prob.astype(low)
@@ -213,16 +186,17 @@
         queries, upstream = operands(head, first)
         d_query = mm(slope, keys[head][first : first + KEYS], TN) * FACTOR
         at = slice(first, first + QUERIES)
-        if head == 0:
-            d_query_ref[at, :NOPE] = d_query[:, :NOPE].astype(low)
-            middle.append(d_query[:, NOPE:])
+        left = head // 2 * 2 * (NOPE + ROPE)
+        if head % 2 == 0:
+            d_query_ref[at, left : left + NOPE] = d_query[:, :NOPE].astype(low)
+            middle[first] = d_query[:, NOPE:]
         else:
-            whole = middle[first // QUERIES] + d_query[:, :NOPE]
-            d_query_ref[at, NOPE : 2 * NOPE] = whole.astype(low)
-            d_query_ref[at, 2 * NOPE :] = d_query[:, NOPE:].astype(low)
+            whole = middle[first] + d_query[:, :NOPE]
+            d_query_ref[at, left + NOPE : left + 2 * NOPE] = whole.astype(low)
+            d_query_ref[at, left + 2 * NOPE : left + 3 * NOPE] = d_query[:, NOPE:].astype(low)
         return mm(slope, queries, NN), mm(prob_low, upstream, NN)
 
-    middle, grads = [], []
+    middle, grads = {}, []
     made, held = {}, {}
     count = len(spans)
     for turn in range(-AHEAD, count + BEHIND):
@@ -234,7 +208,7 @@
             grads.append(gradients(*spans[turn - BEHIND], *held.pop(turn - BEHIND)))
 
     kv_grads, rope_grads = [], []
-    for head in range(2):
+    for head in range(HEADS_DEV):
         key_grad, value_grad = (
             jnp.concatenate(
                 [one[:QUERIES], one[QUERIES:] + two[:-QUERIES], two[-QUERIES:]], axis=0
@@ -242,54 +216,47 @@
             for one, two in zip(*grads[2 * head : 2 * head + 2])
         )
         key_grad = key_grad * FACTOR
-        if head == 0:
+        if head % 2 == 0:
             nope_grad, rope_grad = key_grad[:, :NOPE], key_grad[:, NOPE : NOPE + ROPE]
         else:
             nope_grad, rope_grad = key_grad[:, ROPE : ROPE + NOPE], key_grad[:, ROPE + NOPE :]
         rope_grads.append(rope_grad)
         kv_grads += [nope_grad.astype(low), value_grad.astype(low)]
     kv_grad = jnp.concatenate(kv_grads, axis=1)
-    rope_ref[...] += (rope_grads[0] + rope_grads[1]).reshape(rope_ref.shape)
+    rope_ref[...] = sum(rope_grads[1:], rope_grads[0]).reshape(rope_ref.shape)
+    term_ref[...] = mm(kv_grad, weight_ref[...], NT).reshape(term_ref.shape)
+    plain_ref[...] = latent.T.reshape(2 * N_CTX, PART, WINDOW)
+    for by in range(N_CTX):
+        at = lax.rem(place + by, N_CTX)
+        turned_ref[by] = plain_ref[core * N_CTX + at]
+        turned_ref[N_CTX + by] = plain_ref[(1 - core) * N_CTX + at]
     part = mm(turned_ref[...].reshape(LATENT, WINDOW), kv_grad, NN).astype(low)
     kept_ref[...] = part[: LATENT // 2]
     given_ref[...] = part[LATENT // 2 :]
-    term_ref[...] += mm(kv_grad, weight_ref[...], NT).reshape(term_ref.shape)
-
-    @pl.when(step == pl.num_programs(0) - 1)
-    def _():
-        for by in range(Y):
-            at = lax.rem(spot + by, Y)
-            for outs, first in ((prev_terms, 0), (own_terms, Z)):
-                out = outs[by]
-                out[:, :, :LATENT] = term_ref[first : first + Z, at].astype(out.dtype)
-                out[:, :, LATENT:] = rope_ref[first : first + Z, at].astype(out.dtype)
+
+    for by in range(Y):
+        at = lax.rem(spot + by, Y)
+        for outs, first in ((prev_terms, 0), (own_terms, Z)):
+            out = outs[by]
+            out[:, :, :LATENT] = term_ref[first : first + Z, at].astype(out.dtype)
+            out[:, :, LATENT:] = rope_ref[first : first + Z, at].astype(out.dtype)
 
 
 def attention(spot, low_keys, own_pieces, prev_pieces, weight, query, grad_out):
-    def whole(shape):
-        return pl.BlockSpec(shape, lambda step: (0,) * len(shape))
-
-    def columns(count, width):
-        return pl.BlockSpec((count, width), lambda step: (0, step))
-
+    vmem = pl.BlockSpec(memory_space=pltpu.VMEM)
+    hbm = pl.BlockSpec(memory_space=pltpu.HBM)
     piece = (Z, ROWS, LATENT + ROPE)
     return pl.pallas_call(
         attention_kernel,
-        grid=(HEADS_DEV // 2,),
         in_specs=[
             pl.BlockSpec(memory_space=pltpu.SMEM),
-            whole((1, TOK_CTX)),
-            *[whole(piece)] * (2 * Y),
-            columns(LATENT, 2 * KV_WIDTH),
-            pl.BlockSpec(memory_space=pltpu.HBM),
-            pl.BlockSpec(memory_space=pltpu.HBM),
+            vmem,
+            *[vmem] * (2 * Y),
+            hbm,
+            hbm,
+            hbm,
         ],
-        out_specs=[
-            columns(TOK_CTX, 2 * (NOPE + ROPE)),
-            columns(LATENT // 2, 2 * KV_WIDTH),
-            columns(LATENT // 2, 2 * KV_WIDTH),
-            *[whole(piece)] * (2 * Y),
-        ],
+        out_specs=[vmem] * (3 + 2 * Y),
         out_shape=[
             jax.ShapeDtypeStruct((TOK_CTX, HEADS_DEV * (NOPE + ROPE)), jnp.bfloat16),
             jax.ShapeDtypeStruct((LATENT // 2, HEADS_DEV * KV_WIDTH), jnp.bfloat16),
@@ -298,14 +265,14 @@
         ],
         scratch_shapes=[
             pltpu.VMEM((2 * Z, Y, ROWS, LATENT + ROPE), jnp.bfloat16),
-            pltpu.VMEM((TOK_CTX // QUERIES, KEYS, QUERIES), jnp.float32),
             pltpu.VMEM((2 * N_CTX, PART, WINDOW), jnp.bfloat16),
             pltpu.VMEM((2 * N_CTX, PART, WINDOW), jnp.bfloat16),
             pltpu.VMEM((2 * Z, Y, ROWS, LATENT), jnp.float32),
             pltpu.VMEM((2 * Z, Y, ROWS, ROPE), jnp.float32),
-            pltpu.VMEM((HEADS_DEV // 2, TOK_CTX, 2 * (NOPE + ROPE)), jnp.bfloat16),
-            pltpu.VMEM((HEADS_DEV // 2, TOK_CTX, 2 * VDIM), jnp.bfloat16),
-            pltpu.SemaphoreType.DMA((4,)),
+            pltpu.VMEM((LATENT, HEADS_DEV * KV_WIDTH), jnp.bfloat16),
+            pltpu.VMEM((TOK_CTX, HEADS_DEV * (NOPE + ROPE)), jnp.bfloat16),
+            pltpu.VMEM((TOK_CTX, HEADS_DEV * VDIM), jnp.bfloat16),
+            pltpu.SemaphoreType.DMA((3,)),
         ],
         compiler_params=pltpu.CompilerParams(vmem_limit_bytes=48 * 1024 * 1024),
         cost_estimate=pl.CostEstimate(

time: 96.1 us -> 94.5 us (0.983)
  Pallas kernels: 15 us -> 13.4 us
    pallas_call x1, Pallas kernels: 13.4 us -> 11.7 us  [attention(): pl.pallas_call(attention_kernel, in_specs=[pl.BlockSpec(memory_space=pltp...]
where the time goes in v6:
time: 94.5 us; the launch traced here: 94 us
  starting transfers between devices  50.6 us (54%)
  waiting for transfers between devices  25.3 us (27%)
  Pallas kernels  13.4 us (14%)
  local copies, waits for them, and re-layouts  2.14 us (2%)
  other arithmetic  1.88 us (2%)
    ppermute x12, starting transfers between devices, turned(): return lax.ppermute(array, axis, pairs)  14.8 us
    pallas_call x1, Pallas kernels, attention(): pl.pallas_call(attention_kernel, in_specs=[pl.BlockSpec(memory_space=pltp...  11.7 us
    ppermute x12, waiting for transfers between devices, turned(): return lax.ppermute(array, axis, pairs)  11.5 us
    ppermute x6, starting transfers between devices, turned(): lax.ppermute(array, axis, [(i, (i + by) % N_CTX) for i in range(N_CTX)])  9.11 us
    all_to_all x1, starting transfers between devices, on_device(): block = lax.all_to_all(block, 'head', 0, 0, axis_index_groups=along_z)  9.01 us
    all_to_all x1, waiting for transfers between devices, on_device(): block = lax.all_to_all(block, 'head', 0, 0, axis_index_groups=along_z)  6.6 us
    ppermute x1, starting transfers between devices, on_device(): d_kv_weight = placed(parts, lax.ppermute(parts, 'dp', [(0, 1), (1, 0)]))  5.35 us
    ppermute x1, starting transfers between devices, summed_weight(): other = lax.ppermute(given, 'dp', swap)  4.52 us
  transfers between devices with their start and end apart: 24, of which 11 were waited for; matrix products, arithmetic and copies ran while one was open for 3% of the time, Pallas kernels for 0%

profile of v6, /device:TPU:1, one launch (start us, length us, event | category | flops | bytes accessed | tf_op | source)
XLA Modules:
  0.0 94.0 jit_solution(14536475084607607540)
XLA Ops:
  0.6 1.4 %broadcast_in_dim.29 = bf16[8,16,576]{2,1,0:T(8,128)(2,1)} broadcast(bf16[16,576]{1,0:T(8,128)(2,1)} %bitcast.16), dimensions={1,2} | broadcast | bytes 165888 | tf_op jit(solution)/shard_map/broadcast_in_dim | solution.py:310
  2.0 9.0 %all-to-all-start = ((bf16[8,16,576]{2,1,0:T(8,128)(2,1)}), bf16[8,16,576]{2,1,0:T(8,128)(2,1)S(1)}, u32[]{:S(2)}, u32[]{:S(2)}) async-start(bf16[8,16,576]{2,1,0:T(8,128)(2,1)} %broadcast_in_dim.29), calls=%async_computation | async-start | bytes 327680 | tf_op jit(solution)/shard_map/all_to_all | solution.py:311
  12.6 6.6 %all-to-all-done.refs_0_ = bf16[8,16,576]{2,1,0:T(8,128)(2,1)S(1)} async-done(((bf16[8,16,576]{2,1,0:T(8,128)(2,1)}), bf16[8,16,576]{2,1,0:T(8,128)(2,1)S(1)}, u32[]{:S(2)}, u32[]{:S(2)}) %all-to-all-start) | async-done | bytes 147488 | tf_op jit(solution)/shard_map/all_to_all | solution.py:311
  19.2 3.1 %collective-permute-start.3 = (bf16[8,16,576]{2,1,0:T(8,128)(2,1)S(1)}, bf16[8,16,576]{2,1,0:T(8,128)(2,1)S(1)}, u32[]{:S(2)}, u32[]{:S(2)}) collective-permute-start(bf16[8,16,576]{2,1,0:T(8,128)(2,1)S(1)} %all-to-all-done.refs_0_), channel_id=1, source_target_pairs={{0,32},{32,64},{64,96},{1,33},{33,65},{65,97},{2,34},{34,66},{66,9... | collective-permute-start | bytes 442376 | tf_op jit(solution)/shard_map/ppermute | solution.py:32
  22.3 2.8 %collective-permute-start.2 = (bf16[8,16,576]{2,1,0:T(8,128)(2,1)S(1)}, bf16[8,16,576]{2,1,0:T(8,128)(2,1)S(1)}, u32[]{:S(2)}, u32[]{:S(2)}) collective-permute-start(bf16[8,16,576]{2,1,0:T(8,128)(2,1)S(1)} %all-to-all-done.refs_0_), channel_id=1, source_target_pairs={{0,3},{1,0},{2,1},{3,2},{4,7},{5,4},{6,5},{7,6},{8,11},{9,8},{10,9... | collective-permute-start | bytes 442376 | tf_op jit(solution)/shard_map/ppermute | solution.py:39
  26.4 2.0 %collective-permute-start.6 = (bf16[8,16,576]{2,1,0:T(8,128)(2,1)S(1)}, bf16[8,16,576]{2,1,0:T(8,128)(2,1)S(1)}, u32[]{:S(2)}, u32[]{:S(2)}) collective-permute-start(bf16[8,16,576]{2,1,0:T(8,128)(2,1)S(1)} %collective-permute-done.3.refs_4_), channel_id=1, source_target_pairs={{0,3},{1,0},{2,1},{3,2},{4,7},{5,4},{6,5},{7,6},{8,11},{9,8},{10,9... | collective-permute-start | bytes 442376 | tf_op jit(solution)/shard_map/ppermute | solution.py:39
  28.3 1.4 %collective-permute-start.5 = (bf16[8,16,576]{2,1,0:T(8,128)(2,1)S(1)}, bf16[8,16,576]{2,1,0:T(8,128)(2,1)S(1)}, u32[]{:S(2)}, u32[]{:S(2)}) collective-permute-start(bf16[8,16,576]{2,1,0:T(8,128)(2,1)S(1)} %collective-permute-done.3.refs_4_), channel_id=1, source_target_pairs={{0,2},{1,3},{2,0},{3,1},{4,6},{5,7},{6,4},{7,5},{8,10},{9,11},{10,... | collective-permute-start | bytes 442376 | tf_op jit(solution)/shard_map/ppermute | solution.py:39
  31.1 1.7 %collective-permute-done.refs_1_ = bf16[8,16,576]{2,1,0:T(8,128)(2,1)S(1)} collective-permute-done((bf16[8,16,576]{2,1,0:T(8,128)(2,1)S(1)}, bf16[8,16,576]{2,1,0:T(8,128)(2,1)S(1)}, u32[]{:S(2)}, u32[]{:S(2)}) %collective-permute-start) | collective-permute-done | bytes 147488 | tf_op jit(solution)/shard_map/ppermute | solution.py:39
  32.7 2.7 %collective-permute-done.6.refs_7_ = bf16[8,16,576]{2,1,0:T(8,128)(2,1)S(1)} collective-permute-done((bf16[8,16,576]{2,1,0:T(8,128)(2,1)S(1)}, bf16[8,16,576]{2,1,0:T(8,128)(2,1)S(1)}, u32[]{:S(2)}, u32[]{:S(2)}) %collective-permute-start.6) | collective-permute-done | bytes 147488 | tf_op jit(solution)/shard_map/ppermute | solution.py:39
  36.5 3.6 %collective-permute-done.4.refs_5_ = bf16[8,16,576]{2,1,0:T(8,128)(2,1)S(1)} collective-permute-done((bf16[8,16,576]{2,1,0:T(8,128)(2,1)S(1)}, bf16[8,16,576]{2,1,0:T(8,128)(2,1)S(1)}, u32[]{:S(2)}, u32[]{:S(2)}) %collective-permute-start.4) | collective-permute-done | bytes 147488 | tf_op jit(solution)/shard_map/ppermute | solution.py:39
  40.1 11.7 %attention.1 = (bf16[512,768]{1,0:T(8,128)(2,1)}, bf16[256,1024]{1,0:T(8,128)(2,1)S(1)}, bf16[256,1024]{1,0:T(8,128)(2,1)S(1)}, f32[8,16,576]{2,1,0:T(8,128)S(1)...) custom-call(s32[3]{0:T(128)S(1)} %pad_add_fusion.spot_ref, ...), custom_call_target="tpu_custom_call" | custom-call | flops 8000000000 | bytes 10000000 | tf_op jit(solution)/shard_map/attention/pallas_call | solution.py:249
  51.9 1.4 %collective-permute-start.11 = (bf16[8,16,576]{2,1,0:T(8,128)(2,1)S(1)}, bf16[8,16,576]{2,1,0:T(8,128)(2,1)S(1)}, u32[]{:S(2)}, u32[]{:S(2)}) collective-permute-start(bf16[8,16,576]{2,1,0:T(8,128)(2,1)S(1)} %get-tuple-element.25), channel_id=1, source_target_pairs={{0,2},{1,3},{2,0},{3,1},{4,6},{5,7},{6,4},{7,5},{8,10},{9,11},{10,... | collective-permute-start | bytes 442376 | tf_op jit(solution)/shard_map/ppermute | solution.py:39
  53.3 1.3 %collective-permute-start.12 = (bf16[8,16,576]{2,1,0:T(8,128)(2,1)S(1)}, bf16[8,16,576]{2,1,0:T(8,128)(2,1)S(1)}, u32[]{:S(2)}, u32[]{:S(2)}) collective-permute-start(bf16[8,16,576]{2,1,0:T(8,128)(2,1)S(1)} %get-tuple-element.26), channel_id=1, source_target_pairs={{0,3},{1,0},{2,1},{3,2},{4,7},{5,4},{6,5},{7,6},{8,11},{9,8},{10,9... | collective-permute-start | bytes 442376 | tf_op jit(solution)/shard_map/ppermute | solution.py:39
  54.6 4.5 %collective-permute-start.14 = (bf16[256,1024]{1,0:T(8,128)(2,1)S(1)}, bf16[256,1024]{1,0:T(8,128)(2,1)S(1)}, u32[]{:S(2)}, u32[]{:S(2)}) collective-permute-start(bf16[256,1024]{1,0:T(8,128)(2,1)S(1)} %get-tuple-element.28), channel_id=1, source_target_pairs={{0,128},{128,0},{1,129},{129,1},{2,130},{130,2},{3,131},{131,3},{4... | collective-permute-start | bytes 1572872 | tf_op jit(solution)/shard_map/ppermute | solution.py:75
  60.4 1.3 %collective-permute-start.8 = (bf16[8,16,576]{2,1,0:T(8,128)(2,1)S(1)}, bf16[8,16,576]{2,1,0:T(8,128)(2,1)S(1)}, u32[]{:S(2)}, u32[]{:S(2)}) collective-permute-start(bf16[8,16,576]{2,1,0:T(8,128)(2,1)S(1)} %get-tuple-element.21), channel_id=1, source_target_pairs={{0,2},{1,3},{2,0},{3,1},{4,6},{5,7},{6,4},{7,5},{8,10},{9,11},{10,... | collective-permute-start | bytes 442376 | tf_op jit(solution)/shard_map/ppermute | solution.py:39
  61.7 2.1 %collective-permute-start.9 = (bf16[8,16,576]{2,1,0:T(8,128)(2,1)S(1)}, bf16[8,16,576]{2,1,0:T(8,128)(2,1)S(1)}, u32[]{:S(2)}, u32[]{:S(2)}) collective-permute-start(bf16[8,16,576]{2,1,0:T(8,128)(2,1)S(1)} %get-tuple-element.22), channel_id=1, source_target_pairs={{0,3},{1,0},{2,1},{3,2},{4,7},{5,4},{6,5},{7,6},{8,11},{9,8},{10,9... | collective-permute-start | bytes 442376 | tf_op jit(solution)/shard_map/ppermute | solution.py:39
  65.3 2.2 %collective-permute-start.15 = (bf16[64,1024]{1,0:T(8,128)(2,1)S(1)}, bf16[64,1024]{1,0:T(8,128)(2,1)S(1)}, u32[]{:S(2)}, u32[]{:S(2)}) collective-permute-start(bf16[64,1024]{1,0:T(8,128)(2,1)S(1)} %get-tuple-element.30), channel_id=1, source_target_pairs={{0,32},{32,64},{64,96},{96,0},{1,33},{33,65},{65,97},{97,1},{2,34}... | collective-permute-start | bytes 393224 | tf_op jit(solution)/shard_map/ppermute | solution.py:37
  68.8 2.4 %collective-permute-start.16 = (bf16[64,1024]{1,0:T(8,128)(2,1)S(1)}, bf16[64,1024]{1,0:T(8,128)(2,1)S(1)}, u32[]{:S(2)}, u32[]{:S(2)}) collective-permute-start(bf16[64,1024]{1,0:T(8,128)(2,1)S(1)} %get-tuple-element.31), channel_id=1, source_target_pairs={{0,64},{32,96},{64,0},{96,32},{1,65},{33,97},{65,1},{97,33},{2,66}... | collective-permute-start | bytes 393224 | tf_op jit(solution)/shard_map/ppermute | solution.py:37
  73.1 3.4 %all-to-all-start.1 = ((bf16[8,16,576]{2,1,0:T(8,128)(2,1)}), bf16[8,16,576]{2,1,0:T(8,128)(2,1)S(1)}, u32[]{:S(2)}, u32[]{:S(2)}) async-start(bf16[8,16,576]{2,1,0:T(8,128)(2,1)} %add_convert_fusion.after_ref), calls=%async_computation.1 | async-start | bytes 327680 | tf_op jit(solution)/shard_map/all_to_all | solution.py:331
  76.9 1.7 %collective-permute-start.20 = (bf16[64,1024]{1,0:T(8,128)(2,1)S(1)}, bf16[64,1024]{1,0:T(8,128)(2,1)S(1)}, u32[]{:S(2)}, u32[]{:S(2)}) collective-permute-start(bf16[64,1024]{1,0:T(8,128)(2,1)S(1)} %second_sum.1.one_ref), channel_id=1, source_target_pairs={{0,96},{32,0},{64,32},{96,64},{1,97},{33,1},{65,33},{97,65},{2,98}... | collective-permute-start | bytes 393224 | tf_op jit(solution)/shard_map/ppermute | solution.py:37
  80.2 4.5 %all-to-all-done.1 = bf16[8,16,576]{2,1,0:T(8,128)(2,1)S(1)} async-done(((bf16[8,16,576]{2,1,0:T(8,128)(2,1)}), bf16[8,16,576]{2,1,0:T(8,128)(2,1)S(1)}, u32[]{:S(2)}, u32[]{:S(2)}) %all-to-all-start.1) | async-done | bytes 147488 | tf_op jit(solution)/shard_map/all_to_all | solution.py:331
  85.7 5.4 %collective-permute-start.21 = (bf16[4,64,1024]{2,1,0:T(8,128)(2,1)S(1)}, bf16[4,64,1024]{2,1,0:T(8,128)(2,1)S(1)}, u32[]{:S(2)}, u32[]{:S(2)}) collective-permute-start(bf16[4,64,1024]{2,1,0:T(8,128)(2,1)S(1)} %stacked.1.mine_ref), channel_id=1, source_target_pairs={{0,128},{128,0},{1,129},{129,1},{2,130},{130,2},{3,131},{131,3},{4... | collective-permute-start | bytes 1572872 | tf_op jit(solution)/shard_map/ppermute | solution.py:335
  91.0 1.5 %collective-permute-done.21.other_ref = bf16[4,64,1024]{2,1,0:T(8,128)(2,1)S(1)} collective-permute-done((bf16[4,64,1024]{2,1,0:T(8,128)(2,1)S(1)}, bf16[4,64,1024]{2,1,0:T(8,128)(2,1)S(1)}, u32[]{:S(2)}, u32[]{:S(2)}) %collective-permute-start.21) | collective-permute-done | bytes 524320 | tf_op jit(solution)/shard_map/ppermute | solution.py:335
  92.6 1.5 %placed.1 = f32[8,64,1024]{2,1,0:T(8,128)} custom-call(s32[1]{0:T(128)} %bitcast.core_ref, s32[1]{0:T(128)} %bitcast.1.place_ref, bf16[4,64,1024]{2,1,0:T(8,128)(2,1)S(1)} %stacked.1.mine_ref, bf16[4,64,1024]{2,1,0:T(8,128)(2,1)S(1)} %collective-permute-done.21.other_ref), custom_call_target="tpu_custom_call" | custom-call | tf_op jit(solution)/shard_map/placed/pallas_call | solution.py:103
  (43 shorter events, 14.1 us)
Async XLA Ops:
  2.0 17.2 %all-to-all-start = ((bf16[8,16,576]{2,1,0:T(8,128)(2,1)}), bf16[8,16,576]{2,1,0:T(8,128)(2,1)S(1)}, u32[]{:S(2)}, u32[]{:S(2)}) async-start(bf16[8,16,576]{2,1,0:T(8,128)(2,1)} %broadcast_in_dim.29), calls=%async_computation | async-start | bytes 327680 | tf_op jit(solution)/shard_map/all_to_all | solution.py:311
  19.2 7.2 %collective-permute-start.3 = (bf16[8,16,576]{2,1,0:T(8,128)(2,1)S(1)}, bf16[8,16,576]{2,1,0:T(8,128)(2,1)S(1)}, u32[]{:S(2)}, u32[]{:S(2)}) collective-permute-start(bf16[8,16,576]{2,1,0:T(8,128)(2,1)S(1)} %all-to-all-done.refs_0_), channel_id=1, source_target_pairs={{0,32},{32,64},{64,96},{1,33},{33,65},{65,97},{2,34},{34,66},{66,9... | collective-permute-start | bytes 442376 | tf_op jit(solution)/shard_map/ppermute | solution.py:32
  22.3 7.4 %collective-permute-start.2 = (bf16[8,16,576]{2,1,0:T(8,128)(2,1)S(1)}, bf16[8,16,576]{2,1,0:T(8,128)(2,1)S(1)}, u32[]{:S(2)}, u32[]{:S(2)}) collective-permute-start(bf16[8,16,576]{2,1,0:T(8,128)(2,1)S(1)} %all-to-all-done.refs_0_), channel_id=1, source_target_pairs={{0,3},{1,0},{2,1},{3,2},{4,7},{5,4},{6,5},{7,6},{8,11},{9,8},{10,9... | collective-permute-start | bytes 442376 | tf_op jit(solution)/shard_map/ppermute | solution.py:39
  25.2 5.9 %collective-permute-start.1 = (bf16[8,16,576]{2,1,0:T(8,128)(2,1)S(1)}, bf16[8,16,576]{2,1,0:T(8,128)(2,1)S(1)}, u32[]{:S(2)}, u32[]{:S(2)}) collective-permute-start(bf16[8,16,576]{2,1,0:T(8,128)(2,1)S(1)} %all-to-all-done.refs_0_), channel_id=1, source_target_pairs={{0,2},{1,3},{2,0},{3,1},{4,6},{5,7},{6,4},{7,5},{8,10},{9,11},{10,... | collective-permute-start | bytes 442376 | tf_op jit(solution)/shard_map/ppermute | solution.py:39
  25.7 7.1 %collective-permute-start = (bf16[8,16,576]{2,1,0:T(8,128)(2,1)S(1)}, bf16[8,16,576]{2,1,0:T(8,128)(2,1)S(1)}, u32[]{:S(2)}, u32[]{:S(2)}) collective-permute-start(bf16[8,16,576]{2,1,0:T(8,128)(2,1)S(1)} %all-to-all-done.refs_0_), channel_id=1, source_target_pairs={{0,1},{1,2},{2,3},{3,0},{4,5},{5,6},{6,7},{7,4},{8,9},{9,10},{10,1... | collective-permute-start | bytes 442376 | tf_op jit(solution)/shard_map/ppermute | solution.py:39
  26.4 9.1 %collective-permute-start.6 = (bf16[8,16,576]{2,1,0:T(8,128)(2,1)S(1)}, bf16[8,16,576]{2,1,0:T(8,128)(2,1)S(1)}, u32[]{:S(2)}, u32[]{:S(2)}) collective-permute-start(bf16[8,16,576]{2,1,0:T(8,128)(2,1)S(1)} %collective-permute-done.3.refs_4_), channel_id=1, source_target_pairs={{0,3},{1,0},{2,1},{3,2},{4,7},{5,4},{6,5},{7,6},{8,11},{9,8},{10,9... | collective-permute-start | bytes 442376 | tf_op jit(solution)/shard_map/ppermute | solution.py:39
  28.3 8.1 %collective-permute-start.5 = (bf16[8,16,576]{2,1,0:T(8,128)(2,1)S(1)}, bf16[8,16,576]{2,1,0:T(8,128)(2,1)S(1)}, u32[]{:S(2)}, u32[]{:S(2)}) collective-permute-start(bf16[8,16,576]{2,1,0:T(8,128)(2,1)S(1)} %collective-permute-done.3.refs_4_), channel_id=1, source_target_pairs={{0,2},{1,3},{2,0},{3,1},{4,6},{5,7},{6,4},{7,5},{8,10},{9,11},{10,... | collective-permute-start | bytes 442376 | tf_op jit(solution)/shard_map/ppermute | solution.py:39
  29.8 10.3 %collective-permute-start.4 = (bf16[8,16,576]{2,1,0:T(8,128)(2,1)S(1)}, bf16[8,16,576]{2,1,0:T(8,128)(2,1)S(1)}, u32[]{:S(2)}, u32[]{:S(2)}) collective-permute-start(bf16[8,16,576]{2,1,0:T(8,128)(2,1)S(1)} %collective-permute-done.3.refs_4_), channel_id=1, source_target_pairs={{0,1},{1,2},{2,3},{3,0},{4,5},{5,6},{6,7},{7,4},{8,9},{9,10},{10,1... | collective-permute-start | bytes 442376 | tf_op jit(solution)/shard_map/ppermute | solution.py:39
  51.8 8.6 %collective-permute-start.10 = (bf16[8,16,576]{2,1,0:T(8,128)(2,1)S(1)}, bf16[8,16,576]{2,1,0:T(8,128)(2,1)S(1)}, u32[]{:S(2)}, u32[]{:S(2)}) collective-permute-start(bf16[8,16,576]{2,1,0:T(8,128)(2,1)S(1)} %get-tuple-element.24), channel_id=1, source_target_pairs={{0,1},{1,2},{2,3},{3,0},{4,5},{5,6},{6,7},{7,4},{8,9},{9,10},{10,1... | collective-permute-start | bytes 442376 | tf_op jit(solution)/shard_map/ppermute | solution.py:39
  51.9 9.9 %collective-permute-start.11 = (bf16[8,16,576]{2,1,0:T(8,128)(2,1)S(1)}, bf16[8,16,576]{2,1,0:T(8,128)(2,1)S(1)}, u32[]{:S(2)}, u32[]{:S(2)}) collective-permute-start(bf16[8,16,576]{2,1,0:T(8,128)(2,1)S(1)} %get-tuple-element.25), channel_id=1, source_target_pairs={{0,2},{1,3},{2,0},{3,1},{4,6},{5,7},{6,4},{7,5},{8,10},{9,11},{10,... | collective-permute-start | bytes 442376 | tf_op jit(solution)/shard_map/ppermute | solution.py:39
  53.3 10.5 %collective-permute-start.12 = (bf16[8,16,576]{2,1,0:T(8,128)(2,1)S(1)}, bf16[8,16,576]{2,1,0:T(8,128)(2,1)S(1)}, u32[]{:S(2)}, u32[]{:S(2)}) collective-permute-start(bf16[8,16,576]{2,1,0:T(8,128)(2,1)S(1)} %get-tuple-element.26), channel_id=1, source_target_pairs={{0,3},{1,0},{2,1},{3,2},{4,7},{5,4},{6,5},{7,6},{8,11},{9,8},{10,9... | collective-permute-start | bytes 442376 | tf_op jit(solution)/shard_map/ppermute | solution.py:39
  54.6 10.6 %collective-permute-start.14 = (bf16[256,1024]{1,0:T(8,128)(2,1)S(1)}, bf16[256,1024]{1,0:T(8,128)(2,1)S(1)}, u32[]{:S(2)}, u32[]{:S(2)}) collective-permute-start(bf16[256,1024]{1,0:T(8,128)(2,1)S(1)} %get-tuple-element.28), channel_id=1, source_target_pairs={{0,128},{128,0},{1,129},{129,1},{2,130},{130,2},{3,131},{131,3},{4... | collective-permute-start | bytes 1572872 | tf_op jit(solution)/shard_map/ppermute | solution.py:75
  59.1 9.6 %collective-permute-start.7 = (bf16[8,16,576]{2,1,0:T(8,128)(2,1)S(1)}, bf16[8,16,576]{2,1,0:T(8,128)(2,1)S(1)}, u32[]{:S(2)}, u32[]{:S(2)}) collective-permute-start(bf16[8,16,576]{2,1,0:T(8,128)(2,1)S(1)} %get-tuple-element.20), channel_id=1, source_target_pairs={{0,1},{1,2},{2,3},{3,0},{4,5},{5,6},{6,7},{7,4},{8,9},{9,10},{10,1... | collective-permute-start | bytes 442376 | tf_op jit(solution)/shard_map/ppermute | solution.py:39
  60.4 10.8 %collective-permute-start.8 = (bf16[8,16,576]{2,1,0:T(8,128)(2,1)S(1)}, bf16[8,16,576]{2,1,0:T(8,128)(2,1)S(1)}, u32[]{:S(2)}, u32[]{:S(2)}) collective-permute-start(bf16[8,16,576]{2,1,0:T(8,128)(2,1)S(1)} %get-tuple-element.21), channel_id=1, source_target_pairs={{0,2},{1,3},{2,0},{3,1},{4,6},{5,7},{6,4},{7,5},{8,10},{9,11},{10,... | collective-permute-start | bytes 442376 | tf_op jit(solution)/shard_map/ppermute | solution.py:39
  61.7 10.6 %collective-permute-start.9 = (bf16[8,16,576]{2,1,0:T(8,128)(2,1)S(1)}, bf16[8,16,576]{2,1,0:T(8,128)(2,1)S(1)}, u32[]{:S(2)}, u32[]{:S(2)}) collective-permute-start(bf16[8,16,576]{2,1,0:T(8,128)(2,1)S(1)} %get-tuple-element.22), channel_id=1, source_target_pairs={{0,3},{1,0},{2,1},{3,2},{4,7},{5,4},{6,5},{7,6},{8,11},{9,8},{10,9... | collective-permute-start | bytes 442376 | tf_op jit(solution)/shard_map/ppermute | solution.py:39
  63.9 8.5 %collective-permute-start.13 = (bf16[8,16,576]{2,1,0:T(8,128)(2,1)S(1)}, bf16[8,16,576]{2,1,0:T(8,128)(2,1)S(1)}, u32[]{:S(2)}, u32[]{:S(2)}) collective-permute-start(bf16[8,16,576]{2,1,0:T(8,128)(2,1)S(1)} %add_convert_fusion.1.after_ref), channel_id=1, source_target_pairs={{32,0},{64,32},{96,64},{33,1},{65,33},{97,65},{34,2},{66,34},{98,6... | collective-permute-start | bytes 442376 | tf_op jit(solution)/shard_map/ppermute | solution.py:32
  65.3 11.2 %collective-permute-start.15 = (bf16[64,1024]{1,0:T(8,128)(2,1)S(1)}, bf16[64,1024]{1,0:T(8,128)(2,1)S(1)}, u32[]{:S(2)}, u32[]{:S(2)}) collective-permute-start(bf16[64,1024]{1,0:T(8,128)(2,1)S(1)} %get-tuple-element.30), channel_id=1, source_target_pairs={{0,32},{32,64},{64,96},{96,0},{1,33},{33,65},{65,97},{97,1},{2,34}... | collective-permute-start | bytes 393224 | tf_op jit(solution)/shard_map/ppermute | solution.py:37
  68.8 7.8 %collective-permute-start.16 = (bf16[64,1024]{1,0:T(8,128)(2,1)S(1)}, bf16[64,1024]{1,0:T(8,128)(2,1)S(1)}, u32[]{:S(2)}, u32[]{:S(2)}) collective-permute-start(bf16[64,1024]{1,0:T(8,128)(2,1)S(1)} %get-tuple-element.31), channel_id=1, source_target_pairs={{0,64},{32,96},{64,0},{96,32},{1,65},{33,97},{65,1},{97,33},{2,66}... | collective-permute-start | bytes 393224 | tf_op jit(solution)/shard_map/ppermute | solution.py:37
  71.2 5.6 %collective-permute-start.17 = (bf16[64,1024]{1,0:T(8,128)(2,1)S(1)}, bf16[64,1024]{1,0:T(8,128)(2,1)S(1)}, u32[]{:S(2)}, u32[]{:S(2)}) collective-permute-start(bf16[64,1024]{1,0:T(8,128)(2,1)S(1)} %get-tuple-element.32), channel_id=1, source_target_pairs={{0,96},{32,0},{64,32},{96,64},{1,97},{33,1},{65,33},{97,65},{2,98}... | collective-permute-start | bytes 393224 | tf_op jit(solution)/shard_map/ppermute | solution.py:37
  73.1 11.6 %all-to-all-start.1 = ((bf16[8,16,576]{2,1,0:T(8,128)(2,1)}), bf16[8,16,576]{2,1,0:T(8,128)(2,1)S(1)}, u32[]{:S(2)}, u32[]{:S(2)}) async-start(bf16[8,16,576]{2,1,0:T(8,128)(2,1)} %add_convert_fusion.after_ref), calls=%async_computation.1 | async-start | bytes 327680 | tf_op jit(solution)/shard_map/all_to_all | solution.py:331
  76.9 7.9 %collective-permute-start.20 = (bf16[64,1024]{1,0:T(8,128)(2,1)S(1)}, bf16[64,1024]{1,0:T(8,128)(2,1)S(1)}, u32[]{:S(2)}, u32[]{:S(2)}) collective-permute-start(bf16[64,1024]{1,0:T(8,128)(2,1)S(1)} %second_sum.1.one_ref), channel_id=1, source_target_pairs={{0,96},{32,0},{64,32},{96,64},{1,97},{33,1},{65,33},{97,65},{2,98}... | collective-permute-start | bytes 393224 | tf_op jit(solution)/shard_map/ppermute | solution.py:37
  78.6 6.2 %collective-permute-start.19 = (bf16[64,1024]{1,0:T(8,128)(2,1)S(1)}, bf16[64,1024]{1,0:T(8,128)(2,1)S(1)}, u32[]{:S(2)}, u32[]{:S(2)}) collective-permute-start(bf16[64,1024]{1,0:T(8,128)(2,1)S(1)} %second_sum.1.one_ref), channel_id=1, source_target_pairs={{0,64},{32,96},{64,0},{96,32},{1,65},{33,97},{65,1},{97,33},{2,66}... | collective-permute-start | bytes 393224 | tf_op jit(solution)/shard_map/ppermute | solution.py:37
  79.5 6.1 %collective-permute-start.18 = (bf16[64,1024]{1,0:T(8,128)(2,1)S(1)}, bf16[64,1024]{1,0:T(8,128)(2,1)S(1)}, u32[]{:S(2)}, u32[]{:S(2)}) collective-permute-start(bf16[64,1024]{1,0:T(8,128)(2,1)S(1)} %second_sum.1.one_ref), channel_id=1, source_target_pairs={{0,32},{32,64},{64,96},{96,0},{1,33},{33,65},{65,97},{97,1},{2,34}... | collective-permute-start | bytes 393224 | tf_op jit(solution)/shard_map/ppermute | solution.py:37
  85.7 6.9 %collective-permute-start.21 = (bf16[4,64,1024]{2,1,0:T(8,128)(2,1)S(1)}, bf16[4,64,1024]{2,1,0:T(8,128)(2,1)S(1)}, u32[]{:S(2)}, u32[]{:S(2)}) collective-permute-start(bf16[4,64,1024]{2,1,0:T(8,128)(2,1)S(1)} %stacked.1.mine_ref), channel_id=1, source_target_pairs={{0,128},{128,0},{1,129},{129,1},{2,130},{130,2},{3,131},{131,3},{4... | collective-permute-start | bytes 1572872 | tf_op jit(solution)/shard_map/ppermute | solution.py:335
  (1 other events, 9.3 us)

commit v7 on v6

--- a/solution.py
+++ b/solution.py
@@ -85,30 +85,33 @@
     return pieces
 
 
-def place_kernel(core_ref, place_ref, mine_ref, other_ref, out_ref):
-    core, place = core_ref[0], place_ref[0]
+def place_kernel(core_ref, place_ref, given_ref, *refs):
     for by in range(N_CTX):
-        at = lax.rem(place - by + N_CTX, N_CTX)
-        out_ref[core * N_CTX + at] = mine_ref[by].astype(jnp.float32)
-        out_ref[(1 - core) * N_CTX + at] = other_ref[by].astype(jnp.float32)
+        at = lax.rem(place_ref[0] - by + N_CTX, N_CTX)
+        refs[-1][at] = given_ref[by].astype(jnp.float32)
 
 
 def place_of(axis):
     return lax.axis_index(axis).astype(jnp.int32).reshape(1)
 
 
-def placed(mine, other):
-    vmem = pl.BlockSpec(memory_space=pltpu.VMEM)
-    smem = pl.BlockSpec(memory_space=pltpu.SMEM)
-    whole = pl.pallas_call(
+def placed(given, half, whole, name):
+    shape = given.shape
+    first = whole is None
+    return pl.pallas_call(
         place_kernel,
-        in_specs=[smem, smem, vmem, vmem],
-        out_specs=vmem,
-        out_shape=jax.ShapeDtypeStruct((2 * N_CTX, *mine.shape[1:]), jnp.float32),
+        grid_spec=pltpu.PrefetchScalarGridSpec(
+            num_scalar_prefetch=2,
+            grid=(1,),
+            in_specs=[pl.BlockSpec(shape, lambda step, half, place: (0, 0, 0))]
+            + [pl.BlockSpec(memory_space=pl.ANY)] * (not first),
+            out_specs=pl.BlockSpec(shape, lambda step, half, place: (half[0], 0, 0)),
+        ),
+        out_shape=jax.ShapeDtypeStruct((2 * N_CTX, *shape[1:]), jnp.float32),
+        input_output_aliases={} if first else {3: 0},
         compiler_params=pltpu.CompilerParams(vmem_limit_bytes=16 * 1024 * 1024),
-        name="placed",
-    )(place_of("dp"), place_of("ctx"), mine, other)
-    return whole.reshape(LATENT, -1)
+        name=name,
+    )(half, place_of("ctx"), given, *([] if first else [whole]))
 
 
 NT = (((1,), (1,)), ((), ()))
@@ -331,8 +334,11 @@
     shares = lax.all_to_all(term, "head", 0, 0, axis_index_groups=along_z)
     d_latent = jnp.sum(shares.astype(jnp.float32), axis=0).astype(jnp.bfloat16)
     stacked = jax.ShapeDtypeStruct((N_CTX, *parts[0].shape), jnp.bfloat16)
-    parts = small_call(stack_kernel, stacked, "stacked", *parts, after=d_latent)
-    d_kv_weight = placed(parts, lax.ppermute(parts, "dp", [(0, 1), (1, 0)]))
+    parts = small_call(stack_kernel, stacked, "stacked", *parts, after=shares)
+    other = lax.ppermute(parts, "dp", [(0, 1), (1, 0)])
+    core = place_of("dp")
+    d_kv_weight = placed(parts, core, None, "mine")
+    d_kv_weight = placed(other, 1 - core, d_kv_weight, "other").reshape(LATENT, -1)
     return (d_query[None], d_latent[None], d_kv_weight)
 
 

time: 94.5 us -> 94.2 us (level)
  waiting for transfers between devices: 25.3 us -> 23.8 us
    ppermute x1, waiting for transfers between devices: 1.54 us -> 0.01 us  [on_device(): other = lax.ppermute(parts, 'dp', [(0, 1), (1, 0)])]
    pallas_call x1 -> x2, Pallas kernels: 1.46 us -> 2.08 us  [placed(): pl.pallas_call(place_kernel, grid_spec=pltpu.PrefetchScalarGridSpec(num_s...]
  transfers between devices with their start and end apart: 24 -> 24, of which waited for: 11 -> 10; matrix products, arithmetic and copies ran while one was open for 3% -> 3% of each run, Pallas kernels for 0% -> 1%
where the time goes in v7:
time: 94.2 us; the launch traced here: 93.8 us
  starting transfers between devices  50.6 us (54%)
  waiting for transfers between devices  23.8 us (25%)
  Pallas kernels  14 us (15%)
  other arithmetic  2.5 us (3%)
  local copies, waits for them, and re-layouts  2.14 us (2%)
    ppermute x12, starting transfers between devices, turned(): return lax.ppermute(array, axis, pairs)  14.8 us
    pallas_call x1, Pallas kernels, attention(): pl.pallas_call(attention_kernel, in_specs=[pl.BlockSpec(memory_space=pltp...  11.7 us
    ppermute x12, waiting for transfers between devices, turned(): return lax.ppermute(array, axis, pairs)  11.5 us
    ppermute x6, starting transfers between devices, turned(): lax.ppermute(array, axis, [(i, (i + by) % N_CTX) for i in range(N_CTX)])  9.11 us
    all_to_all x1, starting transfers between devices, on_device(): block = lax.all_to_all(block, 'head', 0, 0, axis_index_groups=along_z)  9.01 us
    all_to_all x1, waiting for transfers between devices, on_device(): block = lax.all_to_all(block, 'head', 0, 0, axis_index_groups=along_z)  6.6 us
    ppermute x1, starting transfers between devices, on_device(): other = lax.ppermute(parts, 'dp', [(0, 1), (1, 0)])  5.36 us
    ppermute x1, starting transfers between devices, summed_weight(): other = lax.ppermute(given, 'dp', swap)  4.52 us
  transfers between devices with their start and end apart: 24, of which 10 were waited for; matrix products, arithmetic and copies ran while one was open for 3% of the time, Pallas kernels for 1%

profile of v7, /device:TPU:1, one launch (start us, length us, event | category | flops | bytes accessed | tf_op | source)
XLA Modules:
  0.0 93.8 jit_solution(12096981606309697483)
XLA Ops:
  0.6 1.4 %broadcast_in_dim.29 = bf16[8,16,576]{2,1,0:T(8,128)(2,1)} broadcast(bf16[16,576]{1,0:T(8,128)(2,1)} %bitcast.15), dimensions={1,2} | broadcast | bytes 165888 | tf_op jit(solution)/shard_map/broadcast_in_dim | solution.py:313
  2.0 9.0 %all-to-all-start = ((bf16[8,16,576]{2,1,0:T(8,128)(2,1)}), bf16[8,16,576]{2,1,0:T(8,128)(2,1)S(1)}, u32[]{:S(2)}, u32[]{:S(2)}) async-start(bf16[8,16,576]{2,1,0:T(8,128)(2,1)} %broadcast_in_dim.29), calls=%async_computation | async-start | bytes 327680 | tf_op jit(solution)/shard_map/all_to_all | solution.py:314
  12.6 6.6 %all-to-all-done.refs_0_ = bf16[8,16,576]{2,1,0:T(8,128)(2,1)S(1)} async-done(((bf16[8,16,576]{2,1,0:T(8,128)(2,1)}), bf16[8,16,576]{2,1,0:T(8,128)(2,1)S(1)}, u32[]{:S(2)}, u32[]{:S(2)}) %all-to-all-start) | async-done | bytes 147488 | tf_op jit(solution)/shard_map/all_to_all | solution.py:314
  19.2 3.1 %collective-permute-start.3 = (bf16[8,16,576]{2,1,0:T(8,128)(2,1)S(1)}, bf16[8,16,576]{2,1,0:T(8,128)(2,1)S(1)}, u32[]{:S(2)}, u32[]{:S(2)}) collective-permute-start(bf16[8,16,576]{2,1,0:T(8,128)(2,1)S(1)} %all-to-all-done.refs_0_), channel_id=1, source_target_pairs={{0,32},{32,64},{64,96},{1,33},{33,65},{65,97},{2,34},{34,66},{66,9... | collective-permute-start | bytes 442376 | tf_op jit(solution)/shard_map/ppermute | solution.py:32
  22.3 2.8 %collective-permute-start.2 = (bf16[8,16,576]{2,1,0:T(8,128)(2,1)S(1)}, bf16[8,16,576]{2,1,0:T(8,128)(2,1)S(1)}, u32[]{:S(2)}, u32[]{:S(2)}) collective-permute-start(bf16[8,16,576]{2,1,0:T(8,128)(2,1)S(1)} %all-to-all-done.refs_0_), channel_id=1, source_target_pairs={{0,3},{1,0},{2,1},{3,2},{4,7},{5,4},{6,5},{7,6},{8,11},{9,8},{10,9... | collective-permute-start | bytes 442376 | tf_op jit(solution)/shard_map/ppermute | solution.py:39
  26.4 2.0 %collective-permute-start.6 = (bf16[8,16,576]{2,1,0:T(8,128)(2,1)S(1)}, bf16[8,16,576]{2,1,0:T(8,128)(2,1)S(1)}, u32[]{:S(2)}, u32[]{:S(2)}) collective-permute-start(bf16[8,16,576]{2,1,0:T(8,128)(2,1)S(1)} %collective-permute-done.3.refs_4_), channel_id=1, source_target_pairs={{0,3},{1,0},{2,1},{3,2},{4,7},{5,4},{6,5},{7,6},{8,11},{9,8},{10,9... | collective-permute-start | bytes 442376 | tf_op jit(solution)/shard_map/ppermute | solution.py:39
  28.3 1.4 %collective-permute-start.5 = (bf16[8,16,576]{2,1,0:T(8,128)(2,1)S(1)}, bf16[8,16,576]{2,1,0:T(8,128)(2,1)S(1)}, u32[]{:S(2)}, u32[]{:S(2)}) collective-permute-start(bf16[8,16,576]{2,1,0:T(8,128)(2,1)S(1)} %collective-permute-done.3.refs_4_), channel_id=1, source_target_pairs={{0,2},{1,3},{2,0},{3,1},{4,6},{5,7},{6,4},{7,5},{8,10},{9,11},{10,... | collective-permute-start | bytes 442376 | tf_op jit(solution)/shard_map/ppermute | solution.py:39
  31.1 1.7 %collective-permute-done.refs_1_ = bf16[8,16,576]{2,1,0:T(8,128)(2,1)S(1)} collective-permute-done((bf16[8,16,576]{2,1,0:T(8,128)(2,1)S(1)}, bf16[8,16,576]{2,1,0:T(8,128)(2,1)S(1)}, u32[]{:S(2)}, u32[]{:S(2)}) %collective-permute-start) | collective-permute-done | bytes 147488 | tf_op jit(solution)/shard_map/ppermute | solution.py:39
  32.7 2.7 %collective-permute-done.6.refs_7_ = bf16[8,16,576]{2,1,0:T(8,128)(2,1)S(1)} collective-permute-done((bf16[8,16,576]{2,1,0:T(8,128)(2,1)S(1)}, bf16[8,16,576]{2,1,0:T(8,128)(2,1)S(1)}, u32[]{:S(2)}, u32[]{:S(2)}) %collective-permute-start.6) | collective-permute-done | bytes 147488 | tf_op jit(solution)/shard_map/ppermute | solution.py:39
  36.5 3.6 %collective-permute-done.4.refs_5_ = bf16[8,16,576]{2,1,0:T(8,128)(2,1)S(1)} collective-permute-done((bf16[8,16,576]{2,1,0:T(8,128)(2,1)S(1)}, bf16[8,16,576]{2,1,0:T(8,128)(2,1)S(1)}, u32[]{:S(2)}, u32[]{:S(2)}) %collective-permute-start.4) | collective-permute-done | bytes 147488 | tf_op jit(solution)/shard_map/ppermute | solution.py:39
  40.1 11.7 %attention.1 = (bf16[512,768]{1,0:T(8,128)(2,1)}, bf16[256,1024]{1,0:T(8,128)(2,1)S(1)}, bf16[256,1024]{1,0:T(8,128)(2,1)S(1)}, f32[8,16,576]{2,1,0:T(8,128)S(1)...) custom-call(s32[3]{0:T(128)S(1)} %pad_add_fusion.spot_ref, ...), custom_call_target="tpu_custom_call" | custom-call | flops 8000000000 | bytes 10000000 | tf_op jit(solution)/shard_map/attention/pallas_call | solution.py:252
  51.9 1.4 %collective-permute-start.11 = (bf16[8,16,576]{2,1,0:T(8,128)(2,1)S(1)}, bf16[8,16,576]{2,1,0:T(8,128)(2,1)S(1)}, u32[]{:S(2)}, u32[]{:S(2)}) collective-permute-start(bf16[8,16,576]{2,1,0:T(8,128)(2,1)S(1)} %get-tuple-element.25), channel_id=1, source_target_pairs={{0,2},{1,3},{2,0},{3,1},{4,6},{5,7},{6,4},{7,5},{8,10},{9,11},{10,... | collective-permute-start | bytes 442376 | tf_op jit(solution)/shard_map/ppermute | solution.py:39
  53.3 1.3 %collective-permute-start.12 = (bf16[8,16,576]{2,1,0:T(8,128)(2,1)S(1)}, bf16[8,16,576]{2,1,0:T(8,128)(2,1)S(1)}, u32[]{:S(2)}, u32[]{:S(2)}) collective-permute-start(bf16[8,16,576]{2,1,0:T(8,128)(2,1)S(1)} %get-tuple-element.26), channel_id=1, source_target_pairs={{0,3},{1,0},{2,1},{3,2},{4,7},{5,4},{6,5},{7,6},{8,11},{9,8},{10,9... | collective-permute-start | bytes 442376 | tf_op jit(solution)/shard_map/ppermute | solution.py:39
  54.6 4.5 %collective-permute-start.14 = (bf16[256,1024]{1,0:T(8,128)(2,1)S(1)}, bf16[256,1024]{1,0:T(8,128)(2,1)S(1)}, u32[]{:S(2)}, u32[]{:S(2)}) collective-permute-start(bf16[256,1024]{1,0:T(8,128)(2,1)S(1)} %get-tuple-element.28), channel_id=1, source_target_pairs={{0,128},{128,0},{1,129},{129,1},{2,130},{130,2},{3,131},{131,3},{4... | collective-permute-start | bytes 1572872 | tf_op jit(solution)/shard_map/ppermute | solution.py:75
  59.1 1.3 %collective-permute-start.7 = (bf16[8,16,576]{2,1,0:T(8,128)(2,1)S(1)}, bf16[8,16,576]{2,1,0:T(8,128)(2,1)S(1)}, u32[]{:S(2)}, u32[]{:S(2)}) collective-permute-start(bf16[8,16,576]{2,1,0:T(8,128)(2,1)S(1)} %get-tuple-element.20), channel_id=1, source_target_pairs={{0,1},{1,2},{2,3},{3,0},{4,5},{5,6},{6,7},{7,4},{8,9},{9,10},{10,1... | collective-permute-start | bytes 442376 | tf_op jit(solution)/shard_map/ppermute | solution.py:39
  60.4 1.3 %collective-permute-start.8 = (bf16[8,16,576]{2,1,0:T(8,128)(2,1)S(1)}, bf16[8,16,576]{2,1,0:T(8,128)(2,1)S(1)}, u32[]{:S(2)}, u32[]{:S(2)}) collective-permute-start(bf16[8,16,576]{2,1,0:T(8,128)(2,1)S(1)} %get-tuple-element.21), channel_id=1, source_target_pairs={{0,2},{1,3},{2,0},{3,1},{4,6},{5,7},{6,4},{7,5},{8,10},{9,11},{10,... | collective-permute-start | bytes 442376 | tf_op jit(solution)/shard_map/ppermute | solution.py:39
  61.7 2.1 %collective-permute-start.9 = (bf16[8,16,576]{2,1,0:T(8,128)(2,1)S(1)}, bf16[8,16,576]{2,1,0:T(8,128)(2,1)S(1)}, u32[]{:S(2)}, u32[]{:S(2)}) collective-permute-start(bf16[8,16,576]{2,1,0:T(8,128)(2,1)S(1)} %get-tuple-element.22), channel_id=1, source_target_pairs={{0,3},{1,0},{2,1},{3,2},{4,7},{5,4},{6,5},{7,6},{8,11},{9,8},{10,9... | collective-permute-start | bytes 442376 | tf_op jit(solution)/shard_map/ppermute | solution.py:39
  63.9 1.3 %collective-permute-start.13 = (bf16[8,16,576]{2,1,0:T(8,128)(2,1)S(1)}, bf16[8,16,576]{2,1,0:T(8,128)(2,1)S(1)}, u32[]{:S(2)}, u32[]{:S(2)}) collective-permute-start(bf16[8,16,576]{2,1,0:T(8,128)(2,1)S(1)} %add_convert_fusion.1.after_ref), channel_id=1, source_target_pairs={{32,0},{64,32},{96,64},{33,1},{65,33},{97,65},{34,2},{66,34},{98,6... | collective-permute-start | bytes 442376 | tf_op jit(solution)/shard_map/ppermute | solution.py:32
  65.3 2.2 %collective-permute-start.15 = (bf16[64,1024]{1,0:T(8,128)(2,1)S(1)}, bf16[64,1024]{1,0:T(8,128)(2,1)S(1)}, u32[]{:S(2)}, u32[]{:S(2)}) collective-permute-start(bf16[64,1024]{1,0:T(8,128)(2,1)S(1)} %get-tuple-element.30), channel_id=1, source_target_pairs={{0,32},{32,64},{64,96},{96,0},{1,33},{33,65},{65,97},{97,1},{2,34}... | collective-permute-start | bytes 393224 | tf_op jit(solution)/shard_map/ppermute | solution.py:37
  68.8 2.4 %collective-permute-start.16 = (bf16[64,1024]{1,0:T(8,128)(2,1)S(1)}, bf16[64,1024]{1,0:T(8,128)(2,1)S(1)}, u32[]{:S(2)}, u32[]{:S(2)}) collective-permute-start(bf16[64,1024]{1,0:T(8,128)(2,1)S(1)} %get-tuple-element.31), channel_id=1, source_target_pairs={{0,64},{32,96},{64,0},{96,32},{1,65},{33,97},{65,1},{97,33},{2,66}... | collective-permute-start | bytes 393224 | tf_op jit(solution)/shard_map/ppermute | solution.py:37
  73.2 3.4 %all-to-all-start.1 = ((bf16[8,16,576]{2,1,0:T(8,128)(2,1)}), bf16[8,16,576]{2,1,0:T(8,128)(2,1)S(1)}, u32[]{:S(2)}, u32[]{:S(2)}) async-start(bf16[8,16,576]{2,1,0:T(8,128)(2,1)} %add_convert_fusion.after_ref), calls=%async_computation.1 | async-start | bytes 327680 | tf_op jit(solution)/shard_map/all_to_all | solution.py:334
  76.9 1.7 %collective-permute-start.20 = (bf16[64,1024]{1,0:T(8,128)(2,1)S(1)}, bf16[64,1024]{1,0:T(8,128)(2,1)S(1)}, u32[]{:S(2)}, u32[]{:S(2)}) collective-permute-start(bf16[64,1024]{1,0:T(8,128)(2,1)S(1)} %second_sum.1.one_ref), channel_id=1, source_target_pairs={{0,96},{32,0},{64,32},{96,64},{1,97},{33,1},{65,33},{97,65},{2,98}... | collective-permute-start | bytes 393224 | tf_op jit(solution)/shard_map/ppermute | solution.py:37
  80.2 4.5 %all-to-all-done.1.after_ref = bf16[8,16,576]{2,1,0:T(8,128)(2,1)S(1)} async-done(((bf16[8,16,576]{2,1,0:T(8,128)(2,1)}), bf16[8,16,576]{2,1,0:T(8,128)(2,1)S(1)}, u32[]{:S(2)}, u32[]{:S(2)}) %all-to-all-start.1) | async-done | bytes 147488 | tf_op jit(solution)/shard_map/all_to_all | solution.py:334
  85.7 5.4 %collective-permute-start.21 = (bf16[4,64,1024]{2,1,0:T(8,128)(2,1)S(1)}, bf16[4,64,1024]{2,1,0:T(8,128)(2,1)S(1)}, u32[]{:S(2)}, u32[]{:S(2)}) collective-permute-start(bf16[4,64,1024]{2,1,0:T(8,128)(2,1)S(1)} %stacked.1.given_ref), channel_id=1, source_target_pairs={{0,128},{128,0},{1,129},{129,1},{2,130},{130,2},{3,131},{131,3},{4... | collective-permute-start | bytes 1572872 | tf_op jit(solution)/shard_map/ppermute | solution.py:338
  (42 shorter events, 14.3 us)
Async XLA Ops:
  2.0 17.2 %all-to-all-start = ((bf16[8,16,576]{2,1,0:T(8,128)(2,1)}), bf16[8,16,576]{2,1,0:T(8,128)(2,1)S(1)}, u32[]{:S(2)}, u32[]{:S(2)}) async-start(bf16[8,16,576]{2,1,0:T(8,128)(2,1)} %broadcast_in_dim.29), calls=%async_computation | async-start | bytes 327680 | tf_op jit(solution)/shard_map/all_to_all | solution.py:314
  19.2 7.2 %collective-permute-start.3 = (bf16[8,16,576]{2,1,0:T(8,128)(2,1)S(1)}, bf16[8,16,576]{2,1,0:T(8,128)(2,1)S(1)}, u32[]{:S(2)}, u32[]{:S(2)}) collective-permute-start(bf16[8,16,576]{2,1,0:T(8,128)(2,1)S(1)} %all-to-all-done.refs_0_), channel_id=1, source_target_pairs={{0,32},{32,64},{64,96},{1,33},{33,65},{65,97},{2,34},{34,66},{66,9... | collective-permute-start | bytes 442376 | tf_op jit(solution)/shard_map/ppermute | solution.py:32
  22.3 7.4 %collective-permute-start.2 = (bf16[8,16,576]{2,1,0:T(8,128)(2,1)S(1)}, bf16[8,16,576]{2,1,0:T(8,128)(2,1)S(1)}, u32[]{:S(2)}, u32[]{:S(2)}) collective-permute-start(bf16[8,16,576]{2,1,0:T(8,128)(2,1)S(1)} %all-to-all-done.refs_0_), channel_id=1, source_target_pairs={{0,3},{1,0},{2,1},{3,2},{4,7},{5,4},{6,5},{7,6},{8,11},{9,8},{10,9... | collective-permute-start | bytes 442376 | tf_op jit(solution)/shard_map/ppermute | solution.py:39
  25.2 5.9 %collective-permute-start.1 = (bf16[8,16,576]{2,1,0:T(8,128)(2,1)S(1)}, bf16[8,16,576]{2,1,0:T(8,128)(2,1)S(1)}, u32[]{:S(2)}, u32[]{:S(2)}) collective-permute-start(bf16[8,16,576]{2,1,0:T(8,128)(2,1)S(1)} %all-to-all-done.refs_0_), channel_id=1, source_target_pairs={{0,2},{1,3},{2,0},{3,1},{4,6},{5,7},{6,4},{7,5},{8,10},{9,11},{10,... | collective-permute-start | bytes 442376 | tf_op jit(solution)/shard_map/ppermute | solution.py:39
  25.7 7.1 %collective-permute-start = (bf16[8,16,576]{2,1,0:T(8,128)(2,1)S(1)}, bf16[8,16,576]{2,1,0:T(8,128)(2,1)S(1)}, u32[]{:S(2)}, u32[]{:S(2)}) collective-permute-start(bf16[8,16,576]{2,1,0:T(8,128)(2,1)S(1)} %all-to-all-done.refs_0_), channel_id=1, source_target_pairs={{0,1},{1,2},{2,3},{3,0},{4,5},{5,6},{6,7},{7,4},{8,9},{9,10},{10,1... | collective-permute-start | bytes 442376 | tf_op jit(solution)/shard_map/ppermute | solution.py:39
  26.4 9.1 %collective-permute-start.6 = (bf16[8,16,576]{2,1,0:T(8,128)(2,1)S(1)}, bf16[8,16,576]{2,1,0:T(8,128)(2,1)S(1)}, u32[]{:S(2)}, u32[]{:S(2)}) collective-permute-start(bf16[8,16,576]{2,1,0:T(8,128)(2,1)S(1)} %collective-permute-done.3.refs_4_), channel_id=1, source_target_pairs={{0,3},{1,0},{2,1},{3,2},{4,7},{5,4},{6,5},{7,6},{8,11},{9,8},{10,9... | collective-permute-start | bytes 442376 | tf_op jit(solution)/shard_map/ppermute | solution.py:39
  28.3 8.1 %collective-permute-start.5 = (bf16[8,16,576]{2,1,0:T(8,128)(2,1)S(1)}, bf16[8,16,576]{2,1,0:T(8,128)(2,1)S(1)}, u32[]{:S(2)}, u32[]{:S(2)}) collective-permute-start(bf16[8,16,576]{2,1,0:T(8,128)(2,1)S(1)} %collective-permute-done.3.refs_4_), channel_id=1, source_target_pairs={{0,2},{1,3},{2,0},{3,1},{4,6},{5,7},{6,4},{7,5},{8,10},{9,11},{10,... | collective-permute-start | bytes 442376 | tf_op jit(solution)/shard_map/ppermute | solution.py:39
  29.8 10.3 %collective-permute-start.4 = (bf16[8,16,576]{2,1,0:T(8,128)(2,1)S(1)}, bf16[8,16,576]{2,1,0:T(8,128)(2,1)S(1)}, u32[]{:S(2)}, u32[]{:S(2)}) collective-permute-start(bf16[8,16,576]{2,1,0:T(8,128)(2,1)S(1)} %collective-permute-done.3.refs_4_), channel_id=1, source_target_pairs={{0,1},{1,2},{2,3},{3,0},{4,5},{5,6},{6,7},{7,4},{8,9},{9,10},{10,1... | collective-permute-start | bytes 442376 | tf_op jit(solution)/shard_map/ppermute | solution.py:39
  51.8 8.6 %collective-permute-start.10 = (bf16[8,16,576]{2,1,0:T(8,128)(2,1)S(1)}, bf16[8,16,576]{2,1,0:T(8,128)(2,1)S(1)}, u32[]{:S(2)}, u32[]{:S(2)}) collective-permute-start(bf16[8,16,576]{2,1,0:T(8,128)(2,1)S(1)} %get-tuple-element.24), channel_id=1, source_target_pairs={{0,1},{1,2},{2,3},{3,0},{4,5},{5,6},{6,7},{7,4},{8,9},{9,10},{10,1... | collective-permute-start | bytes 442376 | tf_op jit(solution)/shard_map/ppermute | solution.py:39
  51.9 9.9 %collective-permute-start.11 = (bf16[8,16,576]{2,1,0:T(8,128)(2,1)S(1)}, bf16[8,16,576]{2,1,0:T(8,128)(2,1)S(1)}, u32[]{:S(2)}, u32[]{:S(2)}) collective-permute-start(bf16[8,16,576]{2,1,0:T(8,128)(2,1)S(1)} %get-tuple-element.25), channel_id=1, source_target_pairs={{0,2},{1,3},{2,0},{3,1},{4,6},{5,7},{6,4},{7,5},{8,10},{9,11},{10,... | collective-permute-start | bytes 442376 | tf_op jit(solution)/shard_map/ppermute | solution.py:39
  53.3 10.5 %collective-permute-start.12 = (bf16[8,16,576]{2,1,0:T(8,128)(2,1)S(1)}, bf16[8,16,576]{2,1,0:T(8,128)(2,1)S(1)}, u32[]{:S(2)}, u32[]{:S(2)}) collective-permute-start(bf16[8,16,576]{2,1,0:T(8,128)(2,1)S(1)} %get-tuple-element.26), channel_id=1, source_target_pairs={{0,3},{1,0},{2,1},{3,2},{4,7},{5,4},{6,5},{7,6},{8,11},{9,8},{10,9... | collective-permute-start | bytes 442376 | tf_op jit(solution)/shard_map/ppermute | solution.py:39
  54.6 10.6 %collective-permute-start.14 = (bf16[256,1024]{1,0:T(8,128)(2,1)S(1)}, bf16[256,1024]{1,0:T(8,128)(2,1)S(1)}, u32[]{:S(2)}, u32[]{:S(2)}) collective-permute-start(bf16[256,1024]{1,0:T(8,128)(2,1)S(1)} %get-tuple-element.28), channel_id=1, source_target_pairs={{0,128},{128,0},{1,129},{129,1},{2,130},{130,2},{3,131},{131,3},{4... | collective-permute-start | bytes 1572872 | tf_op jit(solution)/shard_map/ppermute | solution.py:75
  59.1 9.6 %collective-permute-start.7 = (bf16[8,16,576]{2,1,0:T(8,128)(2,1)S(1)}, bf16[8,16,576]{2,1,0:T(8,128)(2,1)S(1)}, u32[]{:S(2)}, u32[]{:S(2)}) collective-permute-start(bf16[8,16,576]{2,1,0:T(8,128)(2,1)S(1)} %get-tuple-element.20), channel_id=1, source_target_pairs={{0,1},{1,2},{2,3},{3,0},{4,5},{5,6},{6,7},{7,4},{8,9},{9,10},{10,1... | collective-permute-start | bytes 442376 | tf_op jit(solution)/shard_map/ppermute | solution.py:39
  60.4 10.8 %collective-permute-start.8 = (bf16[8,16,576]{2,1,0:T(8,128)(2,1)S(1)}, bf16[8,16,576]{2,1,0:T(8,128)(2,1)S(1)}, u32[]{:S(2)}, u32[]{:S(2)}) collective-permute-start(bf16[8,16,576]{2,1,0:T(8,128)(2,1)S(1)} %get-tuple-element.21), channel_id=1, source_target_pairs={{0,2},{1,3},{2,0},{3,1},{4,6},{5,7},{6,4},{7,5},{8,10},{9,11},{10,... | collective-permute-start | bytes 442376 | tf_op jit(solution)/shard_map/ppermute | solution.py:39
  61.7 10.6 %collective-permute-start.9 = (bf16[8,16,576]{2,1,0:T(8,128)(2,1)S(1)}, bf16[8,16,576]{2,1,0:T(8,128)(2,1)S(1)}, u32[]{:S(2)}, u32[]{:S(2)}) collective-permute-start(bf16[8,16,576]{2,1,0:T(8,128)(2,1)S(1)} %get-tuple-element.22), channel_id=1, source_target_pairs={{0,3},{1,0},{2,1},{3,2},{4,7},{5,4},{6,5},{7,6},{8,11},{9,8},{10,9... | collective-permute-start | bytes 442376 | tf_op jit(solution)/shard_map/ppermute | solution.py:39
  63.9 8.5 %collective-permute-start.13 = (bf16[8,16,576]{2,1,0:T(8,128)(2,1)S(1)}, bf16[8,16,576]{2,1,0:T(8,128)(2,1)S(1)}, u32[]{:S(2)}, u32[]{:S(2)}) collective-permute-start(bf16[8,16,576]{2,1,0:T(8,128)(2,1)S(1)} %add_convert_fusion.1.after_ref), channel_id=1, source_target_pairs={{32,0},{64,32},{96,64},{33,1},{65,33},{97,65},{34,2},{66,34},{98,6... | collective-permute-start | bytes 442376 | tf_op jit(solution)/shard_map/ppermute | solution.py:32
  65.3 11.2 %collective-permute-start.15 = (bf16[64,1024]{1,0:T(8,128)(2,1)S(1)}, bf16[64,1024]{1,0:T(8,128)(2,1)S(1)}, u32[]{:S(2)}, u32[]{:S(2)}) collective-permute-start(bf16[64,1024]{1,0:T(8,128)(2,1)S(1)} %get-tuple-element.30), channel_id=1, source_target_pairs={{0,32},{32,64},{64,96},{96,0},{1,33},{33,65},{65,97},{97,1},{2,34}... | collective-permute-start | bytes 393224 | tf_op jit(solution)/shard_map/ppermute | solution.py:37
  68.8 7.8 %collective-permute-start.16 = (bf16[64,1024]{1,0:T(8,128)(2,1)S(1)}, bf16[64,1024]{1,0:T(8,128)(2,1)S(1)}, u32[]{:S(2)}, u32[]{:S(2)}) collective-permute-start(bf16[64,1024]{1,0:T(8,128)(2,1)S(1)} %get-tuple-element.31), channel_id=1, source_target_pairs={{0,64},{32,96},{64,0},{96,32},{1,65},{33,97},{65,1},{97,33},{2,66}... | collective-permute-start | bytes 393224 | tf_op jit(solution)/shard_map/ppermute | solution.py:37
  71.2 5.6 %collective-permute-start.17 = (bf16[64,1024]{1,0:T(8,128)(2,1)S(1)}, bf16[64,1024]{1,0:T(8,128)(2,1)S(1)}, u32[]{:S(2)}, u32[]{:S(2)}) collective-permute-start(bf16[64,1024]{1,0:T(8,128)(2,1)S(1)} %get-tuple-element.32), channel_id=1, source_target_pairs={{0,96},{32,0},{64,32},{96,64},{1,97},{33,1},{65,33},{97,65},{2,98}... | collective-permute-start | bytes 393224 | tf_op jit(solution)/shard_map/ppermute | solution.py:37
  73.2 11.6 %all-to-all-start.1 = ((bf16[8,16,576]{2,1,0:T(8,128)(2,1)}), bf16[8,16,576]{2,1,0:T(8,128)(2,1)S(1)}, u32[]{:S(2)}, u32[]{:S(2)}) async-start(bf16[8,16,576]{2,1,0:T(8,128)(2,1)} %add_convert_fusion.after_ref), calls=%async_computation.1 | async-start | bytes 327680 | tf_op jit(solution)/shard_map/all_to_all | solution.py:334
  76.9 7.8 %collective-permute-start.20 = (bf16[64,1024]{1,0:T(8,128)(2,1)S(1)}, bf16[64,1024]{1,0:T(8,128)(2,1)S(1)}, u32[]{:S(2)}, u32[]{:S(2)}) collective-permute-start(bf16[64,1024]{1,0:T(8,128)(2,1)S(1)} %second_sum.1.one_ref), channel_id=1, source_target_pairs={{0,96},{32,0},{64,32},{96,64},{1,97},{33,1},{65,33},{97,65},{2,98}... | collective-permute-start | bytes 393224 | tf_op jit(solution)/shard_map/ppermute | solution.py:37
  78.6 6.1 %collective-permute-start.19 = (bf16[64,1024]{1,0:T(8,128)(2,1)S(1)}, bf16[64,1024]{1,0:T(8,128)(2,1)S(1)}, u32[]{:S(2)}, u32[]{:S(2)}) collective-permute-start(bf16[64,1024]{1,0:T(8,128)(2,1)S(1)} %second_sum.1.one_ref), channel_id=1, source_target_pairs={{0,64},{32,96},{64,0},{96,32},{1,65},{33,97},{65,1},{97,33},{2,66}... | collective-permute-start | bytes 393224 | tf_op jit(solution)/shard_map/ppermute | solution.py:37
  79.5 6.1 %collective-permute-start.18 = (bf16[64,1024]{1,0:T(8,128)(2,1)S(1)}, bf16[64,1024]{1,0:T(8,128)(2,1)S(1)}, u32[]{:S(2)}, u32[]{:S(2)}) collective-permute-start(bf16[64,1024]{1,0:T(8,128)(2,1)S(1)} %second_sum.1.one_ref), channel_id=1, source_target_pairs={{0,32},{32,64},{64,96},{96,0},{1,33},{33,65},{65,97},{97,1},{2,34}... | collective-permute-start | bytes 393224 | tf_op jit(solution)/shard_map/ppermute | solution.py:37
  85.7 7.0 %collective-permute-start.21 = (bf16[4,64,1024]{2,1,0:T(8,128)(2,1)S(1)}, bf16[4,64,1024]{2,1,0:T(8,128)(2,1)S(1)}, u32[]{:S(2)}, u32[]{:S(2)}) collective-permute-start(bf16[4,64,1024]{2,1,0:T(8,128)(2,1)S(1)} %stacked.1.given_ref), channel_id=1, source_target_pairs={{0,128},{128,0},{1,129},{129,1},{2,130},{130,2},{3,131},{131,3},{4... | collective-permute-start | bytes 1572872 | tf_op jit(solution)/shard_map/ppermute | solution.py:338
